TPU v7x, 32 devices: a whole 2x2x4 slice. The times are simulated.
32 devices in a mesh: freq: 8 (over z, x), blk: 4 (over y, core).
Axes of the slice: x: 2, y: 2, z: 4, core: 2. Of those that a mesh axis runs over, the one named last changes fastest.
Arguments:
- voltages: int32 [2, 512, 65536], P(None, 'blk', 'freq'), may hold values from -8 to 7
- taps: int32 [4, 1024], replicated, may hold values from -32 to 127
Outputs:
- visibilities: float32 [2, 1024, 512, 512], P(None, 'freq', 'blk')
All inputs are finite; a program needn't handle non-finite values.
Results may differ from a plain program's by a relative error of at most 0.00065.
Values may be sent and summed in bfloat16 or wider, within the bound.
No kernel may reach another device: no remote copies, remote signals or barrier semaphores. Data moves between devices by JAX's collectives and lax.ppermute only.
A program may use at most 256 MiB of HBM per device.

v0:
```python
import math

import jax
import jax.numpy as jnp
from jax import lax
from jax.sharding import PartitionSpec as P


def from_behind(shard, axis, by):
    size = lax.axis_size(axis)
    pairs = [(i, i + by) for i in range(size) if 0 <= i + by < size]
    return lax.ppermute(shard, axis, pairs)


def passed_along(value, axis, steps):
    count = lax.axis_size(axis)
    pairs = [(source, (source + steps) % count) for source in range(count)]
    return lax.ppermute(value, axis, pairs)


def dft_table(channels):
    row_index = lax.broadcasted_iota(jnp.int32, (channels, channels), 0)
    col_index = lax.broadcasted_iota(jnp.int32, (channels, channels), 1)
    phase = (row_index * col_index % channels).astype(jnp.float32) * (2.0 * math.pi / channels)
    factor = 1.0 / math.sqrt(channels)
    cosine = (jnp.cos(phase) * factor).astype(jnp.bfloat16)
    sine = (jnp.sin(phase) * factor).astype(jnp.bfloat16)
    upper = jnp.concatenate([cosine, -sine], axis=1)
    lower = jnp.concatenate([sine, cosine], axis=1)
    return jnp.concatenate([upper, lower], axis=0)


def local(voltages, taps):
    ntaps = taps.shape[0]
    channels = taps.shape[1]
    inputs_blk = voltages.shape[1]
    frames = voltages.shape[2] // channels
    volts = (
        voltages.astype(jnp.float32).reshape(2, inputs_blk, frames, channels).transpose(2, 1, 0, 3)
    )
    coeffs = taps.astype(jnp.float32) / 1024.0
    padded = jnp.pad(volts, ((ntaps - 1, ntaps - 1), (0, 0), (0, 0), (0, 0)))
    span = frames + ntaps - 1
    filtered = jnp.zeros((span, inputs_blk, 2, channels), jnp.float32)
    for tap in range(ntaps):
        filtered = filtered + coeffs[tap][None, None, None, :] * padded[tap : tap + span]
    leftover = filtered[frames:]
    arrived = from_behind(leftover, "freq", 1)
    summed = jnp.concatenate(
        [filtered[: ntaps - 1] + arrived, filtered[ntaps - 1 : frames]], axis=0
    )
    weighted = summed.astype(jnp.bfloat16).reshape(frames * inputs_blk, 2 * channels)
    spectra = jnp.dot(weighted, dft_table(channels), preferred_element_type=jnp.float32)
    spectra = spectra.astype(jnp.bfloat16).reshape(frames, inputs_blk, 2, channels)
    turned = lax.all_to_all(spectra, "freq", split_axis=3, concat_axis=0, tiled=True)
    factor = 1.0 / math.sqrt(turned.shape[0])
    group = turned.shape[3]
    count = lax.axis_size("blk")
    here = lax.axis_index("blk")

    def correlate(tile):
        rotated = jnp.stack([-tile[:, :, 1], tile[:, :, 0]], axis=2)
        partner = jnp.stack([tile, rotated], axis=2)
        return (
            jnp.einsum("sirc,sjorc->ocij", turned, partner, preferred_element_type=jnp.float32)
            * factor
        )

    def place(visible, block, source):
        offset = source * inputs_blk
        zero = jnp.zeros((), jnp.int32)
        return lax.dynamic_update_slice(visible, block, (zero, zero, zero, offset))

    visible = jnp.zeros((2, group, inputs_blk, inputs_blk * count), jnp.float32)
    visible = place(visible, correlate(turned), here)

    def advance(step, carry):
        tile, acc = carry
        tile = passed_along(tile, "blk", 1)
        source = (here - step + count) % count
        return (tile, place(acc, correlate(tile), source))

    carried = lax.fori_loop(1, count, advance, (turned, visible))
    visible = carried[1]
    return visible


def solution(mesh):
    in_specs = (P(None, "blk", "freq"), P())
    out_specs = P(None, "freq", "blk", None)
    return jax.shard_map(local, mesh=mesh, in_specs=in_specs, out_specs=out_specs, check_vma=False)
```

profile of v0, /device:TPU:0, one launch (start us, length us, event | category | flops | bytes accessed | tf_op | source)
XLA Modules:
  0.0 575.2 jit_solution(8659860696897602782)
XLA Ops:
  0.0 0.7 convert_multiply_fusion
  0.7 8.9 %copy.28 = s32[2,128,8192]{1,2,0:T(8,128)} copy(s32[2,128,8192]{2,1,0:T(8,128)} %param.4) | data formatting | bytes 16777216 | tf_op args[0]
  9.6 3.9 convert_element_type.36
  13.5 4.6 fusion.8
  18.1 0.0 copy-start.1
  18.1 4.4 copy-done.1
  22.6 1.8 slice.80
  24.4 2.4 copy.29
  26.8 6.5 %collective-permute-start.1 = (f32[3,128,2,1024]{3,1,2,0:T(8,128)S(1)}, f32[3,128,2,1024]{3,1,2,0:T(8,128)}, u32[]{:S(2)}, u32[]{:S(2)}) collective-permute-start(f32[3,128,2,1024]{3,1,2,0:T(8,128)S(1)} %copy.29), channel_id=1, source_target_pairs={{0,4},{4,8},{8,12},{12,16},{16,20},{20,24},{24,28},{1,5},{5,9},{9,... | collective-permute-start | bytes 9437192 | tf_op jit(solution)/shard_map/ppermute | solution.py:12
  33.3 4.4 slice.114
  37.7 16.5 %fusion.37 = bf16[1024,1024]{1,0:T(8,128)(2,1)} fusion(), kind=kLoop, calls=%fused_computation.56 | loop fusion | flops 19922944 | bytes 2097152 | tf_op jit(solution)/shard_map/neg | solution.py:28
  54.2 18.0 %multiply_convert_fusion = (bf16[1024,1024]{1,0:T(8,128)(2,1)}, bf16[1024,1024]{1,0:T(8,128)(2,1)}) fusion(), kind=kLoop, calls=%fused_computation.44 | loop fusion | flops 18874368 | bytes 4194304 | tf_op jit(solution)/shard_map/convert_element_type | solution.py:27
  72.2 26.8 %collective-permute-done.1 = f32[3,128,2,1024]{3,1,2,0:T(8,128)} collective-permute-done((f32[3,128,2,1024]{3,1,2,0:T(8,128)S(1)}, f32[3,128,2,1024]{3,1,2,0:T(8,128)}, u32[]{:S(2)}, u32[]{:S(2)}) %collective-permute-start.1) | collective-permute-done | bytes 3145760 | tf_op jit(solution)/shard_map/ppermute | solution.py:12
  99.0 2.4 copy.30
  101.4 2.4 fusion.36
  103.7 0.3 copy-done.2
  104.0 0.4 pad_maximum_fusion.1
  104.4 2.7 copy.31
  107.1 25.4 %fusion.30 = bf16[1024,2048]{1,0:T(8,128)(2,1)} fusion(bf16[1024,1024]{1,0:T(8,128)(2,1)} %get-tuple-element.160, bf16[1024,1024]{1,0:T(8,128)(2,1)S(1)} %copy-done.4, bf16[1024,1024]{1,0:T(8,128)(2,1)S(1)} %copy-done.3, bf16[256,8,8,128]{3,2,1,0:T(8,128)(2,1)S(1)} %bitcast.72), kind=kOutput, calls=%fused_computation.49 | convolution fusion | flops 8625586176 | bytes 14680064 | tf_op jit(solution)/shard_map/dot_general | solution.py:53
  132.5 7.8 %reshape.15 = bf16[8,128,2,1024]{3,2,1,0:T(2,128)(2,1)} reshape(bf16[1024,2048]{1,0:T(8,128)(2,1)} %fusion.30) | data formatting | bytes 8388608 | tf_op jit(solution)/shard_map/reshape | solution.py:54
  140.3 8.2 %copy.32 = bf16[8,128,2,1024]{1,0,2,3:T(8,128)(2,1)} copy(bf16[8,128,2,1024]{3,2,1,0:T(2,128)(2,1)} %reshape.15) | data formatting | bytes 8388608 | tf_op jit(solution)/shard_map/reshape | solution.py:54
  148.5 6.9 %all-to-all-start = ((bf16[8,128,2,1024]{1,0,2,3:T(8,128)(2,1)}), bf16[8,128,2,1024]{1,0,2,3:T(8,128)(2,1)}, u32[]{:S(2)}, u32[]{:S(2)}) async-start(bf16[8,128,2,1024]{1,0,2,3:T(8,128)(2,1)} %copy.32), calls=%async_computation | async-start | bytes 8388608 | tf_op jit(solution)/shard_map/all_to_all | solution.py:55
  155.4 92.4 %all-to-all-done = bf16[8,128,2,1024]{1,0,2,3:T(8,128)(2,1)} async-done(((bf16[8,128,2,1024]{1,0,2,3:T(8,128)(2,1)}), bf16[8,128,2,1024]{1,0,2,3:T(8,128)(2,1)}, u32[]{:S(2)}, u32[]{:S(2)}) %all-to-all-start) | async-done | bytes 4194336 | tf_op jit(solution)/shard_map/all_to_all | solution.py:55
  247.8 3.4 copy.55
  251.2 0.4 slice_negate_fusion.1
  251.7 1.6 copy-done
  253.2 2.0 copy.59
  255.2 2.4 maximum_bitcast_fusion.1
  257.6 21.2 %broadcast_in_dim.3 = f32[2,128,128,512]{2,3,0,1:T(8,128)} broadcast(f32[]{:T(128)} %constant.102.clone.1), dimensions={} | broadcast | bytes 67108864 | tf_op jit(solution)/shard_map/broadcast_in_dim | solution.py:74
  278.8 13.0 %bitcast_dynamic-update-slice_fusion.1 = f32[2,128,128,512]{2,3,0,1:T(8,128)} fusion(f32[2,128,128,512]{2,3,0,1:T(8,128)} %broadcast_in_dim.3, s32[]{:T(128)S(6)} %select_n.46, bf16[8,128,2,8,128]{1,0,2,4,3:T(8,128)(2,1)} %bitcast.14, bf16[64,128,1,2,128]{1,0,3,4,2:T(8,128)(2,1)} %maximum_bitcast_fusion.1, bf16[64,128,1,2,128]{1,0,3,4,2:T(8,128)(2,1)} %bitcast.69), kind=kOutput, calls=%fused_computation.13 | convolution fusion | flops 1082130432 | bytes 29360132 | tf_op jit(solution)/shard_map/sirc,sjorc->ocij/dot_general | solution.py:65
  291.8 217.5 %while.17 = (s32[]{:T(128)}, bf16[64,128,2,128]{1,0,2,3:T(8,128)(2,1)}, f32[2,128,128,512]{2,3,0,1:T(8,128)}, bf16[64,128,2,128]{1,0,2,3:T(8,128)(2,1)}, s32[]{:...) while((s32[]{:T(128)}, ...), condition=%wide.region_1.2_spmd, body=%wide.region_0.1_spmd.sunk | while | flops 1085276160 | bytes 71303488 | solution.py:83
  291.8 48.2 %collective-permute-done = bf16[64,128,2,128]{1,0,2,3:T(8,128)(2,1)} collective-permute-done((bf16[64,128,2,128]{1,0,2,3:T(8,128)(2,1)}, bf16[64,128,2,128]{1,0,2,3:T(8,128)(2,1)}, u32[]{:S(2)}, u32[]{:S(2)}) %collective-permute-start) | collective-permute-done | bytes 4194336 | tf_op jit(solution)/shard_map/while/body/eval_jaxpr/ppermute | solution.py:18
  340.0 2.7 slice_negate_fusion.3
  342.7 2.4 maximum_bitcast_fusion.3
  345.1 13.2 %bitcast_dynamic-update-slice_fusion.3 = f32[2,128,128,512]{2,3,0,1:T(8,128)} fusion(f32[2,128,128,512]{2,3,0,1:T(8,128)} %get-tuple-element.209, s32[]{:T(128)S(6)} %select_n.61, bf16[64,128,1,2,128]{1,0,3,2,4:T(8,128)(2,1)} %maximum_bitcast_fusion.3, bf16[64,128,1,2,128]{1,0,3,2,4:T(8,128)(2,1)} %bitcast.66, ...), kind=kOutput, calls=%fused_computation.clone.1 | convolution fusion | flops 1082130432 | bytes 29360132 | tf_op jit(solution)/shard_map/while/body/eval_jaxpr/sirc,sjorc->ocij/dot_general | solution.py:65
  358.2 6.0 %copy.65 = bf16[64,128,2,128]{1,0,2,3:T(8,128)(2,1)} copy(bf16[64,128,2,128]{1,0,2,3:T(8,128)(2,1)} %collective-permute-done) | data formatting | bytes 8388608 | tf_op jit(solution)/shard_map/while
  364.3 0.0 collective-permute-start
  364.3 48.2 %collective-permute-done = bf16[64,128,2,128]{1,0,2,3:T(8,128)(2,1)} collective-permute-done((bf16[64,128,2,128]{1,0,2,3:T(8,128)(2,1)}, bf16[64,128,2,128]{1,0,2,3:T(8,128)(2,1)}, u32[]{:S(2)}, u32[]{:S(2)}) %collective-permute-start) | collective-permute-done | bytes 4194336 | tf_op jit(solution)/shard_map/while/body/eval_jaxpr/ppermute | solution.py:18
  412.5 2.7 slice_negate_fusion.3
  415.2 2.4 maximum_bitcast_fusion.3
  417.6 13.2 %bitcast_dynamic-update-slice_fusion.3 = f32[2,128,128,512]{2,3,0,1:T(8,128)} fusion(f32[2,128,128,512]{2,3,0,1:T(8,128)} %get-tuple-element.209, s32[]{:T(128)S(6)} %select_n.61, bf16[64,128,1,2,128]{1,0,3,2,4:T(8,128)(2,1)} %maximum_bitcast_fusion.3, bf16[64,128,1,2,128]{1,0,3,2,4:T(8,128)(2,1)} %bitcast.66, ...), kind=kOutput, calls=%fused_computation.clone.1 | convolution fusion | flops 1082130432 | bytes 29360132 | tf_op jit(solution)/shard_map/while/body/eval_jaxpr/sirc,sjorc->ocij/dot_general | solution.py:65
  430.7 6.0 %copy.65 = bf16[64,128,2,128]{1,0,2,3:T(8,128)(2,1)} copy(bf16[64,128,2,128]{1,0,2,3:T(8,128)(2,1)} %collective-permute-done) | data formatting | bytes 8388608 | tf_op jit(solution)/shard_map/while
  436.8 48.2 %collective-permute-done = bf16[64,128,2,128]{1,0,2,3:T(8,128)(2,1)} collective-permute-done((bf16[64,128,2,128]{1,0,2,3:T(8,128)(2,1)}, bf16[64,128,2,128]{1,0,2,3:T(8,128)(2,1)}, u32[]{:S(2)}, u32[]{:S(2)}) %collective-permute-start) | collective-permute-done | bytes 4194336 | tf_op jit(solution)/shard_map/while/body/eval_jaxpr/ppermute | solution.py:18
  485.0 2.7 slice_negate_fusion.3
  487.7 2.4 maximum_bitcast_fusion.3
  490.1 13.2 %bitcast_dynamic-update-slice_fusion.3 = f32[2,128,128,512]{2,3,0,1:T(8,128)} fusion(f32[2,128,128,512]{2,3,0,1:T(8,128)} %get-tuple-element.209, s32[]{:T(128)S(6)} %select_n.61, bf16[64,128,1,2,128]{1,0,3,2,4:T(8,128)(2,1)} %maximum_bitcast_fusion.3, bf16[64,128,1,2,128]{1,0,3,2,4:T(8,128)(2,1)} %bitcast.66, ...), kind=kOutput, calls=%fused_computation.clone.1 | convolution fusion | flops 1082130432 | bytes 29360132 | tf_op jit(solution)/shard_map/while/body/eval_jaxpr/sirc,sjorc->ocij/dot_general | solution.py:65
  503.2 6.0 %copy.65 = bf16[64,128,2,128]{1,0,2,3:T(8,128)(2,1)} copy(bf16[64,128,2,128]{1,0,2,3:T(8,128)(2,1)} %collective-permute-done) | data formatting | bytes 8388608 | tf_op jit(solution)/shard_map/while
  509.3 65.9 %copy.35 = f32[2,128,128,512]{3,2,1,0:T(8,128)} copy(f32[2,128,128,512]{2,3,0,1:T(8,128)} %get-tuple-element.138) | data formatting | bytes 134217728 | tf_op jit(solution)/shard_map/while | solution.py:83
  (9 shorter events, 0.0 us)
Async XLA Ops:
  18.1 4.4 copy-start.1
  26.8 72.2 %collective-permute-start.1 = (f32[3,128,2,1024]{3,1,2,0:T(8,128)S(1)}, f32[3,128,2,1024]{3,1,2,0:T(8,128)}, u32[]{:S(2)}, u32[]{:S(2)}) collective-permute-start(f32[3,128,2,1024]{3,1,2,0:T(8,128)S(1)} %copy.29), channel_id=1, source_target_pairs={{0,4},{4,8},{8,12},{12,16},{16,20},{20,24},{24,28},{1,5},{5,9},{9,... | collective-permute-start | bytes 9437192 | tf_op jit(solution)/shard_map/ppermute | solution.py:12
  101.3 2.7 copy-start.2
  104.4 2.7 copy-start.3
  104.4 2.7 copy-start.4
  148.5 99.3 %all-to-all-start = ((bf16[8,128,2,1024]{1,0,2,3:T(8,128)(2,1)}), bf16[8,128,2,1024]{1,0,2,3:T(8,128)(2,1)}, u32[]{:S(2)}, u32[]{:S(2)}) async-start(bf16[8,128,2,1024]{1,0,2,3:T(8,128)(2,1)} %copy.32), calls=%async_computation | async-start | bytes 8388608 | tf_op jit(solution)/shard_map/all_to_all | solution.py:55
  251.2 2.0 copy-start
  291.8 48.2 %collective-permute-start = (bf16[64,128,2,128]{1,0,2,3:T(8,128)(2,1)}, bf16[64,128,2,128]{1,0,2,3:T(8,128)(2,1)}, u32[]{:S(2)}, u32[]{:S(2)}) collective-permute-start(bf16[64,128,2,128]{1,0,2,3:T(8,128)(2,1)} %get-tuple-element.208), channel_id=1, source_target_pairs={{0,1},{1,2},{2,3},{3,0},{4,5},{5,6},{6,7},{7,4},{8,9},{9,10},{10,1... | collective-permute-start | bytes 12582920 | tf_op jit(solution)/shard_map/while/body/eval_jaxpr/ppermute | solution.py:18
  364.3 48.2 %collective-permute-start = (bf16[64,128,2,128]{1,0,2,3:T(8,128)(2,1)}, bf16[64,128,2,128]{1,0,2,3:T(8,128)(2,1)}, u32[]{:S(2)}, u32[]{:S(2)}) collective-permute-start(bf16[64,128,2,128]{1,0,2,3:T(8,128)(2,1)} %get-tuple-element.208), channel_id=1, source_target_pairs={{0,1},{1,2},{2,3},{3,0},{4,5},{5,6},{6,7},{7,4},{8,9},{9,10},{10,1... | collective-permute-start | bytes 12582920 | tf_op jit(solution)/shard_map/while/body/eval_jaxpr/ppermute | solution.py:18
  436.8 48.2 %collective-permute-start = (bf16[64,128,2,128]{1,0,2,3:T(8,128)(2,1)}, bf16[64,128,2,128]{1,0,2,3:T(8,128)(2,1)}, u32[]{:S(2)}, u32[]{:S(2)}) collective-permute-start(bf16[64,128,2,128]{1,0,2,3:T(8,128)(2,1)} %get-tuple-element.208), channel_id=1, source_target_pairs={{0,1},{1,2},{2,3},{3,0},{4,5},{5,6},{6,7},{7,4},{8,9},{9,10},{10,1... | collective-permute-start | bytes 12582920 | tf_op jit(solution)/shard_map/while/body/eval_jaxpr/ppermute | solution.py:18
where the time goes:
time: 577 us; the launch traced here: 575 us
  waiting for transfers between devices  264 us (46%)
  local copies, waits for them, and re-layouts  155 us (27%)
  matrix products  77.9 us (14%)
  other arithmetic  64.3 us (11%)
  starting transfers between devices  13.4 us (2%)
    ppermute x3, waiting for transfers between devices, passed_along(): return lax.ppermute(value, axis, pairs)  145 us
    all_to_all x1, waiting for transfers between devices, local(): lax.all_to_all(spectra, 'freq', split_axis=3, concat_axis=0, tiled=True)  92.4 us
    while x1, local copies, waits for them, and re-layouts, local(): carried = lax.fori_loop(1, count, advance, (turned, visible))  65.9 us
    dot_general x4, matrix products, correlate(): jnp.einsum('sirc,sjorc->ocij', turned, partner, preferred_element_type=jn...  52.5 us
    ppermute x1, waiting for transfers between devices, from_behind(): return lax.ppermute(shard, axis, pairs)  26.8 us
    dot_general x1, matrix products, local(): jnp.dot(weighted, dft_table(channels), preferred_element_type=jnp.float32)  25.4 us
    broadcast_in_dim x1, local copies, waits for them, and re-layouts, local(): visible = jnp.zeros((2, group, inputs_blk, inputs_blk * count), jnp.float32)  21.2 us
    while x3, local copies, waits for them, and re-layouts  18.1 us
  transfers between devices with their start and end apart: 5, of which 5 were waited for; matrix products, arithmetic and copies ran while one was open for 7% of the time, Pallas kernels for 0%

commit v1 on v0

v1 whole, which is shorter than its diff:
```python
import functools
import math

import jax
import jax.numpy as jnp
import numpy as np
from jax import lax
from jax.experimental import pallas as pl
from jax.experimental.pallas import tpu as pltpu
from jax.sharding import PartitionSpec as P

LATE_CHUNKS = 2
EARLY_CHUNKS = 4
MIB = 1 << 20


def swapped(value, axis, distance):
    pairs = [(i, i ^ distance) for i in range(lax.axis_size(axis))]
    return lax.ppermute(value, axis, pairs)


def from_behind(value, axis):
    pairs = [(i, i + 1) for i in range(lax.axis_size(axis) - 1)]
    return lax.ppermute(value, axis, pairs)


def dft_rows(channels, groups, chunks):
    n = np.arange(channels, dtype=np.int64)
    phase = ((n[:, None] * n[None, :]) % channels).astype(np.float32)
    phase = phase * np.float32(2.0 * math.pi / channels)
    factor = np.float32(1.0 / math.sqrt(channels))
    cosine = np.cos(phase.astype(np.float64)).astype(np.float32) * factor
    sine = np.sin(phase.astype(np.float64)).astype(np.float32) * factor
    real = np.concatenate([cosine, sine], axis=1)
    imag = np.concatenate([-sine, cosine], axis=1)
    rows = np.stack([real, imag]).astype(jnp.bfloat16)
    size = channels // groups // chunks
    rows = rows.reshape(2, groups, chunks, size, 2 * channels).transpose(2, 1, 0, 3, 4)
    return [rows[c].reshape(groups * 2 * size, 2 * channels) for c in range(chunks)]


def weigh(taps_ref, *refs):
    *parts, out_ref = refs
    channels = taps_ref.shape[1]
    frames = []
    for ref in parts:
        for f in range(ref.shape[2] // channels):
            frames.append((ref, f * channels))
    ntaps = taps_ref.shape[0]
    count = out_ref.shape[0]
    frames = frames[len(frames) - (count + ntaps - 1):]
    coeffs = taps_ref[...].astype(jnp.float32) * (1.0 / 1024.0)
    for part in range(2):
        held = [ref[part, :, at:at + channels].astype(jnp.float32) for ref, at in frames]
        for s in range(count):
            total = coeffs[0:1] * held[s]
            for t in range(1, ntaps):
                total = total + coeffs[t:t + 1] * held[s + t]
            out_ref[s, :, part * channels:(part + 1) * channels] = total.astype(jnp.bfloat16)


def weighted_spectra(taps, sources, count):
    channels = taps.shape[1]
    inputs = sources[0][0].shape[1]
    step = min(16, inputs)
    specs = [pl.BlockSpec(taps.shape, lambda i: (0, 0))]
    for array, at, width in sources:
        specs.append(pl.BlockSpec((2, step, width), lambda i, at=at: (0, i, at)))
    moved = sum(2 * inputs * w * a.dtype.itemsize for a, _, w in sources)
    return pl.pallas_call(
        weigh,
        out_shape=jax.ShapeDtypeStruct((count, inputs, 2 * channels), jnp.bfloat16),
        grid=(inputs // step,),
        in_specs=specs,
        out_specs=pl.BlockSpec((count, step, 2 * channels), lambda i: (0, i, 0)),
        cost_estimate=pl.CostEstimate(
            flops=count * inputs * channels * 16, bytes_accessed=moved + count * inputs * channels * 4, transcendentals=0
        ),
        compiler_params=pltpu.CompilerParams(vmem_limit_bytes=40 * MIB),
    )(taps, *[a for a, _, _ in sources])


def transform(weighted_ref, table_ref, out_ref, turned_ref):
    count, inputs, depth = weighted_ref.shape
    groups, pairs = out_ref.shape[0], out_ref.shape[1]
    size = 2 * pairs
    weighted = weighted_ref[...].reshape(count * inputs, depth)
    result = lax.dot_general(
        table_ref[...], weighted, (((1,), (1,)), ((), ())), preferred_element_type=jnp.float32
    )
    for g in range(groups):
        for part in range(2):
            base = (g * 2 + part) * size
            for s in range(count):
                turned_ref[g, :, part * count + s, :] = result[base:base + size, s * inputs:(s + 1) * inputs]
    out_ref[...] = turned_ref[...].reshape(groups, pairs, 4 * count, inputs).astype(jnp.bfloat16)


def spectra_of(weighted, table, groups):
    count, inputs, depth = weighted.shape
    size = table.shape[0] // groups // 2
    together = max(1, min(groups, 256 // (2 * size)))
    rows = together * 2 * size
    return pl.pallas_call(
        transform,
        out_shape=jax.ShapeDtypeStruct((groups, size // 2, 4 * count, inputs), jnp.bfloat16),
        grid=(groups // together,),
        in_specs=[
            pl.BlockSpec(weighted.shape, lambda g: (0, 0, 0)),
            pl.BlockSpec((rows, depth), lambda g: (g, 0)),
        ],
        out_specs=pl.BlockSpec((together, size // 2, 4 * count, inputs), lambda g: (g, 0, 0, 0)),
        scratch_shapes=[pltpu.VMEM((together, size, 2 * count, inputs), jnp.float32)],
        cost_estimate=pl.CostEstimate(
            flops=2 * table.shape[0] * depth * count * inputs, bytes_accessed=table.size * 2 + weighted.size * 4, transcendentals=0
        ),
        compiler_params=pltpu.CompilerParams(vmem_limit_bytes=40 * MIB),
    )(weighted, table)


def correlate(factor, blocks, me_ref, *refs):
    late, early = refs[:blocks], refs[blocks:2 * blocks]
    out_ref = refs[-1]
    groups, pairs, rows, inputs = late[0].shape
    half = rows // 2
    offsets = [
        pl.multiple_of(jnp.bitwise_xor(me_ref[0], q) * inputs, inputs) for q in range(blocks)
    ]
    sign = jnp.where(
        lax.broadcasted_iota(jnp.int32, (2 * groups, half, inputs), 1) < half // 2, factor, -factor
    ).astype(jnp.float32)

    def pair(p, carry):
        loaded = []
        for q in range(blocks):
            a = late[q][:, p].astype(jnp.float32).reshape(groups, 2, half, inputs)
            b = early[q][:, p].astype(jnp.float32).reshape(groups, 2, half, inputs)
            loaded.append((a, b))
        for h in range(2):
            whole = [jnp.concatenate([a[:, h], b[:, h]], axis=0) for a, b in loaded]
            flat = [w.reshape(2 * groups * half, inputs).astype(jnp.bfloat16) for w in whole]
            rotated = (pltpu.roll(whole[0], half // 2, axis=1) * sign).reshape(2 * groups * half, inputs)
            scaled = (whole[0] * factor).reshape(2 * groups * half, inputs)
            left = jnp.concatenate([scaled, rotated], axis=1).astype(jnp.bfloat16)
            for q in range(blocks):
                product = lax.dot_general(
                    left, flat[q], (((0,), (0,)), ((), ())), preferred_element_type=jnp.float32
                )
                out_ref[0, 2 * p + h, :, pl.ds(offsets[q], inputs)] = product[:inputs]
                out_ref[1, 2 * p + h, :, pl.ds(offsets[q], inputs)] = product[inputs:]
        return carry

    lax.fori_loop(0, pairs, pair, 0)


def correlated(me, late, early, at, late_at, total, factor, visible):
    blocks = len(late)
    groups, pairs, rows, inputs = early[0].shape
    step = min(4, pairs)
    size = 2 * step
    specs = [pl.BlockSpec((groups, step, rows, inputs), lambda i, m: (0, late_at // step + i, 0, 0))] * blocks
    specs += [pl.BlockSpec((groups, step, rows, inputs), lambda i, m: (0, i, 0, 0))] * blocks
    operands = [me, *late, *early]
    aliases = {}
    if visible is not None:
        aliases = {len(operands): 0}
        operands.append(visible)
        specs.append(pl.BlockSpec(memory_space=pl.ANY))
    wide = inputs * blocks
    depth = 2 * groups * rows // 2
    return pl.pallas_call(
        functools.partial(correlate, factor, blocks),
        out_shape=jax.ShapeDtypeStruct((2, total, inputs, wide), jnp.float32),
        grid_spec=pltpu.PrefetchScalarGridSpec(
            num_scalar_prefetch=1,
            grid=(pairs // step,),
            in_specs=specs,
            out_specs=pl.BlockSpec((2, size, inputs, wide), lambda i, m: (0, at // step + i, 0, 0)),
        ),
        input_output_aliases=aliases,
        cost_estimate=pl.CostEstimate(
            flops=2 * 2 * pairs * 2 * inputs * wide * depth, bytes_accessed=2 * pairs * 2 * inputs * wide * 4, transcendentals=0
        ),
        compiler_params=pltpu.CompilerParams(vmem_limit_bytes=48 * MIB),
    )(*operands)


def local(tables, voltages, taps):
    ntaps, channels = taps.shape
    inputs = voltages.shape[1]
    frames = voltages.shape[2] // channels
    groups = lax.axis_size("freq")
    blocks = lax.axis_size("blk")
    group = channels // groups
    early_tables, late_tables = tables
    half = frames // 2
    factor = 1.0 / math.sqrt(frames * groups)
    me = lax.axis_index("blk").astype(jnp.int32).reshape(1)

    tail = voltages[:, :, (frames - ntaps + 1) * channels:].astype(jnp.bfloat16)
    behind = from_behind(tail, "freq")
    late_weighted = weighted_spectra(taps, [(voltages, 0, frames * channels)], half)
    early_weighted = None

    late_sent = [spectra_of(late_weighted, late_tables[0], groups)]
    nlate, nearly = len(late_tables), len(early_tables)
    count = nlate + nearly
    turned = [None] * count
    visible = None
    sent = list(late_sent)
    for step in range(count + 3):
        made = {}
        if step < count:
            made["turn"] = lax.all_to_all(sent[step], "freq", split_axis=0, concat_axis=0, tiled=True)
        if 0 <= step - 1 < count:
            made["far"] = swapped(turned[step - 1][0], "blk", 2)
        if 0 <= step - 2 < count:
            held = turned[step - 2]
            made["near"] = (swapped(held[0], "blk", 1), swapped(held[2], "blk", 1))
        if step + 1 < nlate:
            made["next"] = spectra_of(late_weighted, late_tables[step + 1], groups)
        elif step + 1 < count:
            if early_weighted is None:
                early_weighted = weighted_spectra(
                    taps, [(behind, 0, (ntaps - 1) * channels), (voltages, 0, half * channels)], half
                )
            made["next"] = spectra_of(early_weighted, early_tables[step + 1 - nlate], groups)
        e = step - 3 - nlate
        if e >= 0:
            per = nearly // nlate
            a, b = turned[e // per], turned[nlate + e]
            size = group // nearly // 2
            visible = correlated(
                me, [a[q] for q in range(blocks)], [b[q] for q in range(blocks)],
                e * size, (e % per) * size, group, factor, visible,
            )
            if e + 1 == nearly:
                break
            made["visible"] = visible
        made, turned = lax.optimization_barrier((made, turned))
        visible = made.get("visible", visible)
        if "turn" in made:
            turned[step] = {0: made["turn"]}
        if "far" in made:
            turned[step - 1] = {**turned[step - 1], 2: made["far"]}
        if "near" in made:
            turned[step - 2] = {**turned[step - 2], 1: made["near"][0], 3: made["near"][1]}
        if "next" in made:
            sent.append(made["next"])
    return visible


def solution(mesh):
    groups = mesh.shape["freq"]

    def run(voltages, taps):
        channels = taps.shape[1]
        tables = (
            dft_rows(channels, groups, EARLY_CHUNKS),
            dft_rows(channels, groups, LATE_CHUNKS),
        )
        return jax.shard_map(
            functools.partial(local, tables),
            mesh=mesh,
            in_specs=(P(None, "blk", "freq"), P()),
            out_specs=P(None, "freq", "blk", None),
            check_vma=False,
        )(voltages, taps)

    return run
```

time: 577 us -> 233 us (0.40)
  waiting for transfers between devices: 264 us -> 85.5 us
  local copies, waits for them, and re-layouts: 155 us -> 22.4 us
  matrix products: 77.9 us -> 0 us
  other arithmetic: 64.3 us -> 2.27 us
  Pallas kernels: 0 us -> 59.9 us
  starting transfers between devices: 13.4 us -> 61.3 us
    ppermute x4 -> x19, waiting for transfers between devices: 172 us -> 54.8 us  [the longest x1 37.4 us: from_behind(): return lax.ppermute(value, axis, pairs)]
    while x4 -> x0, local copies, waits for them, and re-layouts: 84 us -> none  [the longest x1 65.9 us: local(): carried = lax.fori_loop(1, count, advance, (turned, visible))]
    dot_general x5 -> x0, matrix products: 77.9 us -> none  [the longest x4 52.5 us: correlate(): jnp.einsum('sirc,sjorc->ocij', turned, partner, preferred_element_type=jn...]
    all_to_all x1 -> x6, waiting for transfers between devices: 92.4 us -> 30.6 us  [local(): lax.all_to_all(sent[step], 'freq', split_axis=0, concat_axis=0, tiled=True)]
    pallas_call x0 -> x12, Pallas kernels: none -> 59.9 us  [the longest x4 38.7 us: correlated(): pl.pallas_call(functools.partial(correlate, factor, blocks), out_shape=ja...]
    all_to_all x1 -> x6, starting transfers between devices: 6.9 us -> 46 us  [local(): lax.all_to_all(sent[step], 'freq', split_axis=0, concat_axis=0, tiled=True)]
    neg x5 -> x0, other arithmetic: 24.9 us -> none  [the longest x1 16.5 us: dft_table(): upper = jnp.concatenate([cosine, -sine], axis=1)]
    convert_element_type x2 -> x0, other arithmetic: 21.9 us -> none  [the longest x1 18 us: dft_table(): sine = (jnp.sin(phase) * factor).astype(jnp.bfloat16)]
  transfers between devices with their start and end apart: 5 -> 25, of which waited for: 5 -> 7; matrix products, arithmetic and copies ran while one was open for 7% -> 1% of each run, Pallas kernels for 0% -> 19%
where the time goes in v1:
time: 233 us; the launch traced here: 232 us
  waiting for transfers between devices  85.5 us (37%)
  starting transfers between devices  61.3 us (26%)
  Pallas kernels  59.9 us (26%)
  local copies, waits for them, and re-layouts  22.4 us (10%)
    all_to_all x6, starting transfers between devices, local(): lax.all_to_all(sent[step], 'freq', split_axis=0, concat_axis=0, tiled=True)  46 us
    pallas_call x4, Pallas kernels, correlated(): pl.pallas_call(functools.partial(correlate, factor, blocks), out_shape=ja...  38.7 us
    ppermute x1, waiting for transfers between devices, from_behind(): return lax.ppermute(value, axis, pairs)  37.4 us
    all_to_all x6, waiting for transfers between devices, local(): lax.all_to_all(sent[step], 'freq', split_axis=0, concat_axis=0, tiled=True)  30.6 us
    unnamed x38, local copies, waits for them, and re-layouts  22.4 us
    ppermute x18, waiting for transfers between devices, swapped(): return lax.ppermute(value, axis, pairs)  17.5 us
    pallas_call x6, Pallas kernels, spectra_of(): pl.pallas_call(transform, out_shape=jax.ShapeDtypeStruct((groups, size //...  17 us
    ppermute x18, starting transfers between devices, swapped(): return lax.ppermute(value, axis, pairs)  11.4 us
  transfers between devices with their start and end apart: 25, of which 7 were waited for; matrix products, arithmetic and copies ran while one was open for 1% of the time, Pallas kernels for 19%

profile of v1, /device:TPU:0, one launch (start us, length us, event | category | flops | bytes accessed | tf_op | source)
XLA Modules:
  0.0 231.6 jit_solution(3653661687347475068)
XLA Ops:
  0.0 3.4 %copy-done = s32[2,128,8192]{2,1,0:T(8,128)S(1)} copy-done((s32[2,128,8192]{2,1,0:T(8,128)S(1)}, s32[2,128,8192]{2,1,0:T(8,128)}, u32[]{:S(2)}) %copy-start) | copy-done | bytes 8388632
  3.4 0.7 copy-done.15
  4.1 2.2 shard_map.82.weighted_ref
  6.3 4.8 %shard_map.84 = bf16[8,32,16,128]{3,2,1,0:T(8,128)(2,1)} custom-call(bf16[4,128,2048]{2,1,0:T(8,128)(2,1)S(1)} %shard_map.82.weighted_ref, bf16[1024,2048]{1,0:T(8,128)(2,1)S(1)} %copy-done.18), custom_call_target="tpu_custom_call" | custom-call | flops 2147483648 | bytes 8388608 | tf_op jit(solution)/shard_map/pallas_call | solution.py:104
  11.1 7.3 %all-to-all-start = ((bf16[8,32,16,128]{3,2,1,0:T(8,128)(2,1)}), bf16[8,32,16,128]{3,2,1,0:T(8,128)(2,1)}, u32[]{:S(2)}, u32[]{:S(2)}) async-start(bf16[8,32,16,128]{3,2,1,0:T(8,128)(2,1)} %shard_map.84), calls=%async_computation | async-start | bytes 2097152 | tf_op jit(solution)/shard_map/all_to_all | solution.py:214
  18.3 2.2 copy-done.17
  20.5 4.0 %shard_map.83 = bf16[8,32,16,128]{3,2,1,0:T(8,128)(2,1)S(1)} custom-call(bf16[4,128,2048]{2,1,0:T(8,128)(2,1)S(1)} %shard_map.82.weighted_ref, bf16[1024,2048]{1,0:T(8,128)(2,1)S(1)} %copy-done.17), custom_call_target="tpu_custom_call" | custom-call | flops 2147483648 | bytes 8388608 | tf_op jit(solution)/shard_map/pallas_call | solution.py:104
  24.6 1.0 copy-done.10
  25.6 18.7 %all-to-all-done.refs_0_ = bf16[8,32,16,128]{3,2,1,0:T(8,128)(2,1)} async-done(((bf16[8,32,16,128]{3,2,1,0:T(8,128)(2,1)}), bf16[8,32,16,128]{3,2,1,0:T(8,128)(2,1)}, u32[]{:S(2)}, u32[]{:S(2)}) %all-to-all-start) | async-done | bytes 1048608 | tf_op jit(solution)/shard_map/all_to_all | solution.py:214
  44.2 3.6 %all-to-all-start.1 = ((bf16[8,32,16,128]{3,2,1,0:T(8,128)(2,1)}), bf16[8,32,16,128]{3,2,1,0:T(8,128)(2,1)S(1)}, u32[]{:S(2)}, u32[]{:S(2)}) async-start(bf16[8,32,16,128]{3,2,1,0:T(8,128)(2,1)} %copy-done.10), calls=%async_computation.1 | async-start | bytes 2097152 | tf_op jit(solution)/shard_map/all_to_all | solution.py:214
  47.8 2.3 slice_convert_fusion
  50.1 4.0 %collective-permute-start.1 = (bf16[2,128,3072]{2,1,0:T(8,128)(2,1)S(1)}, bf16[2,128,3072]{2,1,0:T(8,128)(2,1)S(1)}, u32[]{:S(2)}, u32[]{:S(2)}) collective-permute-start(bf16[2,128,3072]{2,1,0:T(8,128)(2,1)S(1)} %slice_convert_fusion), channel_id=1, source_target_pairs={{0,4},{4,8},{8,12},{12,16},{16,20},{20,24},{24,28},{1,5},{5,9},{9,... | collective-permute-start | bytes 4718600 | tf_op jit(solution)/shard_map/ppermute | solution.py:24
  54.1 1.6 collective-permute-start
  55.7 37.4 %collective-permute-done.1.refs_0_ = bf16[2,128,3072]{2,1,0:T(8,128)(2,1)S(1)} collective-permute-done((bf16[2,128,3072]{2,1,0:T(8,128)(2,1)S(1)}, bf16[2,128,3072]{2,1,0:T(8,128)(2,1)S(1)}, u32[]{:S(2)}, u32[]{:S(2)}) %collective-permute-start.1) | collective-permute-done | bytes 1572896 | tf_op jit(solution)/shard_map/ppermute | solution.py:24
  93.1 3.4 %copy-done.1 = s32[2,128,8192]{2,1,0:T(8,128)S(1)} copy-done((s32[2,128,8192]{2,1,0:T(8,128)S(1)}, s32[2,128,8192]{2,1,0:T(8,128)}, u32[]{:S(2)}) %copy-start.1) | copy-done | bytes 8388632
  96.5 2.0 shard_map.85.weighted_ref
  98.5 2.0 shard_map.86
  100.6 0.8 copy-done.5
  101.5 1.5 collective-permute-start.2
  103.5 17.2 %all-to-all-start.2 = ((bf16[8,16,16,128]{3,2,1,0:T(8,128)(2,1)}), bf16[8,16,16,128]{3,2,1,0:T(8,128)(2,1)}, u32[]{:S(2)}, u32[]{:S(2)}) async-start(bf16[8,16,16,128]{3,2,1,0:T(8,128)(2,1)} %copy-done.5), calls=%async_computation.2 | async-start | bytes 1048576 | tf_op jit(solution)/shard_map/all_to_all | solution.py:214
  120.6 1.6 copy-done.8
  122.2 2.0 shard_map.87
  124.3 0.8 copy-done.4
  125.1 10.7 %all-to-all-done.2.refs_4_ = bf16[8,16,16,128]{3,2,1,0:T(8,128)(2,1)} async-done(((bf16[8,16,16,128]{3,2,1,0:T(8,128)(2,1)}), bf16[8,16,16,128]{3,2,1,0:T(8,128)(2,1)}, u32[]{:S(2)}, u32[]{:S(2)}) %all-to-all-start.2) | async-done | bytes 524320 | tf_op jit(solution)/shard_map/all_to_all | solution.py:214
  136.4 7.9 %all-to-all-start.3 = ((bf16[8,16,16,128]{3,2,1,0:T(8,128)(2,1)}), bf16[8,16,16,128]{3,2,1,0:T(8,128)(2,1)}, u32[]{:S(2)}, u32[]{:S(2)}) async-start(bf16[8,16,16,128]{3,2,1,0:T(8,128)(2,1)} %copy-done.4), calls=%async_computation.3 | async-start | bytes 1048576 | tf_op jit(solution)/shard_map/all_to_all | solution.py:214
  144.3 1.5 collective-permute-start.5
  145.8 1.6 copy-done.7
  147.4 2.0 shard_map.88
  149.5 0.8 copy-done.3
  150.3 8.0 %collective-permute-done.5.refs_6_ = bf16[8,16,16,128]{3,2,1,0:T(8,128)(2,1)} collective-permute-done((bf16[8,16,16,128]{3,2,1,0:T(8,128)(2,1)}, bf16[8,16,16,128]{3,2,1,0:T(8,128)(2,1)}, u32[]{:S(2)}, u32[]{:S(2)}) %collective-permute-start.5) | collective-permute-done | bytes 524320 | tf_op jit(solution)/shard_map/ppermute | solution.py:19
  158.3 1.3 all-to-all-done.3.refs_4_
  159.6 4.4 %all-to-all-start.4 = ((bf16[8,16,16,128]{3,2,1,0:T(8,128)(2,1)}), bf16[8,16,16,128]{3,2,1,0:T(8,128)(2,1)}, u32[]{:S(2)}, u32[]{:S(2)}) async-start(bf16[8,16,16,128]{3,2,1,0:T(8,128)(2,1)} %copy-done.3), calls=%async_computation.4 | async-start | bytes 1048576 | tf_op jit(solution)/shard_map/all_to_all | solution.py:214
  164.0 1.5 collective-permute-start.8
  166.0 1.6 copy-done.6
  167.6 2.0 shard_map.89
  169.7 0.8 copy-done.2
  170.5 6.5 %collective-permute-done.8.refs_6_ = bf16[8,16,16,128]{3,2,1,0:T(8,128)(2,1)} collective-permute-done((bf16[8,16,16,128]{3,2,1,0:T(8,128)(2,1)}, bf16[8,16,16,128]{3,2,1,0:T(8,128)(2,1)}, u32[]{:S(2)}, u32[]{:S(2)}) %collective-permute-start.8) | collective-permute-done | bytes 524320 | tf_op jit(solution)/shard_map/ppermute | solution.py:19
  177.0 0.8 copy-done.11
  177.8 0.8 copy-done.13
  178.6 5.6 %all-to-all-start.5 = ((bf16[8,16,16,128]{3,2,1,0:T(8,128)(2,1)}), bf16[8,16,16,128]{3,2,1,0:T(8,128)(2,1)S(1)}, u32[]{:S(2)}, u32[]{:S(2)}) async-start(bf16[8,16,16,128]{3,2,1,0:T(8,128)(2,1)} %copy-done.2), calls=%async_computation.5 | async-start | bytes 1048576 | tf_op jit(solution)/shard_map/all_to_all | solution.py:214
  184.2 1.5 collective-permute-start.11
  186.2 1.0 copy-done.12
  187.2 1.0 copy-done.14
  188.3 9.9 %shard_map.90.refs_8_ = f32[2,128,128,512]{3,2,1,0:T(8,128)} custom-call(s32[1]{0:T(128)} %bitcast.me_ref, bf16[8,32,16,128]{3,2,1,0:T(8,128)(2,1)} %all-to-all-done.refs_0_, bf16[8,32,16,128]{3,2,1,0:T(8,128)(2,1)} %collective-permute-done.3.refs_1_, bf16[8,32,16,128]{3,2,1,0:T(8,128)(2,1)} %collective-permute-done.refs_2_, ...), custom_call_target="tpu_custom_call" | custom-call | flops 1073741824 | bytes 16777216 | tf_op jit(solution)/shard_map/pallas_call | solution.py:171
  199.3 9.9 %shard_map.91.refs_8_ = f32[2,128,128,512]{3,2,1,0:T(8,128)} custom-call(s32[1]{0:T(128)} %bitcast.me_ref, bf16[8,32,16,128]{3,2,1,0:T(8,128)(2,1)} %all-to-all-done.refs_0_, bf16[8,32,16,128]{3,2,1,0:T(8,128)(2,1)} %collective-permute-done.3.refs_1_, bf16[8,32,16,128]{3,2,1,0:T(8,128)(2,1)} %collective-permute-done.refs_2_, ...), custom_call_target="tpu_custom_call", output_to_operand_aliasing={{}: (9, {})} | custom-call | flops 1073741824 | bytes 16777216 | tf_op jit(solution)/shard_map/pallas_call | solution.py:171
  209.2 2.9 %collective-permute-done.14.refs_6_ = bf16[8,16,16,128]{3,2,1,0:T(8,128)(2,1)S(1)} collective-permute-done((bf16[8,16,16,128]{3,2,1,0:T(8,128)(2,1)S(1)}, bf16[8,16,16,128]{3,2,1,0:T(8,128)(2,1)S(1)}, u32[]{:S(2)}, u32[]{:S(2)}) %collective-permute-start.14) | collective-permute-done | bytes 524320 | tf_op jit(solution)/shard_map/ppermute | solution.py:19
  212.6 9.6 %shard_map.92.refs_8_ = f32[2,128,128,512]{3,2,1,0:T(8,128)} custom-call(s32[1]{0:T(128)} %bitcast.me_ref, bf16[8,32,16,128]{3,2,1,0:T(8,128)(2,1)S(1)} %all-to-all-done.1.refs_0_, bf16[8,32,16,128]{3,2,1,0:T(8,128)(2,1)} %collective-permute-done.6.refs_1_, bf16[8,32,16,128]{3,2,1,0:T(8,128)(2,1)} %collective-permute-done.2.refs_2_, ...), custom_call_target="tpu_custom_call", output_to_operand_aliasing={{}: (9, {})} | custom-call | flops 1073741824 | bytes 16777216 | tf_op jit(solution)/shard_map/pallas_call | solution.py:171
  222.2 9.4 %shard_map.93 = f32[2,128,128,512]{3,2,1,0:T(8,128)} custom-call(s32[1]{0:T(128)} %bitcast.me_ref, bf16[8,32,16,128]{3,2,1,0:T(8,128)(2,1)S(1)} %all-to-all-done.1.refs_0_, bf16[8,32,16,128]{3,2,1,0:T(8,128)(2,1)} %collective-permute-done.6.refs_1_, bf16[8,32,16,128]{3,2,1,0:T(8,128)(2,1)} %collective-permute-done.2.refs_2_, ...), custom_call_target="tpu_custom_call", output_to_operand_aliasing={{}: (9, {})} | custom-call | flops 1073741824 | bytes 16777216 | tf_op jit(solution)/shard_map/pallas_call | solution.py:171
  (53 shorter events, 3.8 us)
Async XLA Ops:
  0.0 3.4 %copy-start = (s32[2,128,8192]{2,1,0:T(8,128)S(1)}, s32[2,128,8192]{2,1,0:T(8,128)}, u32[]{:S(2)}) copy-start(s32[2,128,8192]{2,1,0:T(8,128)} %refs_1_.1) | copy-start | bytes 25165828
  3.4 0.7 copy-start.15
  4.1 2.2 copy-start.18
  11.1 33.1 %all-to-all-start = ((bf16[8,32,16,128]{3,2,1,0:T(8,128)(2,1)}), bf16[8,32,16,128]{3,2,1,0:T(8,128)(2,1)}, u32[]{:S(2)}, u32[]{:S(2)}) async-start(bf16[8,32,16,128]{3,2,1,0:T(8,128)(2,1)} %shard_map.84), calls=%async_computation | async-start | bytes 2097152 | tf_op jit(solution)/shard_map/all_to_all | solution.py:214
  18.3 2.2 copy-start.17
  24.6 1.0 copy-start.10
  25.6 67.5 %copy-start.16 = (s32[4,1024]{1,0:T(4,128)S(1)}, s32[4,1024]{1,0:T(4,128)}, u32[]{:S(2)}) copy-start(s32[4,1024]{1,0:T(4,128)} %taps_ref.3) | copy-start | bytes 49156
  44.2 57.2 %all-to-all-start.1 = ((bf16[8,32,16,128]{3,2,1,0:T(8,128)(2,1)}), bf16[8,32,16,128]{3,2,1,0:T(8,128)(2,1)S(1)}, u32[]{:S(2)}, u32[]{:S(2)}) async-start(bf16[8,32,16,128]{3,2,1,0:T(8,128)(2,1)} %copy-done.10), calls=%async_computation.1 | async-start | bytes 2097152 | tf_op jit(solution)/shard_map/all_to_all | solution.py:214
  47.8 50.7 %copy-start.9 = (bf16[512,2048]{1,0:T(8,128)(2,1)S(1)}, bf16[512,2048]{1,0:T(8,128)(2,1)}, u32[]{:S(2)}) copy-start(bf16[512,2048]{1,0:T(8,128)(2,1)} %constant.18.clone.table_ref) | copy-start | bytes 6291460
  50.1 43.0 %collective-permute-start.1 = (bf16[2,128,3072]{2,1,0:T(8,128)(2,1)S(1)}, bf16[2,128,3072]{2,1,0:T(8,128)(2,1)S(1)}, u32[]{:S(2)}, u32[]{:S(2)}) collective-permute-start(bf16[2,128,3072]{2,1,0:T(8,128)(2,1)S(1)} %slice_convert_fusion), channel_id=1, source_target_pairs={{0,4},{4,8},{8,12},{12,16},{16,20},{20,24},{24,28},{1,5},{5,9},{9,... | collective-permute-start | bytes 4718600 | tf_op jit(solution)/shard_map/ppermute | solution.py:24
  54.1 47.3 %collective-permute-start = (bf16[8,32,16,128]{3,2,1,0:T(8,128)(2,1)}, bf16[8,32,16,128]{3,2,1,0:T(8,128)(2,1)}, u32[]{:S(2)}, u32[]{:S(2)}) collective-permute-start(bf16[8,32,16,128]{3,2,1,0:T(8,128)(2,1)} %all-to-all-done.refs_0_), channel_id=1, source_target_pairs={{0,2},{1,3},{2,0},{3,1},{4,6},{5,7},{6,4},{7,5},{8,10},{9,11},{10,... | collective-permute-start | bytes 3145736 | tf_op jit(solution)/shard_map/ppermute | solution.py:19
  93.1 3.4 %copy-start.1 = (s32[2,128,8192]{2,1,0:T(8,128)S(1)}, s32[2,128,8192]{2,1,0:T(8,128)}, u32[]{:S(2)}) copy-start(s32[2,128,8192]{2,1,0:T(8,128)} %refs_1_.1) | copy-start | bytes 25165828
  100.6 0.8 copy-start.5
  101.5 34.3 %collective-permute-start.2 = (bf16[8,32,16,128]{3,2,1,0:T(8,128)(2,1)S(1)}, bf16[8,32,16,128]{3,2,1,0:T(8,128)(2,1)}, u32[]{:S(2)}, u32[]{:S(2)}) collective-permute-start(bf16[8,32,16,128]{3,2,1,0:T(8,128)(2,1)S(1)} %all-to-all-done.1.refs_0_), channel_id=1, source_target_pairs={{0,2},{1,3},{2,0},{3,1},{4,6},{5,7},{6,4},{7,5},{8,10},{9,11},{10,... | collective-permute-start | bytes 3145736 | tf_op jit(solution)/shard_map/ppermute | solution.py:19
  103.0 32.8 %collective-permute-start.3 = (bf16[8,32,16,128]{3,2,1,0:T(8,128)(2,1)}, bf16[8,32,16,128]{3,2,1,0:T(8,128)(2,1)}, u32[]{:S(2)}, u32[]{:S(2)}) collective-permute-start(bf16[8,32,16,128]{3,2,1,0:T(8,128)(2,1)} %all-to-all-done.refs_0_), channel_id=1, source_target_pairs={{0,1},{1,0},{2,3},{3,2},{4,5},{5,4},{6,7},{7,6},{8,9},{9,8},{10,11... | collective-permute-start | bytes 3145736 | tf_op jit(solution)/shard_map/ppermute | solution.py:19
  103.0 32.8 %collective-permute-start.4 = (bf16[8,32,16,128]{3,2,1,0:T(8,128)(2,1)}, bf16[8,32,16,128]{3,2,1,0:T(8,128)(2,1)}, u32[]{:S(2)}, u32[]{:S(2)}) collective-permute-start(bf16[8,32,16,128]{3,2,1,0:T(8,128)(2,1)} %collective-permute-done.refs_2_), channel_id=1, source_target_pairs={{0,1},{1,0},{2,3},{3,2},{4,5},{5,4},{6,7},{7,6},{8,9},{9,8},{10,11... | collective-permute-start | bytes 3145736 | tf_op jit(solution)/shard_map/ppermute | solution.py:19
  103.5 32.3 %all-to-all-start.2 = ((bf16[8,16,16,128]{3,2,1,0:T(8,128)(2,1)}), bf16[8,16,16,128]{3,2,1,0:T(8,128)(2,1)}, u32[]{:S(2)}, u32[]{:S(2)}) async-start(bf16[8,16,16,128]{3,2,1,0:T(8,128)(2,1)} %copy-done.5), calls=%async_computation.2 | async-start | bytes 1048576 | tf_op jit(solution)/shard_map/all_to_all | solution.py:214
  120.6 1.6 copy-start.8
  124.3 0.8 copy-start.4
  135.8 23.8 %collective-permute-start.6 = (bf16[8,32,16,128]{3,2,1,0:T(8,128)(2,1)S(1)}, bf16[8,32,16,128]{3,2,1,0:T(8,128)(2,1)}, u32[]{:S(2)}, u32[]{:S(2)}) collective-permute-start(bf16[8,32,16,128]{3,2,1,0:T(8,128)(2,1)S(1)} %all-to-all-done.1.refs_0_), channel_id=1, source_target_pairs={{0,1},{1,0},{2,3},{3,2},{4,5},{5,4},{6,7},{7,6},{8,9},{9,8},{10,11... | collective-permute-start | bytes 3145736 | tf_op jit(solution)/shard_map/ppermute | solution.py:19
  135.9 23.7 %collective-permute-start.7 = (bf16[8,32,16,128]{3,2,1,0:T(8,128)(2,1)}, bf16[8,32,16,128]{3,2,1,0:T(8,128)(2,1)}, u32[]{:S(2)}, u32[]{:S(2)}) collective-permute-start(bf16[8,32,16,128]{3,2,1,0:T(8,128)(2,1)} %collective-permute-done.2.refs_2_), channel_id=1, source_target_pairs={{0,1},{1,0},{2,3},{3,2},{4,5},{5,4},{6,7},{7,6},{8,9},{9,8},{10,11... | collective-permute-start | bytes 3145736 | tf_op jit(solution)/shard_map/ppermute | solution.py:19
  136.4 23.2 %all-to-all-start.3 = ((bf16[8,16,16,128]{3,2,1,0:T(8,128)(2,1)}), bf16[8,16,16,128]{3,2,1,0:T(8,128)(2,1)}, u32[]{:S(2)}, u32[]{:S(2)}) async-start(bf16[8,16,16,128]{3,2,1,0:T(8,128)(2,1)} %copy-done.4), calls=%async_computation.3 | async-start | bytes 1048576 | tf_op jit(solution)/shard_map/all_to_all | solution.py:214
  144.3 13.9 %collective-permute-start.5 = (bf16[8,16,16,128]{3,2,1,0:T(8,128)(2,1)}, bf16[8,16,16,128]{3,2,1,0:T(8,128)(2,1)}, u32[]{:S(2)}, u32[]{:S(2)}) collective-permute-start(bf16[8,16,16,128]{3,2,1,0:T(8,128)(2,1)} %all-to-all-done.2.refs_4_), channel_id=1, source_target_pairs={{0,2},{1,3},{2,0},{3,1},{4,6},{5,7},{6,4},{7,5},{8,10},{9,11},{10,... | collective-permute-start | bytes 1572872 | tf_op jit(solution)/shard_map/ppermute | solution.py:19
  145.8 1.6 copy-start.7
  149.5 0.8 copy-start.3
  159.6 19.1 %all-to-all-start.4 = ((bf16[8,16,16,128]{3,2,1,0:T(8,128)(2,1)}), bf16[8,16,16,128]{3,2,1,0:T(8,128)(2,1)}, u32[]{:S(2)}, u32[]{:S(2)}) async-start(bf16[8,16,16,128]{3,2,1,0:T(8,128)(2,1)} %copy-done.3), calls=%async_computation.4 | async-start | bytes 1048576 | tf_op jit(solution)/shard_map/all_to_all | solution.py:214
  164.0 13.0 %collective-permute-start.8 = (bf16[8,16,16,128]{3,2,1,0:T(8,128)(2,1)}, bf16[8,16,16,128]{3,2,1,0:T(8,128)(2,1)}, u32[]{:S(2)}, u32[]{:S(2)}) collective-permute-start(bf16[8,16,16,128]{3,2,1,0:T(8,128)(2,1)} %all-to-all-done.3.refs_4_), channel_id=1, source_target_pairs={{0,2},{1,3},{2,0},{3,1},{4,6},{5,7},{6,4},{7,5},{8,10},{9,11},{10,... | collective-permute-start | bytes 1572872 | tf_op jit(solution)/shard_map/ppermute | solution.py:19
  165.5 11.5 %collective-permute-start.9 = (bf16[8,16,16,128]{3,2,1,0:T(8,128)(2,1)}, bf16[8,16,16,128]{3,2,1,0:T(8,128)(2,1)S(1)}, u32[]{:S(2)}, u32[]{:S(2)}) collective-permute-start(bf16[8,16,16,128]{3,2,1,0:T(8,128)(2,1)} %all-to-all-done.2.refs_4_), channel_id=1, source_target_pairs={{0,1},{1,0},{2,3},{3,2},{4,5},{5,4},{6,7},{7,6},{8,9},{9,8},{10,11... | collective-permute-start | bytes 1572872 | tf_op jit(solution)/shard_map/ppermute | solution.py:19
  165.5 12.3 %collective-permute-start.10 = (bf16[8,16,16,128]{3,2,1,0:T(8,128)(2,1)}, bf16[8,16,16,128]{3,2,1,0:T(8,128)(2,1)S(1)}, u32[]{:S(2)}, u32[]{:S(2)}) collective-permute-start(bf16[8,16,16,128]{3,2,1,0:T(8,128)(2,1)} %collective-permute-done.5.refs_6_), channel_id=1, source_target_pairs={{0,1},{1,0},{2,3},{3,2},{4,5},{5,4},{6,7},{7,6},{8,9},{9,8},{10,11... | collective-permute-start | bytes 1572872 | tf_op jit(solution)/shard_map/ppermute | solution.py:19
  166.0 1.6 copy-start.6
  169.7 0.8 copy-start.2
  177.0 0.8 copy-start.11
  177.8 0.8 copy-start.13
  178.6 19.6 %all-to-all-start.5 = ((bf16[8,16,16,128]{3,2,1,0:T(8,128)(2,1)}), bf16[8,16,16,128]{3,2,1,0:T(8,128)(2,1)S(1)}, u32[]{:S(2)}, u32[]{:S(2)}) async-start(bf16[8,16,16,128]{3,2,1,0:T(8,128)(2,1)} %copy-done.2), calls=%async_computation.5 | async-start | bytes 1048576 | tf_op jit(solution)/shard_map/all_to_all | solution.py:214
  184.2 14.0 %collective-permute-start.11 = (bf16[8,16,16,128]{3,2,1,0:T(8,128)(2,1)}, bf16[8,16,16,128]{3,2,1,0:T(8,128)(2,1)S(1)}, u32[]{:S(2)}, u32[]{:S(2)}) collective-permute-start(bf16[8,16,16,128]{3,2,1,0:T(8,128)(2,1)} %all-to-all-done.4.refs_4_), channel_id=1, source_target_pairs={{0,2},{1,3},{2,0},{3,1},{4,6},{5,7},{6,4},{7,5},{8,10},{9,11},{10,... | collective-permute-start | bytes 1572872 | tf_op jit(solution)/shard_map/ppermute | solution.py:19
  185.7 12.5 %collective-permute-start.12 = (bf16[8,16,16,128]{3,2,1,0:T(8,128)(2,1)}, bf16[8,16,16,128]{3,2,1,0:T(8,128)(2,1)S(1)}, u32[]{:S(2)}, u32[]{:S(2)}) collective-permute-start(bf16[8,16,16,128]{3,2,1,0:T(8,128)(2,1)} %all-to-all-done.3.refs_4_), channel_id=1, source_target_pairs={{0,1},{1,0},{2,3},{3,2},{4,5},{5,4},{6,7},{7,6},{8,9},{9,8},{10,11... | collective-permute-start | bytes 1572872 | tf_op jit(solution)/shard_map/ppermute | solution.py:19
  185.7 12.5 %collective-permute-start.13 = (bf16[8,16,16,128]{3,2,1,0:T(8,128)(2,1)}, bf16[8,16,16,128]{3,2,1,0:T(8,128)(2,1)S(1)}, u32[]{:S(2)}, u32[]{:S(2)}) collective-permute-start(bf16[8,16,16,128]{3,2,1,0:T(8,128)(2,1)} %collective-permute-done.8.refs_6_), channel_id=1, source_target_pairs={{0,1},{1,0},{2,3},{3,2},{4,5},{5,4},{6,7},{7,6},{8,9},{9,8},{10,11... | collective-permute-start | bytes 1572872 | tf_op jit(solution)/shard_map/ppermute | solution.py:19
  186.2 1.0 copy-start.12
  187.2 1.0 copy-start.14
  198.2 13.9 %collective-permute-start.14 = (bf16[8,16,16,128]{3,2,1,0:T(8,128)(2,1)S(1)}, bf16[8,16,16,128]{3,2,1,0:T(8,128)(2,1)S(1)}, u32[]{:S(2)}, u32[]{:S(2)}) collective-permute-start(bf16[8,16,16,128]{3,2,1,0:T(8,128)(2,1)S(1)} %all-to-all-done.5.refs_4_), channel_id=1, source_target_pairs={{0,2},{1,3},{2,0},{3,1},{4,6},{5,7},{6,4},{7,5},{8,10},{9,11},{10,... | collective-permute-start | bytes 1572872 | tf_op jit(solution)/shard_map/ppermute | solution.py:19
  198.8 13.3 %collective-permute-start.15 = (bf16[8,16,16,128]{3,2,1,0:T(8,128)(2,1)}, bf16[8,16,16,128]{3,2,1,0:T(8,128)(2,1)S(1)}, u32[]{:S(2)}, u32[]{:S(2)}) collective-permute-start(bf16[8,16,16,128]{3,2,1,0:T(8,128)(2,1)} %all-to-all-done.4.refs_4_), channel_id=1, source_target_pairs={{0,1},{1,0},{2,3},{3,2},{4,5},{5,4},{6,7},{7,6},{8,9},{9,8},{10,11... | collective-permute-start | bytes 1572872 | tf_op jit(solution)/shard_map/ppermute | solution.py:19
  198.8 13.3 %collective-permute-start.16 = (bf16[8,16,16,128]{3,2,1,0:T(8,128)(2,1)S(1)}, bf16[8,16,16,128]{3,2,1,0:T(8,128)(2,1)S(1)}, u32[]{:S(2)}, u32[]{:S(2)}) collective-permute-start(bf16[8,16,16,128]{3,2,1,0:T(8,128)(2,1)S(1)} %collective-permute-done.11.refs_6_), channel_id=1, source_target_pairs={{0,1},{1,0},{2,3},{3,2},{4,5},{5,4},{6,7},{7,6},{8,9},{9,8},{10,11... | collective-permute-start | bytes 1572872 | tf_op jit(solution)/shard_map/ppermute | solution.py:19
  212.1 10.1 %collective-permute-start.17 = (bf16[8,16,16,128]{3,2,1,0:T(8,128)(2,1)S(1)}, bf16[8,16,16,128]{3,2,1,0:T(8,128)(2,1)S(1)}, u32[]{:S(2)}, u32[]{:S(2)}) collective-permute-start(bf16[8,16,16,128]{3,2,1,0:T(8,128)(2,1)S(1)} %all-to-all-done.5.refs_4_), channel_id=1, source_target_pairs={{0,1},{1,0},{2,3},{3,2},{4,5},{5,4},{6,7},{7,6},{8,9},{9,8},{10,11... | collective-permute-start | bytes 1572872 | tf_op jit(solution)/shard_map/ppermute | solution.py:19
  212.1 10.1 %collective-permute-start.18 = (bf16[8,16,16,128]{3,2,1,0:T(8,128)(2,1)S(1)}, bf16[8,16,16,128]{3,2,1,0:T(8,128)(2,1)S(1)}, u32[]{:S(2)}, u32[]{:S(2)}) collective-permute-start(bf16[8,16,16,128]{3,2,1,0:T(8,128)(2,1)S(1)} %collective-permute-done.14.refs_6_), channel_id=1, source_target_pairs={{0,1},{1,0},{2,3},{3,2},{4,5},{5,4},{6,7},{7,6},{8,9},{9,8},{10,11... | collective-permute-start | bytes 1572872 | tf_op jit(solution)/shard_map/ppermute | solution.py:19

commit v2 on v0

v2 whole, which is shorter than its diff:
```python
import functools
import math

import jax
import jax.numpy as jnp
import numpy as np
from jax import lax
from jax.experimental import pallas as pl
from jax.experimental.pallas import tpu as pltpu
from jax.sharding import PartitionSpec as P

EARLY = (7, 5, 4)
MIB = 1 << 20
VMEM = 60 * MIB
RATED = 10**11


def swapped(value, axis, distance):
    pairs = [(i, i ^ distance) for i in range(lax.axis_size(axis))]
    return lax.ppermute(value, axis, pairs)


def handed(value, even=True):
    groups, blocks = lax.axis_size("freq"), lax.axis_size("blk")
    pairs = []
    for f in range(groups):
        for k in range(blocks):
            if k % 2 == 1:
                pairs.append((f * blocks + k, (f - 1) % groups * blocks + k))
            elif even and f + 1 < groups:
                pairs.append((f * blocks + k, (f + 1) * blocks + k))
    return lax.ppermute(value, ("freq", "blk"), pairs)


def reached(f, groups, shift, other):
    return (f // 2 + shift) % (groups // 2) * 2 + (f % 2 + other) % 2


def shifted(value, shift, other):
    groups = lax.axis_size("freq")
    pairs = [(f, reached(f, groups, shift, other)) for f in range(groups)]
    return lax.ppermute(value, "freq", pairs)


def cuts(pairs, shares):
    unit = pairs // 16
    ends = [0]
    for share in shares:
        ends.append(ends[-1] + share * unit)
    return ends


def dft_rows(channels, groups, parts):
    n = np.arange(channels, dtype=np.int64)
    phase = ((n[:, None] * n[None, :]) % channels).astype(np.float32)
    phase = phase * np.float32(2.0 * math.pi / channels)
    factor = np.float32(1.0 / math.sqrt(channels))
    cosine = np.cos(phase.astype(np.float64)).astype(np.float32) * factor
    sine = np.sin(phase.astype(np.float64)).astype(np.float32) * factor
    real = np.concatenate([cosine, sine], axis=1)
    imag = np.concatenate([-sine, cosine], axis=1)
    rows = np.stack([real, imag]).astype(jnp.bfloat16)
    rows = rows.reshape(2, groups, channels // groups, 2 * channels).transpose(1, 0, 2, 3)
    return [rows[:, :, 2 * a:2 * b].reshape(groups, -1, 2 * channels) for a, b in parts]


def weigh_frames(taps_ref, frames, out_ref):
    ntaps, channels = taps_ref.shape
    coeffs = taps_ref[...].astype(jnp.float32) * (1.0 / 1024.0)
    for part in range(2):
        held = [frame(part).astype(jnp.float32) for frame in frames]
        for s in range(out_ref.shape[0]):
            total = coeffs[0:1] * held[s]
            for t in range(1, ntaps):
                total = total + coeffs[t:t + 1] * held[s + t]
            out_ref[s, :, part * channels:(part + 1) * channels] = total.astype(jnp.bfloat16)


def frames_of(refs, first, last, channels):
    return [lambda part, f=f: refs[part][0, :, f * channels:(f + 1) * channels] for f in range(first, last)]


def weigh_late(taps_ref, real_ref, imag_ref, out_ref):
    ntaps, channels = taps_ref.shape
    frames = real_ref.shape[2] // channels
    first = frames - out_ref.shape[0] - ntaps + 1
    weigh_frames(taps_ref, frames_of((real_ref, imag_ref), first, frames, channels), out_ref)


def weigh_early(where_ref, taps_ref, real_ref, imag_ref, *refs):
    ntaps, channels = taps_ref.shape
    volts = (real_ref, imag_ref)
    frames = real_ref.shape[2] // channels
    passed, more, out_ref = refs[:2], refs[2:4], refs[4]
    count = out_ref.shape[0]

    @pl.when(where_ref[0] == 0)
    def _():
        before = frames_of(passed, 0, ntaps - 1, channels)
        weigh_frames(taps_ref, before + frames_of(volts, 0, count, channels), out_ref)

    @pl.when(where_ref[0] != 0)
    def _():
        keep = where_ref[1]
        before = [
            lambda part, frame=frame: frame(part) * keep
            for frame in frames_of(volts, frames - ntaps + 1, frames, channels)
        ]
        after = frames_of(passed, 0, ntaps - 1, channels) + frames_of(more, 0, count - ntaps + 1, channels)
        weigh_frames(taps_ref, before + after, out_ref)


def weighted_spectra(taps, voltages, count, where=None, passed=()):
    channels = taps.shape[1]
    _, inputs, samples = voltages.shape
    step = min(64, inputs)
    operands = [taps]
    specs = [pl.BlockSpec(taps.shape, lambda i, *_: (0, 0))]
    for array in (voltages, *passed):
        for part in range(2):
            operands.append(array)
            specs.append(pl.BlockSpec((1, step, array.shape[2]), lambda i, *_, part=part: (part, i, 0)))
    if passed:
        operands = [where, *operands]
    return pl.pallas_call(
        weigh_early if passed else weigh_late,
        out_shape=jax.ShapeDtypeStruct((count, inputs, 2 * channels), jnp.bfloat16),
        grid_spec=pltpu.PrefetchScalarGridSpec(
            num_scalar_prefetch=1 if passed else 0,
            grid=(inputs // step,),
            in_specs=specs,
            out_specs=pl.BlockSpec((count, step, 2 * channels), lambda i, *_: (0, i, 0)),
        ),
        cost_estimate=pl.CostEstimate(
            flops=count * inputs * channels * 16, bytes_accessed=2 * inputs * samples * 4, transcendentals=0
        ),
        compiler_params=pltpu.CompilerParams(vmem_limit_bytes=VMEM),
    )(*operands)


def transform(weighted_ref, table_ref, turned_ref):
    count, inputs, depth = weighted_ref.shape
    groups, rows, _ = table_ref.shape
    size = rows // 2
    weighted = weighted_ref[...].reshape(count * inputs, depth)
    result = lax.dot_general(
        table_ref[...].reshape(groups * rows, depth), weighted, (((1,), (1,)), ((), ())),
        preferred_element_type=jnp.float32,
    )
    for g in range(groups):
        for part in range(2):
            base = g * rows + part * size
            for s in range(count):
                turned_ref[g, :, part * count + s, :] = result[base:base + size, s * inputs:(s + 1) * inputs]


def transform_to(ends, me_ref, weighted_ref, table_ref, *refs):
    *out_refs, turned_ref = refs
    transform(weighted_ref, table_ref, turned_ref)
    low = me_ref[0] % 2
    chunks = len(ends) - 1
    for i in range(len(out_refs) // (2 * chunks)):
        @pl.when(pl.program_id(0) == i)
        def _(i=i):
            for other in range(2):
                source_ref = turned_ref.at[jnp.bitwise_xor(low, other)]
                for c in range(chunks):
                    out_ref = out_refs[(2 * i + other) * chunks + c]
                    value = source_ref[2 * ends[c]:2 * ends[c + 1]]
                    out_ref[...] = value.reshape(out_ref.shape).astype(jnp.bfloat16)


def spectra_to(me, weighted, table, ends):
    count, inputs, depth = weighted.shape
    groups, rows, _ = table.shape
    chunks = len(ends) - 1
    sizes = [b - a for a, b in zip(ends[:-1], ends[1:])]
    shapes = [(size, 4 * count, inputs) for size in sizes] * groups
    made = pl.pallas_call(
        functools.partial(transform_to, ends),
        out_shape=[jax.ShapeDtypeStruct(shape, jnp.bfloat16) for shape in shapes],
        grid_spec=pltpu.PrefetchScalarGridSpec(
            num_scalar_prefetch=1,
            grid=(groups // 2,),
            in_specs=[
                pl.BlockSpec(weighted.shape, lambda i, m: (0, 0, 0)),
                pl.BlockSpec((2, rows, depth), lambda i, m: ((m[0] // 2 + i) % (groups // 2), 0, 0)),
            ],
            out_specs=[pl.BlockSpec(shape, lambda i, m: (0, 0, 0)) for shape in shapes],
            scratch_shapes=[pltpu.VMEM((2, rows // 2, 2 * count, inputs), jnp.float32)],
        ),
        cost_estimate=pl.CostEstimate(
            flops=2 * groups * rows * depth * count * inputs,
            bytes_accessed=groups * rows * depth * 2 + weighted.size * 4,
            transcendentals=0,
        ),
        compiler_params=pltpu.CompilerParams(vmem_limit_bytes=VMEM),
    )(me, weighted, table)
    return [[made[g * chunks + c] for g in range(groups)] for c in range(chunks)]


def transform_by(ends, weighted_ref, table_ref, *refs):
    *out_refs, turned_ref = refs
    transform(weighted_ref, table_ref, turned_ref)
    for c, out_ref in enumerate(out_refs):
        value = turned_ref[:, 2 * ends[c]:2 * ends[c + 1]]
        out_ref[...] = value.reshape(out_ref.shape).astype(jnp.bfloat16)


def spectra_by(weighted, table, ends):
    count, inputs, depth = weighted.shape
    groups, rows, _ = table.shape
    sizes = [b - a for a, b in zip(ends[:-1], ends[1:])]
    some = 4 if rows < 128 * 4 // 3 else 2
    return pl.pallas_call(
        functools.partial(transform_by, ends),
        out_shape=[jax.ShapeDtypeStruct((groups, size, 4 * count, inputs), jnp.bfloat16) for size in sizes],
        grid=(groups // some,),
        in_specs=[
            pl.BlockSpec(weighted.shape, lambda i: (0, 0, 0)),
            pl.BlockSpec((some, rows, depth), lambda i: (i, 0, 0)),
        ],
        out_specs=[pl.BlockSpec((some, size, 4 * count, inputs), lambda i: (i, 0, 0, 0)) for size in sizes],
        scratch_shapes=[pltpu.VMEM((some, rows // 2, 2 * count, inputs), jnp.float32)],
        cost_estimate=pl.CostEstimate(
            flops=2 * groups * rows * depth * count * inputs,
            bytes_accessed=groups * rows * depth * 2 + weighted.size * 4,
            transcendentals=0,
        ),
        compiler_params=pltpu.CompilerParams(vmem_limit_bytes=VMEM),
    )(weighted, table)


def tick(token, *values):
    def body(token_ref, *refs):
        refs[-1][...] = token_ref[...]

    return pl.pallas_call(
        body,
        out_shape=jax.ShapeDtypeStruct(token.shape, token.dtype),
        in_specs=[pl.BlockSpec(token.shape, lambda: (0, 0))] + [pl.BlockSpec(memory_space=pl.ANY)] * len(values),
        out_specs=pl.BlockSpec(token.shape, lambda: (0, 0)),
        cost_estimate=pl.CostEstimate(flops=RATED, bytes_accessed=0, transcendentals=0),
        compiler_params=pltpu.CompilerParams(vmem_limit_bytes=VMEM),
    )(token, *values)


def correlate(factor, distances, nlate, me_ref, order_ref, *refs):
    blocks = len(distances) + 1
    late = [refs[q * nlate:(q + 1) * nlate] for q in range(blocks)]
    early = refs[blocks * nlate:blocks * (nlate + 1)]
    out_ref = refs[-1]
    groups, pairs, rows, inputs = early[0].shape
    half = rows // 2
    width = out_ref.shape[3] // inputs
    at = [jnp.bitwise_xor(me_ref[0], q) for q in distances]
    offsets = [pl.multiple_of(a % width * inputs, inputs) for a in at]
    odd = [a % 2 for a in (me_ref[0], *at)]
    depth = 2 * groups * rows
    sign = jnp.where(
        lax.broadcasted_iota(jnp.int32, (4 * groups, half, inputs), 1) < half // 2, factor, -factor
    ).astype(jnp.float32)
    of_first = lax.broadcasted_iota(jnp.int32, (inputs, depth), 1) % rows < half
    keep = [jnp.where(of_first, 1.0, 0.0).astype(jnp.bfloat16), jnp.where(of_first, 0.0, 1.0).astype(jnp.bfloat16)]

    def pair(p):
        loaded = []
        for q in range(blocks):
            if q and distances[q - 1] == 0:
                loaded.append(loaded[0])
                continue
            tiles = [ref[j, p] for ref in late[q] for j in range(ref.shape[0])]
            tiles += [early[q][order_ref[odd[q], j], p] for j in range(groups)]
            loaded.append(jnp.concatenate(tiles, axis=0))
        own = loaded[0].astype(jnp.float32)
        turned = pltpu.roll(own.reshape(4 * groups, half, inputs), half // 2, axis=1) * sign
        straight = (own * factor).astype(jnp.bfloat16).T
        turned = turned.reshape(depth, inputs).astype(jnp.bfloat16).T
        left = jnp.concatenate([side * mask for mask in keep for side in (straight, turned)], axis=0)
        product = jnp.dot(left, jnp.concatenate(loaded[1:], axis=1), preferred_element_type=jnp.float32)
        for q in range(blocks - 1):
            columns = pl.ds(offsets[q], inputs)
            for h in range(2):
                for part in range(2):
                    at_row = (2 * h + part) * inputs
                    out_ref[part, 2 * p + h, :, columns] = product[at_row:at_row + inputs, q * inputs:(q + 1) * inputs]

    for p in range(pairs):
        pair(p)


def correlated(me, order, held, distances, at, shape, factor, visible, token=None):
    *late, early = held
    groups, pairs, rows, inputs = early[0].shape
    step = math.gcd(4, math.gcd(pairs, at))
    wide = inputs * len(distances)
    operands, specs = [me, order], []
    for q in (0, *distances):
        for array in late:
            operands.append(array[q])
            specs.append(pl.BlockSpec((array[q].shape[0], step, rows, inputs), lambda i, *_: (0, at // step + i, 0, 0)))
    for q in (0, *distances):
        operands.append(early[q])
        specs.append(pl.BlockSpec((groups, step, rows, inputs), lambda i, *_: (0, i, 0, 0)))
    aliases = {}
    if visible is not None:
        aliases = {len(operands): 0}
        operands.append(visible)
        specs.append(pl.BlockSpec(memory_space=pl.ANY))
    if token is not None:
        operands.append(token)
        specs.append(pl.BlockSpec(memory_space=pl.ANY))
    whole = shape[3] == wide
    high = distances[0] // len(distances)
    depth = groups * rows
    return pl.pallas_call(
        functools.partial(correlate, factor, distances, len(late)),
        out_shape=jax.ShapeDtypeStruct(shape, jnp.float32),
        grid_spec=pltpu.PrefetchScalarGridSpec(
            num_scalar_prefetch=2,
            grid=(pairs // step,),
            in_specs=specs,
            out_specs=pl.BlockSpec(
                (2, 2 * step, inputs, wide),
                lambda i, m, _: (0, at // step + i, 0, 0 if whole else jnp.bitwise_xor(m[0] // len(distances), high)),
            ),
        ),
        input_output_aliases=aliases,
        cost_estimate=pl.CostEstimate(
            flops=2 * 2 * pairs * 2 * inputs * wide * depth, bytes_accessed=2 * pairs * 2 * inputs * wide * 4, transcendentals=0
        ),
        compiler_params=pltpu.CompilerParams(vmem_limit_bytes=VMEM),
    )(*operands)


def local(tables, voltages, taps):
    ntaps, channels = taps.shape
    inputs = voltages.shape[1]
    frames = voltages.shape[2] // channels
    groups = lax.axis_size("freq")
    blocks = lax.axis_size("blk")
    group = channels // groups
    ends = cuts(group // 2, EARLY)
    half = frames // 2
    factor = 1.0 / math.sqrt(frames * groups)
    freq = lax.axis_index("freq").astype(jnp.int32)
    blk = lax.axis_index("blk").astype(jnp.int32)
    odd = blk % 2
    me = freq.reshape(1)
    high = groups // 2
    shape = (2, group, inputs, inputs * blocks)
    both = lax.optimization_barrier
    table, first_table, other_table = tables

    begin = jnp.where(odd == 0, frames - ntaps + 1, 0) * channels
    given = lax.dynamic_slice_in_dim(voltages, begin, (ntaps - 1) * channels, 2).astype(jnp.bfloat16)
    more = voltages[:, :, (ntaps - 1) * channels:half * channels].astype(jnp.bfloat16)
    where = jnp.stack([odd, (freq < groups - 1).astype(jnp.int32)])

    passed = [handed(given), handed(more, even=False)]
    (made,) = spectra_to(me, weighted_spectra(taps, voltages, half), table, (0, group // 2))
    near = [made[0]] + [shifted(made[2 * s], s, 0) for s in range(1, high)]
    near, passed, made = both((near, passed, made))

    held = [{0: jnp.stack(near)}]
    far = [shifted(made[2 * s + 1], s, 1) for s in range(high)]
    held[0][2] = swapped(held[0][0], "blk", 2)
    early_weighted = weighted_spectra(taps, voltages, half, where, passed)
    early = spectra_by(early_weighted, first_table, ends[:2])
    held.append({0: jnp.stack(far)})
    held, early, early_weighted = both((held, early, early_weighted))

    index = jnp.arange(groups, dtype=jnp.int32)
    order = jnp.stack([index, (index - 1) % groups])

    nearly = len(ends) - 1
    visible = None
    token = jnp.zeros((8, 128), jnp.float32)
    for step in range(nearly + 2):
        new = {}
        if step < nearly:
            new[step + 2, 0] = lax.all_to_all(early[step], "freq", split_axis=0, concat_axis=0, tiled=True)
        if step <= nearly:
            new[step + 1, 2] = swapped(held[step + 1][0], "blk", 2)
            new[step + 1, 1] = swapped(held[step + 1][0], "blk", 1)
        if step == 0:
            new[0, 1] = swapped(held[0][0], "blk", 1)
            early = early + spectra_by(early_weighted, other_table, [end - ends[1] for end in ends[1:]])
        new[step, 3] = swapped(held[step][2], "blk", 1)
        if step >= 2:
            parts = [held[0], held[1], {**held[step], 3: new[step, 3]}]
            visible = correlated(blk.reshape(1), order, parts, (0, 1, 2, 3), ends[step - 2], shape, factor, visible, token)
        if step < nearly:
            token = tick(token, new[step + 1, 2], *([] if visible is None else [visible]))
        if step == nearly + 1:
            break
        new, held, early, visible, token = both((new, held, early, visible, token))
        held.append({})
        for (c, q), value in new.items():
            held[c][q] = value
    return visible


def solution(mesh):
    groups = mesh.shape["freq"]

    def run(voltages, taps):
        channels = taps.shape[1]
        ends = cuts(channels // groups // 2, EARLY)
        tables = dft_rows(channels, groups, ((0, ends[-1]), (0, ends[1]), (ends[1], ends[-1])))
        return jax.shard_map(
            functools.partial(local, tables),
            mesh=mesh,
            in_specs=(P(None, "blk", "freq"), P()),
            out_specs=P(None, "freq", "blk", None),
            check_vma=False,
        )(voltages, taps)

    return run
```

time: 577 us -> 196 us (0.34)
  waiting for transfers between devices: 264 us -> 55.6 us
  local copies, waits for them, and re-layouts: 155 us -> 4.16 us
  Pallas kernels: 0 us -> 79.2 us
  matrix products: 77.9 us -> 0 us
  other arithmetic: 64.3 us -> 8.03 us
  starting transfers between devices: 13.4 us -> 47.1 us
    ppermute x4 -> x24, waiting for transfers between devices: 172 us -> 50.5 us  [the longest x15 29.1 us: swapped(): return lax.ppermute(value, axis, pairs)]
    all_to_all x1 -> x3, waiting for transfers between devices: 92.4 us -> 5.1 us  [local(): lax.all_to_all(early[step], 'freq', split_axis=0, concat_axis=0, tiled=True)]
    while x4 -> x0, local copies, waits for them, and re-layouts: 84 us -> none  [the longest x1 65.9 us: local(): carried = lax.fori_loop(1, count, advance, (turned, visible))]
    pallas_call x0 -> x11, Pallas kernels: none -> 79.2 us  [the longest x3 39.4 us: correlated(): pl.pallas_call(functools.partial(correlate, factor, distances, len(late))...]
    dot_general x5 -> x0, matrix products: 77.9 us -> none  [the longest x4 52.5 us: correlate(): jnp.einsum('sirc,sjorc->ocij', turned, partner, preferred_element_type=jn...]
    ppermute x4 -> x24, starting transfers between devices: 6.49 us -> 31.7 us  [the longest x7 18.4 us: shifted(): return lax.ppermute(value, 'freq', pairs)]
    neg x5 -> x0, other arithmetic: 24.9 us -> none  [the longest x1 16.5 us: dft_table(): upper = jnp.concatenate([cosine, -sine], axis=1)]
    broadcast_in_dim x1, local copies, waits for them, and re-layouts: 21.2 us -> 0.59 us  [local(): token = jnp.zeros((8, 128), jnp.float32)]
  transfers between devices with their start and end apart: 5 -> 27, of which waited for: 5 -> 8; matrix products, arithmetic and copies ran while one was open for 7% -> 2% of each run, Pallas kernels for 0% -> 35%
where the time goes in v2:
time: 196 us; the launch traced here: 195 us
  Pallas kernels  79.2 us (40%)
  waiting for transfers between devices  55.6 us (28%)
  starting transfers between devices  47.1 us (24%)
  other arithmetic  8.03 us (4%)
  local copies, waits for them, and re-layouts  4.16 us (2%)
    pallas_call x3, Pallas kernels, correlated(): pl.pallas_call(functools.partial(correlate, factor, distances, len(late))...  39.4 us
    ppermute x15, waiting for transfers between devices, swapped(): return lax.ppermute(value, axis, pairs)  29.1 us
    ppermute x7, waiting for transfers between devices, shifted(): return lax.ppermute(value, 'freq', pairs)  21.4 us
    ppermute x7, starting transfers between devices, shifted(): return lax.ppermute(value, 'freq', pairs)  18.4 us
    all_to_all x3, starting transfers between devices, local(): lax.all_to_all(early[step], 'freq', split_axis=0, concat_axis=0, tiled=True)  15.4 us
    pallas_call x2, Pallas kernels, spectra_by(): pl.pallas_call(functools.partial(transform_by, ends), out_shape=[jax.Shap...  13.4 us
    pallas_call x2, Pallas kernels, weighted_spectra(): pl.pallas_call(weigh_early if passed else weigh_late, out_shape=jax.Shape...  11.8 us
    pallas_call x1, Pallas kernels, spectra_to(): pl.pallas_call(functools.partial(transform_to, ends), out_shape=[jax.Shap...  10.8 us
  transfers between devices with their start and end apart: 27, of which 8 were waited for; matrix products, arithmetic and copies ran while one was open for 2% of the time, Pallas kernels for 35%

profile of v2, /device:TPU:0, one launch (start us, length us, event | category | flops | bytes accessed | tf_op | source)
XLA Modules:
  0.0 194.6 jit_solution(2682940397056808501)
XLA Ops:
  0.0 3.3 %dynamic-slice_convert_fusion = bf16[2,128,3072]{2,1,0:T(8,128)(2,1)} fusion(s32[2,128,8192]{2,1,0:T(8,128)} %imag_ref.3, s32[]{:T(128)S(6)} %select_n.30), kind=kLoop, calls=%fused_computation | loop fusion | flops 786432 | bytes 4718596 | tf_op jit(solution)/shard_map/convert_element_type | solution.py:356
  3.3 4.9 %collective-permute-start.3 = (bf16[2,128,3072]{2,1,0:T(8,128)(2,1)}, bf16[2,128,3072]{2,1,0:T(8,128)(2,1)S(1)}, u32[]{:S(2)}, u32[]{:S(2)}) collective-permute-start(bf16[2,128,3072]{2,1,0:T(8,128)(2,1)} %dynamic-slice_convert_fusion), channel_id=1, source_target_pairs={{0,4},{1,29},{2,6},{3,31},{4,8},{5,1},{6,10},{7,3},{8,12},{9,5},{1... | collective-permute-start | bytes 4718600 | tf_op jit(solution)/shard_map/ppermute | solution.py:32
  8.2 1.3 slice_convert_fusion
  9.5 0.7 collective-permute-start.4
  10.3 5.2 %shard_map.55.weighted_ref = bf16[4,128,2048]{2,1,0:T(8,128)(2,1)} custom-call(s32[4,1024]{1,0:T(4,128)} %taps_ref.3, s32[2,128,8192]{2,1,0:T(8,128)} %imag_ref.3, s32[2,128,8192]{2,1,0:T(8,128)} %imag_ref.3), custom_call_target="tpu_custom_call" | custom-call | flops 8388608 | bytes 8388608 | tf_op jit(solution)/shard_map/pallas_call | solution.py:125
  15.4 10.8 %shard_map.56 = (bf16[64,16,128]{2,1,0:T(8,128)(2,1)}, bf16[64,16,128]{2,1,0:T(8,128)(2,1)}, bf16[64,16,128]{2,1,0:T(8,128)(2,1)}, bf16[64,16,128]{2,1,0:T(8,128...) custom-call(s32[1]{0:T(128)} %bitcast.1.me_ref, ...), custom_call_target="tpu_custom_call" | custom-call | flops 4294967296 | bytes 12582912 | tf_op jit(solution)/shard_map/pallas_call | solution.py:179
  26.2 1.5 collective-permute-start
  27.7 2.6 %collective-permute-start.1 = (bf16[64,16,128]{2,1,0:T(8,128)(2,1)}, bf16[64,16,128]{2,1,0:T(8,128)(2,1)S(1)}, u32[]{:S(2)}, u32[]{:S(2)}) collective-permute-start(bf16[64,16,128]{2,1,0:T(8,128)(2,1)} %get-tuple-element.84), channel_id=1, source_target_pairs={{0,16},{4,20},{8,24},{12,28},{16,0},{20,4},{24,8},{28,12},{1,17},{... | collective-permute-start | bytes 786440 | tf_op jit(solution)/shard_map/ppermute | solution.py:42
  30.3 1.3 collective-permute-start.2
  31.6 5.8 %collective-permute-done = bf16[64,16,128]{2,1,0:T(8,128)(2,1)S(1)} collective-permute-done((bf16[64,16,128]{2,1,0:T(8,128)(2,1)}, bf16[64,16,128]{2,1,0:T(8,128)(2,1)S(1)}, u32[]{:S(2)}, u32[]{:S(2)}) %collective-permute-start) | collective-permute-done | bytes 262176 | tf_op jit(solution)/shard_map/ppermute | solution.py:42
  37.5 11.6 %collective-permute-done.1 = bf16[64,16,128]{2,1,0:T(8,128)(2,1)S(1)} collective-permute-done((bf16[64,16,128]{2,1,0:T(8,128)(2,1)}, bf16[64,16,128]{2,1,0:T(8,128)(2,1)S(1)}, u32[]{:S(2)}, u32[]{:S(2)}) %collective-permute-start.1) | collective-permute-done | bytes 262176 | tf_op jit(solution)/shard_map/ppermute | solution.py:42
  49.1 1.2 copy-done.4
  50.3 1.1 pad_maximum_fusion.refs_0_.refs_2_
  51.4 1.6 collective-permute-start.5
  52.9 1.9 collective-permute-start.6
  54.8 8.3 %collective-permute-start.7 = (bf16[64,16,128]{2,1,0:T(8,128)(2,1)}, bf16[64,16,128]{2,1,0:T(8,128)(2,1)S(1)}, u32[]{:S(2)}, u32[]{:S(2)}) collective-permute-start(bf16[64,16,128]{2,1,0:T(8,128)(2,1)} %get-tuple-element.95), channel_id=1, source_target_pairs={{0,12},{4,8},{8,20},{12,16},{16,28},{20,24},{24,4},{28,0},{1,13},{... | collective-permute-start | bytes 786440 | tf_op jit(solution)/shard_map/ppermute | solution.py:42
  63.2 2.7 %collective-permute-start.8 = (bf16[64,16,128]{2,1,0:T(8,128)(2,1)}, bf16[64,16,128]{2,1,0:T(8,128)(2,1)S(1)}, u32[]{:S(2)}, u32[]{:S(2)}) collective-permute-start(bf16[64,16,128]{2,1,0:T(8,128)(2,1)} %get-tuple-element.96), channel_id=1, source_target_pairs={{0,20},{4,16},{8,28},{12,24},{16,4},{20,0},{24,12},{28,8},{1,21},{... | collective-permute-start | bytes 786440 | tf_op jit(solution)/shard_map/ppermute | solution.py:42
  65.9 0.7 pad_add_fusion.1.where_ref
  66.6 6.7 %shard_map.57.weighted_ref = bf16[4,128,2048]{2,1,0:T(8,128)(2,1)} custom-call(s32[2]{0:T(128)} %pad_add_fusion.1.where_ref, s32[4,1024]{1,0:T(4,128)} %taps_ref.3, s32[2,128,8192]{2,1,0:T(8,128)} %imag_ref.3, s32[2,128,8192]{2,1,0:T(8,128)} %imag_ref.3, bf16[2,128,3072]{2,1,0:T(8,128)(2,1)} %copy-done.4, bf16[2,128,3072]{2,1,0:T(8,128)(2,1)} %copy-done.4, ...), custom_call_target="tpu_custom_call" | custom-call | flops 8388608 | bytes 8388608 | tf_op jit(solution)/shard_map/pallas_call | solution.py:125
  73.2 6.2 %shard_map.58 = bf16[8,28,16,128]{3,2,1,0:T(8,128)(2,1)} custom-call(bf16[4,128,2048]{2,1,0:T(8,128)(2,1)} %shard_map.57.weighted_ref, bf16[8,112,2048]{2,1,0:T(8,128)(2,1)} %constant.56.clone.table_ref), custom_call_target="tpu_custom_call" | custom-call | flops 1879048192 | bytes 7864320 | tf_op jit(solution)/shard_map/pallas_call | solution.py:215
  79.4 4.0 %collective-permute-done.8 = bf16[64,16,128]{2,1,0:T(8,128)(2,1)S(1)} collective-permute-done((bf16[64,16,128]{2,1,0:T(8,128)(2,1)}, bf16[64,16,128]{2,1,0:T(8,128)(2,1)S(1)}, u32[]{:S(2)}, u32[]{:S(2)}) %collective-permute-start.8) | collective-permute-done | bytes 262176 | tf_op jit(solution)/shard_map/ppermute | solution.py:42
  83.5 0.7 copy-done.13
  84.2 1.1 pad_maximum_fusion.1.refs_1_.refs_3_
  85.3 0.6 collective-permute-start.13
  85.9 0.5 collective-permute-start.10
  86.4 7.4 %all-to-all-start = ((bf16[8,28,16,128]{3,2,1,0:T(8,128)(2,1)}), bf16[8,28,16,128]{3,2,1,0:T(8,128)(2,1)}, u32[]{:S(2)}, u32[]{:S(2)}) async-start(bf16[8,28,16,128]{3,2,1,0:T(8,128)(2,1)} %shard_map.58), calls=%async_computation | async-start | bytes 1835008 | tf_op jit(solution)/shard_map/all_to_all | solution.py:382
  93.7 7.2 %shard_map.59 = (bf16[8,20,16,128]{3,2,1,0:T(8,128)(2,1)}, bf16[8,16,16,128]{3,2,1,0:T(8,128)(2,1)}) custom-call(bf16[4,128,2048]{2,1,0:T(8,128)(2,1)} %shard_map.57.weighted_ref, bf16[8,144,2048]{2,1,0:T(8,128)(2,1)} %constant.57.clone.table_ref), custom_call_target="tpu_custom_call" | custom-call | flops 2415919104 | bytes 8912896 | tf_op jit(solution)/shard_map/pallas_call | solution.py:215
  100.9 9.5 %collective-permute-done.13.refs_0_.refs_7_ = bf16[4,64,16,128]{3,2,1,0:T(8,128)(2,1)} collective-permute-done((bf16[4,64,16,128]{3,2,1,0:T(8,128)(2,1)S(1)}, bf16[4,64,16,128]{3,2,1,0:T(8,128)(2,1)}, u32[]{:S(2)}, u32[]{:S(2)}) %collective-permute-start.13) | collective-permute-done | bytes 1048608 | tf_op jit(solution)/shard_map/ppermute | solution.py:20
  110.5 0.6 broadcast_in_dim.3.token_ref
  111.0 1.3 shard_map.60.token_ref
  112.3 5.1 %all-to-all-done.refs_10_.refs_11_ = bf16[8,28,16,128]{3,2,1,0:T(8,128)(2,1)} async-done(((bf16[8,28,16,128]{3,2,1,0:T(8,128)(2,1)}), bf16[8,28,16,128]{3,2,1,0:T(8,128)(2,1)}, u32[]{:S(2)}, u32[]{:S(2)}) %all-to-all-start) | async-done | bytes 917536 | tf_op jit(solution)/shard_map/all_to_all | solution.py:382
  117.4 1.5 collective-permute-start.16
  119.0 0.5 collective-permute-start.14
  119.5 3.7 %all-to-all-start.1 = ((bf16[8,20,16,128]{3,2,1,0:T(8,128)(2,1)}), bf16[8,20,16,128]{3,2,1,0:T(8,128)(2,1)S(1)}, u32[]{:S(2)}, u32[]{:S(2)}) async-start(bf16[8,20,16,128]{3,2,1,0:T(8,128)(2,1)} %get-tuple-element.109), calls=%async_computation.1 | async-start | bytes 1310720 | tf_op jit(solution)/shard_map/all_to_all | solution.py:382
  123.1 16.3 %collective-permute-done.16.refs_0_.refs_13_ = bf16[8,28,16,128]{3,2,1,0:T(8,128)(2,1)} collective-permute-done((bf16[8,28,16,128]{3,2,1,0:T(8,128)(2,1)}, bf16[8,28,16,128]{3,2,1,0:T(8,128)(2,1)}, u32[]{:S(2)}, u32[]{:S(2)}) %collective-permute-start.16) | collective-permute-done | bytes 917536 | tf_op jit(solution)/shard_map/ppermute | solution.py:20
  139.4 1.3 shard_map.61.refs_15_.token_ref
  140.8 1.6 collective-permute-start.19
  142.4 0.6 pad_add_fusion.order_ref
  143.2 4.3 %all-to-all-start.2 = ((bf16[8,16,16,128]{3,2,1,0:T(8,128)(2,1)}), bf16[8,16,16,128]{3,2,1,0:T(8,128)(2,1)S(1)}, u32[]{:S(2)}, u32[]{:S(2)}) async-start(bf16[8,16,16,128]{3,2,1,0:T(8,128)(2,1)} %get-tuple-element.120), calls=%async_computation.2 | async-start | bytes 1048576 | tf_op jit(solution)/shard_map/all_to_all | solution.py:382
  147.5 16.1 %shard_map.62.refs_1_.refs_15_ = f32[2,128,128,512]{3,2,1,0:T(8,128)} custom-call(s32[1]{0:T(128)} %bitcast.me_ref, s32[2,8]{1,0:T(2,128)} %pad_add_fusion.order_ref, bf16[4,64,16,128]{3,2,1,0:T(8,128)(2,1)} %copy-done, bf16[4,64,16,128]{3,2,1,0:T(8,128)(2,1)} %copy-done.1, bf16[4,64,16,128]{3,2,1,0:T(8,128)(2,1)} %copy-done, ...), custom_call_target="tpu_custom_call" | custom-call | flops 1879048192 | bytes 29360128 | tf_op jit(solution)/shard_map/pallas_call | solution.py:316
  163.7 1.3 shard_map.63.refs_16_
  165.6 0.5 collective-permute-start.22
  166.0 1.5 collective-permute-done.20.refs_14_
  167.5 0.8 copy-done.9
  168.3 12.5 %shard_map.64.refs_15_ = f32[2,128,128,512]{3,2,1,0:T(8,128)} custom-call(s32[1]{0:T(128)} %bitcast.me_ref, s32[2,8]{1,0:T(2,128)} %pad_add_fusion.order_ref, bf16[4,64,16,128]{3,2,1,0:T(8,128)(2,1)} %copy-done, bf16[4,64,16,128]{3,2,1,0:T(8,128)(2,1)} %copy-done.1, bf16[4,64,16,128]{3,2,1,0:T(8,128)(2,1)} %copy-done, ...), custom_call_target="tpu_custom_call", output_to_operand_aliasing={{}: (17, {})} | custom-call | flops 1342177280 | bytes 20971520 | tf_op jit(solution)/shard_map/pallas_call | solution.py:316
  181.1 1.8 collective-permute-done.23.refs_14_
  182.9 0.8 copy-done.12
  183.7 10.7 %shard_map.65 = f32[2,128,128,512]{3,2,1,0:T(8,128)} custom-call(s32[1]{0:T(128)} %bitcast.me_ref, s32[2,8]{1,0:T(2,128)} %pad_add_fusion.order_ref, bf16[4,64,16,128]{3,2,1,0:T(8,128)(2,1)} %copy-done, bf16[4,64,16,128]{3,2,1,0:T(8,128)(2,1)} %copy-done.1, bf16[4,64,16,128]{3,2,1,0:T(8,128)(2,1)} %copy-done, ...), custom_call_target="tpu_custom_call", output_to_operand_aliasing={{}: (17, {})} | custom-call | flops 1073741824 | bytes 16777216 | tf_op jit(solution)/shard_map/pallas_call | solution.py:316
  (54 shorter events, 1.1 us)
Async XLA Ops:
  3.3 45.8 %collective-permute-start.3 = (bf16[2,128,3072]{2,1,0:T(8,128)(2,1)}, bf16[2,128,3072]{2,1,0:T(8,128)(2,1)S(1)}, u32[]{:S(2)}, u32[]{:S(2)}) collective-permute-start(bf16[2,128,3072]{2,1,0:T(8,128)(2,1)} %dynamic-slice_convert_fusion), channel_id=1, source_target_pairs={{0,4},{1,29},{2,6},{3,31},{4,8},{5,1},{6,10},{7,3},{8,12},{9,5},{1... | collective-permute-start | bytes 4718600 | tf_op jit(solution)/shard_map/ppermute | solution.py:32
  9.5 39.5 %collective-permute-start.4 = (bf16[2,128,1024]{2,1,0:T(8,128)(2,1)S(1)}, bf16[2,128,1024]{2,1,0:T(8,128)(2,1)S(1)}, u32[]{:S(2)}, u32[]{:S(2)}) collective-permute-start(bf16[2,128,1024]{2,1,0:T(8,128)(2,1)S(1)} %slice_convert_fusion), channel_id=1, source_target_pairs={{1,29},{3,31},{5,1},{7,3},{9,5},{11,7},{13,9},{15,11},{17,13},{19,... | collective-permute-start | bytes 1572872 | tf_op jit(solution)/shard_map/ppermute | solution.py:32
  26.2 11.3 %collective-permute-start = (bf16[64,16,128]{2,1,0:T(8,128)(2,1)}, bf16[64,16,128]{2,1,0:T(8,128)(2,1)S(1)}, u32[]{:S(2)}, u32[]{:S(2)}) collective-permute-start(bf16[64,16,128]{2,1,0:T(8,128)(2,1)} %get-tuple-element.83), channel_id=1, source_target_pairs={{0,8},{4,12},{8,16},{12,20},{16,24},{20,28},{24,0},{28,4},{1,9},{5... | collective-permute-start | bytes 786440 | tf_op jit(solution)/shard_map/ppermute | solution.py:42
  27.7 21.3 %collective-permute-start.1 = (bf16[64,16,128]{2,1,0:T(8,128)(2,1)}, bf16[64,16,128]{2,1,0:T(8,128)(2,1)S(1)}, u32[]{:S(2)}, u32[]{:S(2)}) collective-permute-start(bf16[64,16,128]{2,1,0:T(8,128)(2,1)} %get-tuple-element.84), channel_id=1, source_target_pairs={{0,16},{4,20},{8,24},{12,28},{16,0},{20,4},{24,8},{28,12},{1,17},{... | collective-permute-start | bytes 786440 | tf_op jit(solution)/shard_map/ppermute | solution.py:42
  30.3 18.7 %collective-permute-start.2 = (bf16[64,16,128]{2,1,0:T(8,128)(2,1)}, bf16[64,16,128]{2,1,0:T(8,128)(2,1)S(1)}, u32[]{:S(2)}, u32[]{:S(2)}) collective-permute-start(bf16[64,16,128]{2,1,0:T(8,128)(2,1)} %get-tuple-element.85), channel_id=1, source_target_pairs={{0,24},{4,28},{8,0},{12,4},{16,8},{20,12},{24,16},{28,20},{1,25},{... | collective-permute-start | bytes 786440 | tf_op jit(solution)/shard_map/ppermute | solution.py:42
  49.0 17.5 %copy-start.7 = (bf16[2,128,1024]{2,1,0:T(8,128)(2,1)}, bf16[2,128,1024]{2,1,0:T(8,128)(2,1)S(1)}, u32[]{:S(2)}) copy-start(bf16[2,128,1024]{2,1,0:T(8,128)(2,1)S(1)} %collective-permute-done.4.refs_2_.refs_3_) | copy-start | bytes 1572868
  49.1 1.2 copy-start.4
  51.3 34.5 %copy-start = (bf16[4,64,16,128]{3,2,1,0:T(8,128)(2,1)}, bf16[4,64,16,128]{3,2,1,0:T(8,128)(2,1)S(1)}, u32[]{:S(2)}) copy-start(bf16[4,64,16,128]{3,2,1,0:T(8,128)(2,1)S(1)} %pad_maximum_fusion.refs_0_.refs_2_) | copy-start | bytes 3145732
  51.4 33.9 %collective-permute-start.5 = (bf16[4,64,16,128]{3,2,1,0:T(8,128)(2,1)S(1)}, bf16[4,64,16,128]{3,2,1,0:T(8,128)(2,1)S(1)}, u32[]{:S(2)}, u32[]{:S(2)}) collective-permute-start(bf16[4,64,16,128]{3,2,1,0:T(8,128)(2,1)S(1)} %pad_maximum_fusion.refs_0_.refs_2_), channel_id=1, source_target_pairs={{0,2},{1,3},{2,0},{3,1},{4,6},{5,7},{6,4},{7,5},{8,10},{9,11},{10,... | collective-permute-start | bytes 3145736 | tf_op jit(solution)/shard_map/ppermute | solution.py:20
  52.9 26.5 %collective-permute-start.6 = (bf16[64,16,128]{2,1,0:T(8,128)(2,1)}, bf16[64,16,128]{2,1,0:T(8,128)(2,1)S(1)}, u32[]{:S(2)}, u32[]{:S(2)}) collective-permute-start(bf16[64,16,128]{2,1,0:T(8,128)(2,1)} %get-tuple-element.94), channel_id=1, source_target_pairs={{0,4},{4,0},{8,12},{12,8},{16,20},{20,16},{24,28},{28,24},{1,5},{5... | collective-permute-start | bytes 786440 | tf_op jit(solution)/shard_map/ppermute | solution.py:42
  54.8 24.6 %collective-permute-start.7 = (bf16[64,16,128]{2,1,0:T(8,128)(2,1)}, bf16[64,16,128]{2,1,0:T(8,128)(2,1)S(1)}, u32[]{:S(2)}, u32[]{:S(2)}) collective-permute-start(bf16[64,16,128]{2,1,0:T(8,128)(2,1)} %get-tuple-element.95), channel_id=1, source_target_pairs={{0,12},{4,8},{8,20},{12,16},{16,28},{20,24},{24,4},{28,0},{1,13},{... | collective-permute-start | bytes 786440 | tf_op jit(solution)/shard_map/ppermute | solution.py:42
  63.2 20.3 %collective-permute-start.8 = (bf16[64,16,128]{2,1,0:T(8,128)(2,1)}, bf16[64,16,128]{2,1,0:T(8,128)(2,1)S(1)}, u32[]{:S(2)}, u32[]{:S(2)}) collective-permute-start(bf16[64,16,128]{2,1,0:T(8,128)(2,1)} %get-tuple-element.96), channel_id=1, source_target_pairs={{0,20},{4,16},{8,28},{12,24},{16,4},{20,0},{24,12},{28,8},{1,21},{... | collective-permute-start | bytes 786440 | tf_op jit(solution)/shard_map/ppermute | solution.py:42
  65.9 17.6 %collective-permute-start.9 = (bf16[64,16,128]{2,1,0:T(8,128)(2,1)}, bf16[64,16,128]{2,1,0:T(8,128)(2,1)S(1)}, u32[]{:S(2)}, u32[]{:S(2)}) collective-permute-start(bf16[64,16,128]{2,1,0:T(8,128)(2,1)} %get-tuple-element.97), channel_id=1, source_target_pairs={{0,28},{4,24},{8,4},{12,0},{16,12},{20,8},{24,20},{28,16},{1,29},{... | collective-permute-start | bytes 786440 | tf_op jit(solution)/shard_map/ppermute | solution.py:42
  83.5 0.7 copy-start.13
  85.3 15.7 %copy-start.1 = (bf16[4,64,16,128]{3,2,1,0:T(8,128)(2,1)}, bf16[4,64,16,128]{3,2,1,0:T(8,128)(2,1)S(1)}, u32[]{:S(2)}) copy-start(bf16[4,64,16,128]{3,2,1,0:T(8,128)(2,1)S(1)} %pad_maximum_fusion.1.refs_1_.refs_3_) | copy-start | bytes 3145732
  85.3 15.6 %copy-start.2 = (bf16[4,64,16,128]{3,2,1,0:T(8,128)(2,1)}, bf16[4,64,16,128]{3,2,1,0:T(8,128)(2,1)S(1)}, u32[]{:S(2)}) copy-start(bf16[4,64,16,128]{3,2,1,0:T(8,128)(2,1)S(1)} %collective-permute-done.5.refs_6_) | copy-start | bytes 3145732
  85.3 25.2 %collective-permute-start.13 = (bf16[4,64,16,128]{3,2,1,0:T(8,128)(2,1)S(1)}, bf16[4,64,16,128]{3,2,1,0:T(8,128)(2,1)}, u32[]{:S(2)}, u32[]{:S(2)}) collective-permute-start(bf16[4,64,16,128]{3,2,1,0:T(8,128)(2,1)S(1)} %pad_maximum_fusion.1.refs_1_.refs_3_), channel_id=1, source_target_pairs={{0,2},{1,3},{2,0},{3,1},{4,6},{5,7},{6,4},{7,5},{8,10},{9,11},{10,... | collective-permute-start | bytes 3145736 | tf_op jit(solution)/shard_map/ppermute | solution.py:20
  85.9 26.5 %collective-permute-start.12 = (bf16[4,64,16,128]{3,2,1,0:T(8,128)(2,1)S(1)}, bf16[4,64,16,128]{3,2,1,0:T(8,128)(2,1)}, u32[]{:S(2)}, u32[]{:S(2)}) collective-permute-start(bf16[4,64,16,128]{3,2,1,0:T(8,128)(2,1)S(1)} %pad_maximum_fusion.1.refs_1_.refs_3_), channel_id=1, source_target_pairs={{0,1},{1,0},{2,3},{3,2},{4,5},{5,4},{6,7},{7,6},{8,9},{9,8},{10,11... | collective-permute-start | bytes 3145736 | tf_op jit(solution)/shard_map/ppermute | solution.py:20
  85.9 26.5 %collective-permute-start.10 = (bf16[4,64,16,128]{3,2,1,0:T(8,128)(2,1)S(1)}, bf16[4,64,16,128]{3,2,1,0:T(8,128)(2,1)}, u32[]{:S(2)}, u32[]{:S(2)}) collective-permute-start(bf16[4,64,16,128]{3,2,1,0:T(8,128)(2,1)S(1)} %pad_maximum_fusion.refs_0_.refs_2_), channel_id=1, source_target_pairs={{0,1},{1,0},{2,3},{3,2},{4,5},{5,4},{6,7},{7,6},{8,9},{9,8},{10,11... | collective-permute-start | bytes 3145736 | tf_op jit(solution)/shard_map/ppermute | solution.py:20
  86.4 25.9 %collective-permute-start.11 = (bf16[4,64,16,128]{3,2,1,0:T(8,128)(2,1)S(1)}, bf16[4,64,16,128]{3,2,1,0:T(8,128)(2,1)}, u32[]{:S(2)}, u32[]{:S(2)}) collective-permute-start(bf16[4,64,16,128]{3,2,1,0:T(8,128)(2,1)S(1)} %collective-permute-done.5.refs_6_), channel_id=1, source_target_pairs={{0,1},{1,0},{2,3},{3,2},{4,5},{5,4},{6,7},{7,6},{8,9},{9,8},{10,11... | collective-permute-start | bytes 3145736 | tf_op jit(solution)/shard_map/ppermute | solution.py:20
  86.4 31.1 %all-to-all-start = ((bf16[8,28,16,128]{3,2,1,0:T(8,128)(2,1)}), bf16[8,28,16,128]{3,2,1,0:T(8,128)(2,1)}, u32[]{:S(2)}, u32[]{:S(2)}) async-start(bf16[8,28,16,128]{3,2,1,0:T(8,128)(2,1)} %shard_map.58), calls=%async_computation | async-start | bytes 1835008 | tf_op jit(solution)/shard_map/all_to_all | solution.py:382
  117.4 22.0 %collective-permute-start.16 = (bf16[8,28,16,128]{3,2,1,0:T(8,128)(2,1)}, bf16[8,28,16,128]{3,2,1,0:T(8,128)(2,1)}, u32[]{:S(2)}, u32[]{:S(2)}) collective-permute-start(bf16[8,28,16,128]{3,2,1,0:T(8,128)(2,1)} %all-to-all-done.refs_10_.refs_11_), channel_id=1, source_target_pairs={{0,2},{1,3},{2,0},{3,1},{4,6},{5,7},{6,4},{7,5},{8,10},{9,11},{10,... | collective-permute-start | bytes 2752520 | tf_op jit(solution)/shard_map/ppermute | solution.py:20
  119.0 21.7 %collective-permute-start.15 = (bf16[8,28,16,128]{3,2,1,0:T(8,128)(2,1)}, bf16[8,28,16,128]{3,2,1,0:T(8,128)(2,1)S(1)}, u32[]{:S(2)}, u32[]{:S(2)}) collective-permute-start(bf16[8,28,16,128]{3,2,1,0:T(8,128)(2,1)} %all-to-all-done.refs_10_.refs_11_), channel_id=1, source_target_pairs={{0,1},{1,0},{2,3},{3,2},{4,5},{5,4},{6,7},{7,6},{8,9},{9,8},{10,11... | collective-permute-start | bytes 2752520 | tf_op jit(solution)/shard_map/ppermute | solution.py:20
  119.0 21.7 %collective-permute-start.14 = (bf16[4,64,16,128]{3,2,1,0:T(8,128)(2,1)}, bf16[4,64,16,128]{3,2,1,0:T(8,128)(2,1)S(1)}, u32[]{:S(2)}, u32[]{:S(2)}) collective-permute-start(bf16[4,64,16,128]{3,2,1,0:T(8,128)(2,1)} %collective-permute-done.13.refs_0_.refs_7_), channel_id=1, source_target_pairs={{0,1},{1,0},{2,3},{3,2},{4,5},{5,4},{6,7},{7,6},{8,9},{9,8},{10,11... | collective-permute-start | bytes 3145736 | tf_op jit(solution)/shard_map/ppermute | solution.py:20
  119.5 21.2 %all-to-all-start.1 = ((bf16[8,20,16,128]{3,2,1,0:T(8,128)(2,1)}), bf16[8,20,16,128]{3,2,1,0:T(8,128)(2,1)S(1)}, u32[]{:S(2)}, u32[]{:S(2)}) async-start(bf16[8,20,16,128]{3,2,1,0:T(8,128)(2,1)} %get-tuple-element.109), calls=%async_computation.1 | async-start | bytes 1310720 | tf_op jit(solution)/shard_map/all_to_all | solution.py:382
  140.7 6.8 %copy-start.8 = (bf16[8,28,16,128]{3,2,1,0:T(8,128)(2,1)}, bf16[8,28,16,128]{3,2,1,0:T(8,128)(2,1)S(1)}, u32[]{:S(2)}) copy-start(bf16[8,28,16,128]{3,2,1,0:T(8,128)(2,1)S(1)} %collective-permute-done.15.refs_12_) | copy-start | bytes 2752516
  140.7 6.8 %copy-start.3 = (bf16[4,64,16,128]{3,2,1,0:T(8,128)(2,1)}, bf16[4,64,16,128]{3,2,1,0:T(8,128)(2,1)S(1)}, u32[]{:S(2)}) copy-start(bf16[4,64,16,128]{3,2,1,0:T(8,128)(2,1)S(1)} %collective-permute-done.14.refs_9_) | copy-start | bytes 3145732
  140.7 23.0 %copy-start.5 = (bf16[8,20,16,128]{3,2,1,0:T(8,128)(2,1)}, bf16[8,20,16,128]{3,2,1,0:T(8,128)(2,1)S(1)}, u32[]{:S(2)}) copy-start(bf16[8,20,16,128]{3,2,1,0:T(8,128)(2,1)S(1)} %all-to-all-done.1.refs_10_.refs_11_) | copy-start | bytes 1966084
  140.7 6.8 %collective-permute-start.17 = (bf16[8,28,16,128]{3,2,1,0:T(8,128)(2,1)}, bf16[8,28,16,128]{3,2,1,0:T(8,128)(2,1)}, u32[]{:S(2)}, u32[]{:S(2)}) collective-permute-start(bf16[8,28,16,128]{3,2,1,0:T(8,128)(2,1)} %collective-permute-done.16.refs_0_.refs_13_), channel_id=1, source_target_pairs={{0,1},{1,0},{2,3},{3,2},{4,5},{5,4},{6,7},{7,6},{8,9},{9,8},{10,11... | collective-permute-start | bytes 2752520 | tf_op jit(solution)/shard_map/ppermute | solution.py:20
  140.8 22.9 %collective-permute-start.19 = (bf16[8,20,16,128]{3,2,1,0:T(8,128)(2,1)S(1)}, bf16[8,20,16,128]{3,2,1,0:T(8,128)(2,1)}, u32[]{:S(2)}, u32[]{:S(2)}) collective-permute-start(bf16[8,20,16,128]{3,2,1,0:T(8,128)(2,1)S(1)} %all-to-all-done.1.refs_10_.refs_11_), channel_id=1, source_target_pairs={{0,2},{1,3},{2,0},{3,1},{4,6},{5,7},{6,4},{7,5},{8,10},{9,11},{10,... | collective-permute-start | bytes 1966088 | tf_op jit(solution)/shard_map/ppermute | solution.py:20
  143.0 22.0 %collective-permute-start.18 = (bf16[8,20,16,128]{3,2,1,0:T(8,128)(2,1)S(1)}, bf16[8,20,16,128]{3,2,1,0:T(8,128)(2,1)}, u32[]{:S(2)}, u32[]{:S(2)}) collective-permute-start(bf16[8,20,16,128]{3,2,1,0:T(8,128)(2,1)S(1)} %all-to-all-done.1.refs_10_.refs_11_), channel_id=1, source_target_pairs={{0,1},{1,0},{2,3},{3,2},{4,5},{5,4},{6,7},{7,6},{8,9},{9,8},{10,11... | collective-permute-start | bytes 1966088 | tf_op jit(solution)/shard_map/ppermute | solution.py:20
  143.2 21.8 %all-to-all-start.2 = ((bf16[8,16,16,128]{3,2,1,0:T(8,128)(2,1)}), bf16[8,16,16,128]{3,2,1,0:T(8,128)(2,1)S(1)}, u32[]{:S(2)}, u32[]{:S(2)}) async-start(bf16[8,16,16,128]{3,2,1,0:T(8,128)(2,1)} %get-tuple-element.120), calls=%async_computation.2 | async-start | bytes 1048576 | tf_op jit(solution)/shard_map/all_to_all | solution.py:382
  165.0 15.9 %copy-start.6 = (bf16[8,16,16,128]{3,2,1,0:T(8,128)(2,1)}, bf16[8,16,16,128]{3,2,1,0:T(8,128)(2,1)S(1)}, u32[]{:S(2)}) copy-start(bf16[8,16,16,128]{3,2,1,0:T(8,128)(2,1)S(1)} %all-to-all-done.2.refs_10_.refs_11_) | copy-start | bytes 1572868
  165.0 2.5 %collective-permute-start.20 = (bf16[8,20,16,128]{3,2,1,0:T(8,128)(2,1)}, bf16[8,20,16,128]{3,2,1,0:T(8,128)(2,1)S(1)}, u32[]{:S(2)}, u32[]{:S(2)}) collective-permute-start(bf16[8,20,16,128]{3,2,1,0:T(8,128)(2,1)} %collective-permute-done.19.refs_0_.refs_13_), channel_id=1, source_target_pairs={{0,1},{1,0},{2,3},{3,2},{4,5},{5,4},{6,7},{7,6},{8,9},{9,8},{10,11... | collective-permute-start | bytes 1966088 | tf_op jit(solution)/shard_map/ppermute | solution.py:20
  165.1 15.8 %collective-permute-start.21 = (bf16[8,16,16,128]{3,2,1,0:T(8,128)(2,1)S(1)}, bf16[8,16,16,128]{3,2,1,0:T(8,128)(2,1)S(1)}, u32[]{:S(2)}, u32[]{:S(2)}) collective-permute-start(bf16[8,16,16,128]{3,2,1,0:T(8,128)(2,1)S(1)} %all-to-all-done.2.refs_10_.refs_11_), channel_id=1, source_target_pairs={{0,1},{1,0},{2,3},{3,2},{4,5},{5,4},{6,7},{7,6},{8,9},{9,8},{10,11... | collective-permute-start | bytes 1572872 | tf_op jit(solution)/shard_map/ppermute | solution.py:20
  165.6 15.3 %collective-permute-start.22 = (bf16[8,16,16,128]{3,2,1,0:T(8,128)(2,1)S(1)}, bf16[8,16,16,128]{3,2,1,0:T(8,128)(2,1)S(1)}, u32[]{:S(2)}, u32[]{:S(2)}) collective-permute-start(bf16[8,16,16,128]{3,2,1,0:T(8,128)(2,1)S(1)} %all-to-all-done.2.refs_10_.refs_11_), channel_id=1, source_target_pairs={{0,2},{1,3},{2,0},{3,1},{4,6},{5,7},{6,4},{7,5},{8,10},{9,11},{10,... | collective-permute-start | bytes 1572872 | tf_op jit(solution)/shard_map/ppermute | solution.py:20
  167.5 0.8 copy-start.9
  180.9 2.0 %copy-start.10 = (bf16[8,16,16,128]{3,2,1,0:T(8,128)(2,1)}, bf16[8,16,16,128]{3,2,1,0:T(8,128)(2,1)S(1)}, u32[]{:S(2)}) copy-start(bf16[8,16,16,128]{3,2,1,0:T(8,128)(2,1)S(1)} %collective-permute-done.21.refs_12_) | copy-start | bytes 1572868
  180.9 2.0 %copy-start.11 = (bf16[8,16,16,128]{3,2,1,0:T(8,128)(2,1)}, bf16[8,16,16,128]{3,2,1,0:T(8,128)(2,1)S(1)}, u32[]{:S(2)}) copy-start(bf16[8,16,16,128]{3,2,1,0:T(8,128)(2,1)S(1)} %collective-permute-done.22.refs_13_) | copy-start | bytes 1572868
  180.9 2.0 %collective-permute-start.23 = (bf16[8,16,16,128]{3,2,1,0:T(8,128)(2,1)S(1)}, bf16[8,16,16,128]{3,2,1,0:T(8,128)(2,1)S(1)}, u32[]{:S(2)}, u32[]{:S(2)}) collective-permute-start(bf16[8,16,16,128]{3,2,1,0:T(8,128)(2,1)S(1)} %collective-permute-done.22.refs_13_), channel_id=1, source_target_pairs={{0,1},{1,0},{2,3},{3,2},{4,5},{5,4},{6,7},{7,6},{8,9},{9,8},{10,11... | collective-permute-start | bytes 1572872 | tf_op jit(solution)/shard_map/ppermute | solution.py:20
  182.9 0.8 copy-start.12

commit v3 on v2

v3 whole, which is shorter than its diff:
```python
import functools
import math

import jax
import jax.numpy as jnp
import numpy as np
from jax import lax
from jax.experimental import pallas as pl
from jax.experimental.pallas import tpu as pltpu
from jax.sharding import PartitionSpec as P

EARLY = (6, 5, 5)
MIB = 1 << 20
VMEM = 60 * MIB
RATED = 10**11


def swapped(value, axis, distance):
    pairs = [(i, i ^ distance) for i in range(lax.axis_size(axis))]
    return lax.ppermute(value, axis, pairs)


def handed(value):
    groups, blocks = lax.axis_size("freq"), lax.axis_size("blk")
    pairs = []
    for f in range(groups):
        for k in range(blocks):
            if k % 2 == 1:
                pairs.append((f * blocks + k, (f - 1) % groups * blocks + k))
            elif f + 1 < groups:
                pairs.append((f * blocks + k, (f + 1) * blocks + k))
    return lax.ppermute(value, ("freq", "blk"), pairs)


def reached(f, groups, shift, other):
    return (f // 2 + shift) % (groups // 2) * 2 + (f % 2 + other) % 2


def shifted(value, shift, other):
    groups = lax.axis_size("freq")
    pairs = [(f, reached(f, groups, shift, other)) for f in range(groups)]
    return lax.ppermute(value, "freq", pairs)


def cuts(pairs, shares):
    unit = pairs // 16
    ends = [0]
    for share in shares:
        ends.append(ends[-1] + share * unit)
    return ends


def dft_rows(channels, groups, parts):
    n = np.arange(channels, dtype=np.int64)
    phase = ((n[:, None] * n[None, :]) % channels).astype(np.float32)
    phase = phase * np.float32(2.0 * math.pi / channels)
    factor = np.float32(1.0 / math.sqrt(channels))
    cosine = np.cos(phase.astype(np.float64)).astype(np.float32) * factor
    sine = np.sin(phase.astype(np.float64)).astype(np.float32) * factor
    rows = np.stack([cosine, sine]).astype(jnp.bfloat16)
    rows = rows.reshape(2, groups, channels // groups, channels).transpose(1, 0, 2, 3)
    return [rows[:, :, 2 * a:2 * b].reshape(groups, -1, channels) for a, b in parts]


def weigh_frames(taps_ref, windows, out_ref):
    ntaps, channels = taps_ref.shape
    coeffs = taps_ref[...].astype(jnp.float32) * (1.0 / 1024.0)
    for part in range(2):
        held = {}
        for s, window in enumerate(windows):
            for frame in window:
                if frame not in held:
                    held[frame] = frame(part).astype(jnp.float32)
            total = coeffs[0:1] * held[window[0]]
            for t in range(1, ntaps):
                total = total + coeffs[t:t + 1] * held[window[t]]
            out_ref[s, :, part * channels:(part + 1) * channels] = total.astype(jnp.bfloat16)


def frames_of(refs, first, last, channels):
    return [lambda part, f=f: refs[part][0, :, f * channels:(f + 1) * channels] for f in range(first, last)]


def windows_of(frames, ntaps):
    return [frames[s:s + ntaps] for s in range(len(frames) - ntaps + 1)]


def weigh_late(taps_ref, real_ref, imag_ref, out_ref):
    ntaps, channels = taps_ref.shape
    frames = real_ref.shape[2] // channels
    used = frames_of((real_ref, imag_ref), frames - out_ref.shape[0] - ntaps + 1, frames, channels)
    weigh_frames(taps_ref, windows_of(used, ntaps), out_ref)


def weigh_early(where_ref, taps_ref, real_ref, imag_ref, passed_real_ref, passed_imag_ref, out_ref):
    ntaps, channels = taps_ref.shape
    frames = real_ref.shape[2] // channels
    passed = frames_of((passed_real_ref, passed_imag_ref), 0, ntaps - 1, channels)
    own = frames_of((real_ref, imag_ref), 0, frames, channels)
    count = out_ref.shape[0]

    @pl.when(where_ref[0] == 0)
    def _():
        weigh_frames(taps_ref, windows_of(passed + own[:count], ntaps), out_ref)

    @pl.when(where_ref[0] != 0)
    def _():
        keep = where_ref[1]
        before = [lambda part, frame=frame: frame(part) * keep for frame in own[frames - ntaps + 1:]]
        weigh_frames(taps_ref, windows_of(before + passed, ntaps) + windows_of(own[:count], ntaps), out_ref)


def weighted_spectra(taps, voltages, count, where=None, passed=None):
    channels = taps.shape[1]
    _, inputs, samples = voltages.shape
    step = min(64, inputs)
    operands = [taps]
    specs = [pl.BlockSpec(taps.shape, lambda i, *_: (0, 0))]
    for array in (voltages,) if passed is None else (voltages, passed):
        for part in range(2):
            operands.append(array)
            specs.append(pl.BlockSpec((1, step, array.shape[2]), lambda i, *_, part=part: (part, i, 0)))
    if passed is not None:
        operands = [where, *operands]
    return pl.pallas_call(
        weigh_late if passed is None else weigh_early,
        out_shape=jax.ShapeDtypeStruct((count, inputs, 2 * channels), jnp.bfloat16),
        grid_spec=pltpu.PrefetchScalarGridSpec(
            num_scalar_prefetch=0 if passed is None else 1,
            grid=(inputs // step,),
            in_specs=specs,
            out_specs=pl.BlockSpec((count, step, 2 * channels), lambda i, *_: (0, i, 0)),
        ),
        cost_estimate=pl.CostEstimate(
            flops=count * inputs * channels * 16, bytes_accessed=2 * inputs * samples * 4, transcendentals=0
        ),
        compiler_params=pltpu.CompilerParams(vmem_limit_bytes=VMEM),
    )(*operands)


def transform(weighted_ref, table_ref, turned_ref):
    count, inputs, _ = weighted_ref.shape
    groups, rows, depth = table_ref.shape
    size = rows // 2
    table = table_ref[...].reshape(groups * rows, depth)
    real, imag = [
        lax.dot_general(
            table, weighted_ref[:, :, part * depth:(part + 1) * depth].reshape(count * inputs, depth),
            (((1,), (1,)), ((), ())), preferred_element_type=jnp.float32,
        )
        for part in range(2)
    ]
    for g in range(groups):
        cosine, sine = slice(g * rows, g * rows + size), slice(g * rows + size, (g + 1) * rows)
        for s in range(count):
            of = slice(s * inputs, (s + 1) * inputs)
            turned_ref[g, :, s, :] = real[cosine, of] + imag[sine, of]
            turned_ref[g, :, count + s, :] = imag[cosine, of] - real[sine, of]


def transform_to(me_ref, weighted_ref, table_ref, *refs):
    *out_refs, turned_ref = refs
    transform(weighted_ref, table_ref, turned_ref)
    for i, out_ref in enumerate(out_refs):
        @pl.when(pl.program_id(0) == i)
        def _(out_ref=out_ref):
            out_ref[...] = turned_ref[...].reshape(out_ref.shape).astype(jnp.bfloat16)


def spectra_to(me, weighted, table, other):
    count, inputs, _ = weighted.shape
    groups, rows, depth = table.shape
    shifts = groups // 2
    shape = (rows // 4, 4 * count, inputs)
    return pl.pallas_call(
        transform_to,
        out_shape=[jax.ShapeDtypeStruct(shape, jnp.bfloat16)] * shifts,
        grid_spec=pltpu.PrefetchScalarGridSpec(
            num_scalar_prefetch=1,
            grid=(shifts,),
            in_specs=[
                pl.BlockSpec(weighted.shape, lambda i, m: (0, 0, 0)),
                pl.BlockSpec((1, rows, depth), lambda i, m: (reached(m[0], groups, i, other), 0, 0)),
            ],
            out_specs=[pl.BlockSpec(shape, lambda i, m: (0, 0, 0))] * shifts,
            scratch_shapes=[pltpu.VMEM((1, rows // 2, 2 * count, inputs), jnp.float32)],
        ),
        cost_estimate=pl.CostEstimate(
            flops=2 * groups * rows * depth * count * inputs,
            bytes_accessed=groups * rows * depth + weighted.size * 3,
            transcendentals=0,
        ),
        compiler_params=pltpu.CompilerParams(vmem_limit_bytes=VMEM),
    )(me, weighted, table)


def transform_by(ends, weighted_ref, table_ref, *refs):
    *out_refs, turned_ref = refs
    transform(weighted_ref, table_ref, turned_ref)
    for c, out_ref in enumerate(out_refs):
        value = turned_ref[:, 2 * ends[c]:2 * ends[c + 1]]
        out_ref[...] = value.reshape(out_ref.shape).astype(jnp.bfloat16)


def spectra_by(weighted, table, ends):
    count, inputs, _ = weighted.shape
    groups, rows, depth = table.shape
    sizes = [b - a for a, b in zip(ends[:-1], ends[1:])]
    some = 4 if rows < 128 * 4 // 3 else 2
    return pl.pallas_call(
        functools.partial(transform_by, ends),
        out_shape=[jax.ShapeDtypeStruct((groups, size, 4 * count, inputs), jnp.bfloat16) for size in sizes],
        grid=(groups // some,),
        in_specs=[
            pl.BlockSpec(weighted.shape, lambda i: (0, 0, 0)),
            pl.BlockSpec((some, rows, depth), lambda i: (i, 0, 0)),
        ],
        out_specs=[pl.BlockSpec((some, size, 4 * count, inputs), lambda i: (i, 0, 0, 0)) for size in sizes],
        scratch_shapes=[pltpu.VMEM((some, rows // 2, 2 * count, inputs), jnp.float32)],
        cost_estimate=pl.CostEstimate(
            flops=4 * groups * rows * depth * count * inputs,
            bytes_accessed=groups * rows * depth * 2 + weighted.size * 4,
            transcendentals=0,
        ),
        compiler_params=pltpu.CompilerParams(vmem_limit_bytes=VMEM),
    )(weighted, table)


def tick(token, *values):
    def body(token_ref, *refs):
        refs[-1][...] = token_ref[...]

    return pl.pallas_call(
        body,
        out_shape=jax.ShapeDtypeStruct(token.shape, token.dtype),
        in_specs=[pl.BlockSpec(token.shape, lambda: (0, 0))] + [pl.BlockSpec(memory_space=pl.ANY)] * len(values),
        out_specs=pl.BlockSpec(token.shape, lambda: (0, 0)),
        cost_estimate=pl.CostEstimate(flops=RATED, bytes_accessed=0, transcendentals=0),
        compiler_params=pltpu.CompilerParams(vmem_limit_bytes=VMEM),
    )(token, *values)


def correlate(factor, distances, nlate, ntaps, me_ref, *refs):
    blocks = len(distances)
    late = [refs[q * nlate:(q + 1) * nlate] for q in range(blocks)]
    early = refs[blocks * nlate:blocks * (nlate + 1)]
    out_ref = refs[-1]
    groups, pairs, rows, inputs = early[0].shape
    half = rows // 2
    depth = 2 * groups * rows
    sign = jnp.where(
        lax.broadcasted_iota(jnp.int32, (4 * groups, half, inputs), 1) < half // 2, factor, -factor
    ).astype(jnp.float32)
    of_first = lax.broadcasted_iota(jnp.int32, (inputs, depth), 1) % rows < half
    keep = [jnp.where(of_first, 1.0, 0.0).astype(jnp.bfloat16), jnp.where(of_first, 0.0, 1.0).astype(jnp.bfloat16)]

    ahead = lax.broadcasted_iota(jnp.int32, (rows, inputs), 0) % (half // 2) < ntaps - 1
    ahead, level = [jnp.where(ahead, a, 1.0 - a).astype(jnp.bfloat16) for a in (1.0, 0.0)]

    def pair(p, mine):
        loaded = []
        for q in range(blocks):
            tiles = [ref[j, p] for ref in late[q] for j in range(ref.shape[0])]
            for j in range(groups):
                if (mine ^ distances[q]) % 2 == 0:
                    tiles.append(early[q][j, p])
                else:
                    tiles.append(early[q][(j - 1) % groups, p] * ahead + early[q][j, p] * level)
            loaded.append(jnp.concatenate(tiles, axis=0))
        own = loaded[0].astype(jnp.float32)
        turned = pltpu.roll(own.reshape(4 * groups, half, inputs), half // 2, axis=1) * sign
        straight = (own * factor).astype(jnp.bfloat16).T
        turned = turned.reshape(depth, inputs).astype(jnp.bfloat16).T
        left = jnp.concatenate([side * mask for mask in keep for side in (straight, turned)], axis=0)
        product = jnp.dot(left, jnp.concatenate(loaded, axis=1), preferred_element_type=jnp.float32)
        for q in range(blocks):
            first = (mine ^ distances[q]) * inputs
            for h in range(2):
                for part in range(2):
                    block = product[(2 * h + part) * inputs:(2 * h + part + 1) * inputs, q * inputs:(q + 1) * inputs]
                    out_ref[part, 2 * p + h, :, first:first + inputs] = block

    for mine in range(blocks):
        @pl.when(me_ref[0] == mine)
        def _(mine=mine):
            for p in range(pairs):
                pair(p, mine)


def correlated(me, held, distances, at, shape, factor, ntaps, visible, token=None):
    *late, early = held
    groups, pairs, rows, inputs = early[0].shape
    step = math.gcd(4, math.gcd(pairs, at))
    wide = inputs * len(distances)
    operands, specs = [me], []
    for q in distances:
        for array in late:
            operands.append(array[q])
            specs.append(pl.BlockSpec((array[q].shape[0], step, rows, inputs), lambda i, *_: (0, at // step + i, 0, 0)))
    for q in distances:
        operands.append(early[q])
        specs.append(pl.BlockSpec((groups, step, rows, inputs), lambda i, *_: (0, i, 0, 0)))
    aliases = {}
    if visible is not None:
        aliases = {len(operands): 0}
        operands.append(visible)
        specs.append(pl.BlockSpec(memory_space=pl.ANY))
    if token is not None:
        operands.append(token)
        specs.append(pl.BlockSpec(memory_space=pl.ANY))
    depth = groups * rows
    return pl.pallas_call(
        functools.partial(correlate, factor, distances, len(late), ntaps),
        out_shape=jax.ShapeDtypeStruct(shape, jnp.float32),
        grid_spec=pltpu.PrefetchScalarGridSpec(
            num_scalar_prefetch=1,
            grid=(pairs // step,),
            in_specs=specs,
            out_specs=pl.BlockSpec(
                (2, 2 * step, inputs, wide), lambda i, *_: (0, at // step + i, 0, 0)
            ),
        ),
        input_output_aliases=aliases,
        cost_estimate=pl.CostEstimate(
            flops=2 * 2 * pairs * 2 * inputs * wide * depth, bytes_accessed=2 * pairs * 2 * inputs * wide * 4, transcendentals=0
        ),
        compiler_params=pltpu.CompilerParams(vmem_limit_bytes=VMEM),
    )(*operands)


def local(tables, voltages, taps):
    ntaps, channels = taps.shape
    inputs = voltages.shape[1]
    frames = voltages.shape[2] // channels
    groups = lax.axis_size("freq")
    blocks = lax.axis_size("blk")
    group = channels // groups
    ends = cuts(group // 2, EARLY)
    half = frames // 2
    factor = 1.0 / math.sqrt(frames * groups)
    freq = lax.axis_index("freq").astype(jnp.int32)
    blk = lax.axis_index("blk").astype(jnp.int32)
    odd = blk % 2
    me = freq.reshape(1)
    high = groups // 2
    shape = (2, group, inputs, inputs * blocks)
    both = lax.optimization_barrier
    table, first_table, other_table = tables

    begin = jnp.where(odd == 0, frames - ntaps + 1, 0) * channels
    given = lax.dynamic_slice_in_dim(voltages, begin, (ntaps - 1) * channels, 2).astype(jnp.bfloat16)
    where = jnp.stack([odd, (freq < groups - 1).astype(jnp.int32)])

    passed = handed(given)
    weighted = weighted_spectra(taps, voltages, half)
    made = spectra_to(me, weighted, table, 0)
    near = [made[0]] + [shifted(made[shift], shift, 0) for shift in range(1, high)]
    made = spectra_to(me, weighted, table, 1)
    near, passed, made = both((near, passed, made))

    held = [{0: jnp.stack(near)}]
    far = [shifted(made[shift], shift, 1) for shift in range(high)]
    held[0][2] = swapped(held[0][0], "blk", 2)
    early_weighted = weighted_spectra(taps, voltages, half, where, passed)
    early = spectra_by(early_weighted, first_table, ends[:2])
    held.append({0: jnp.stack(far)})
    held, early, early_weighted = both((held, early, early_weighted))

    nearly = len(ends) - 1
    visible = None
    token = jnp.zeros((8, 128), jnp.float32)
    for step in range(nearly + 2):
        new = {}
        if step < nearly:
            new[step + 2, 0] = lax.all_to_all(early[step], "freq", split_axis=0, concat_axis=0, tiled=True)
        if step <= nearly:
            new[step + 1, 2] = swapped(held[step + 1][0], "blk", 2)
            new[step + 1, 1] = swapped(held[step + 1][0], "blk", 1)
        if step == 0:
            new[0, 1] = swapped(held[0][0], "blk", 1)
            early = early + spectra_by(early_weighted, other_table, [end - ends[1] for end in ends[1:]])
        new[step, 3] = swapped(held[step][2], "blk", 1)
        if step >= 2:
            parts = [held[0], held[1], {**held[step], 3: new[step, 3]}]
            visible = correlated(blk.reshape(1), parts, (0, 1, 2, 3), ends[step - 2], shape, factor, ntaps, visible, token)
        if step < nearly:
            token = tick(token, new[step + 1, 2], *([] if visible is None else [visible]))
        if step == nearly + 1:
            break
        new, held, early, visible, token = both((new, held, early, visible, token))
        held.append({})
        for (c, q), value in new.items():
            held[c][q] = value
    return visible


def solution(mesh):
    groups = mesh.shape["freq"]

    def run(voltages, taps):
        channels = taps.shape[1]
        ends = cuts(channels // groups // 2, EARLY)
        tables = dft_rows(channels, groups, ((0, ends[-1]), (0, ends[1]), (ends[1], ends[-1])))
        return jax.shard_map(
            functools.partial(local, tables),
            mesh=mesh,
            in_specs=(P(None, "blk", "freq"), P()),
            out_specs=P(None, "freq", "blk", None),
            check_vma=False,
        )(voltages, taps)

    return run
```

time: 196 us -> 186 us (0.949)
  Pallas kernels: 79.2 us -> 75.2 us
  other arithmetic: 8.03 us -> 4.86 us
  waiting for transfers between devices: 55.6 us -> 52.8 us
    ppermute x7, waiting for transfers between devices: 21.4 us -> 15.4 us  [shifted(): return lax.ppermute(value, 'freq', pairs)]
    pallas_call x6 -> x7, Pallas kernels: 62 us -> 58.5 us  [the longest x3 33.1 us: correlated(): pl.pallas_call(functools.partial(correlate, factor, distances, len(late),...]
    all_to_all x3, waiting for transfers between devices: 5.1 us -> 8.23 us  [local(): lax.all_to_all(early[step], 'freq', split_axis=0, concat_axis=0, tiled=True)]
    unnamed x28 -> x30, local copies, waits for them, and re-layouts: 3.57 us -> 5.33 us
    ppermute x2 -> x1, starting transfers between devices: 5.62 us -> 4.94 us  [handed(): return lax.ppermute(value, ('freq', 'blk'), pairs)]
  transfers between devices with their start and end apart: 27 -> 26, of which waited for: 8 -> 10; matrix products, arithmetic and copies ran while one was open for 2% -> 1% of each run, Pallas kernels for 35% -> 35%
where the time goes in v3:
time: 186 us; the launch traced here: 185 us
  Pallas kernels  75.2 us (40%)
  waiting for transfers between devices  52.8 us (28%)
  starting transfers between devices  46.2 us (25%)
  local copies, waits for them, and re-layouts  5.93 us (3%)
  other arithmetic  4.86 us (3%)
    pallas_call x3, Pallas kernels, correlated(): pl.pallas_call(functools.partial(correlate, factor, distances, len(late),...  33.1 us
    ppermute x15, waiting for transfers between devices, swapped(): return lax.ppermute(value, axis, pairs)  29.1 us
    ppermute x7, starting transfers between devices, shifted(): return lax.ppermute(value, 'freq', pairs)  18.4 us
    all_to_all x3, starting transfers between devices, local(): lax.all_to_all(early[step], 'freq', split_axis=0, concat_axis=0, tiled=True)  15.8 us
    ppermute x7, waiting for transfers between devices, shifted(): return lax.ppermute(value, 'freq', pairs)  15.4 us
    pallas_call x2, Pallas kernels, spectra_to(): pl.pallas_call(transform_to, out_shape=[jax.ShapeDtypeStruct(shape, jnp.b...  13.9 us
    pallas_call x2, Pallas kernels, spectra_by(): pl.pallas_call(functools.partial(transform_by, ends), out_shape=[jax.Shap...  12.8 us
    pallas_call x2, Pallas kernels, weighted_spectra(): pl.pallas_call(weigh_late if passed is None else weigh_early, out_shape=j...  11.6 us
  transfers between devices with their start and end apart: 26, of which 10 were waited for; matrix products, arithmetic and copies ran while one was open for 1% of the time, Pallas kernels for 35%

profile of v3, /device:TPU:0, one launch (start us, length us, event | category | flops | bytes accessed | tf_op | source)
XLA Modules:
  0.0 185.2 jit_solution(11565010560816792059)
XLA Ops:
  0.0 2.1 %dynamic-slice_convert_fusion = bf16[2,128,3072]{2,1,0:T(8,128)(2,1)S(1)} fusion(s32[2,128,8192]{2,1,0:T(8,128)} %imag_ref.3, s32[]{:T(128)S(6)} %select_n.16), kind=kLoop, calls=%fused_computation | loop fusion | flops 786432 | bytes 4718596 | tf_op jit(solution)/shard_map/convert_element_type | solution.py:351
  2.1 4.9 %collective-permute-start.3 = (bf16[2,128,3072]{2,1,0:T(8,128)(2,1)S(1)}, bf16[2,128,3072]{2,1,0:T(8,128)(2,1)S(1)}, u32[]{:S(2)}, u32[]{:S(2)}) collective-permute-start(bf16[2,128,3072]{2,1,0:T(8,128)(2,1)S(1)} %dynamic-slice_convert_fusion), channel_id=1, source_target_pairs={{0,4},{1,29},{2,6},{3,31},{4,8},{5,1},{6,10},{7,3},{8,12},{9,5},{1... | collective-permute-start | bytes 4718600 | tf_op jit(solution)/shard_map/ppermute | solution.py:32
  7.1 5.2 %shard_map.55.weighted_ref = bf16[4,128,2048]{2,1,0:T(8,128)(2,1)} custom-call(s32[4,1024]{1,0:T(4,128)} %taps_ref.3, s32[2,128,8192]{2,1,0:T(8,128)} %imag_ref.3, s32[2,128,8192]{2,1,0:T(8,128)} %imag_ref.3), custom_call_target="tpu_custom_call" | custom-call | flops 8388608 | bytes 8388608 | tf_op jit(solution)/shard_map/pallas_call | solution.py:125
  12.2 6.9 %shard_map.56 = (bf16[64,16,128]{2,1,0:T(8,128)(2,1)}, bf16[64,16,128]{2,1,0:T(8,128)(2,1)}, bf16[64,16,128]{2,1,0:T(8,128)(2,1)}, bf16[64,16,128]{2,1,0:T(8,128)(2,1)}) custom-call(s32[1]{0:T(128)} %bitcast.1.me_ref, bf16[4,128,2048]{2,1,0:T(8,128)(2,1)} %shard_map.55.weighted_ref, bf16[8,256,1024]{2,1,0:T(8,128)(2,1)} %constant.39.clone.table_ref), custom_call_target="tpu_custom_call" | custom-call | flops 2147483648 | bytes 5242880 | tf_op jit(solution)/shard_map/pallas_call | solution.py:175
  19.2 1.5 collective-permute-start
  20.7 2.6 %collective-permute-start.1 = (bf16[64,16,128]{2,1,0:T(8,128)(2,1)}, bf16[64,16,128]{2,1,0:T(8,128)(2,1)S(1)}, u32[]{:S(2)}, u32[]{:S(2)}) collective-permute-start(bf16[64,16,128]{2,1,0:T(8,128)(2,1)} %get-tuple-element.83), channel_id=1, source_target_pairs={{0,16},{4,20},{8,24},{12,28},{16,0},{20,4},{24,8},{28,12},{1,17},{... | collective-permute-start | bytes 786440 | tf_op jit(solution)/shard_map/ppermute | solution.py:42
  23.3 1.3 collective-permute-start.2
  24.6 6.9 %shard_map.57 = (bf16[64,16,128]{2,1,0:T(8,128)(2,1)}, bf16[64,16,128]{2,1,0:T(8,128)(2,1)}, bf16[64,16,128]{2,1,0:T(8,128)(2,1)}, bf16[64,16,128]{2,1,0:T(8,128)(2,1)}) custom-call(s32[1]{0:T(128)} %bitcast.1.me_ref, bf16[4,128,2048]{2,1,0:T(8,128)(2,1)} %shard_map.55.weighted_ref, bf16[8,256,1024]{2,1,0:T(8,128)(2,1)} %constant.39.clone.table_ref), custom_call_target="tpu_custom_call" | custom-call | flops 2147483648 | bytes 5242880 | tf_op jit(solution)/shard_map/pallas_call | solution.py:175
  31.5 10.5 %collective-permute-done.1 = bf16[64,16,128]{2,1,0:T(8,128)(2,1)S(1)} collective-permute-done((bf16[64,16,128]{2,1,0:T(8,128)(2,1)}, bf16[64,16,128]{2,1,0:T(8,128)(2,1)S(1)}, u32[]{:S(2)}, u32[]{:S(2)}) %collective-permute-start.1) | collective-permute-done | bytes 262176 | tf_op jit(solution)/shard_map/ppermute | solution.py:42
  42.0 1.2 copy-done.4
  43.2 1.1 pad_maximum_fusion.refs_0_
  44.3 1.6 collective-permute-start.4
  45.9 2.0 %collective-permute-start.5 = (bf16[64,16,128]{2,1,0:T(8,128)(2,1)}, bf16[64,16,128]{2,1,0:T(8,128)(2,1)S(1)}, u32[]{:S(2)}, u32[]{:S(2)}) collective-permute-start(bf16[64,16,128]{2,1,0:T(8,128)(2,1)} %get-tuple-element.93), channel_id=1, source_target_pairs={{0,4},{4,0},{8,12},{12,8},{16,20},{20,16},{24,28},{28,24},{1,5},{5... | collective-permute-start | bytes 786440 | tf_op jit(solution)/shard_map/ppermute | solution.py:42
  47.8 8.3 %collective-permute-start.6 = (bf16[64,16,128]{2,1,0:T(8,128)(2,1)}, bf16[64,16,128]{2,1,0:T(8,128)(2,1)S(1)}, u32[]{:S(2)}, u32[]{:S(2)}) collective-permute-start(bf16[64,16,128]{2,1,0:T(8,128)(2,1)} %get-tuple-element.94), channel_id=1, source_target_pairs={{0,12},{4,8},{8,20},{12,16},{16,28},{20,24},{24,4},{28,0},{1,13},{... | collective-permute-start | bytes 786440 | tf_op jit(solution)/shard_map/ppermute | solution.py:42
  56.2 2.7 %collective-permute-start.7 = (bf16[64,16,128]{2,1,0:T(8,128)(2,1)}, bf16[64,16,128]{2,1,0:T(8,128)(2,1)S(1)}, u32[]{:S(2)}, u32[]{:S(2)}) collective-permute-start(bf16[64,16,128]{2,1,0:T(8,128)(2,1)} %get-tuple-element.95), channel_id=1, source_target_pairs={{0,20},{4,16},{8,28},{12,24},{16,4},{20,0},{24,12},{28,8},{1,21},{... | collective-permute-start | bytes 786440 | tf_op jit(solution)/shard_map/ppermute | solution.py:42
  58.9 0.6 pad_add_fusion.where_ref
  59.5 6.5 %shard_map.58.weighted_ref = bf16[4,128,2048]{2,1,0:T(8,128)(2,1)} custom-call(s32[2]{0:T(128)} %pad_add_fusion.where_ref, s32[4,1024]{1,0:T(4,128)} %taps_ref.3, s32[2,128,8192]{2,1,0:T(8,128)} %imag_ref.3, s32[2,128,8192]{2,1,0:T(8,128)} %imag_ref.3, bf16[2,128,3072]{2,1,0:T(8,128)(2,1)} %copy-done.4, bf16[2,128,3072]{2,1,0:T(8,128)(2,1)} %copy-done.4), custom_call_target="tpu_custom_call" | custom-call | flops 8388608 | bytes 8388608 | tf_op jit(solution)/shard_map/pallas_call | solution.py:125
  65.9 5.5 %shard_map.59 = bf16[8,24,16,128]{3,2,1,0:T(8,128)(2,1)} custom-call(bf16[4,128,2048]{2,1,0:T(8,128)(2,1)} %shard_map.58.weighted_ref, bf16[8,96,1024]{2,1,0:T(8,128)(2,1)} %constant.40.clone.table_ref), custom_call_target="tpu_custom_call" | custom-call | flops 1610612736 | bytes 5767168 | tf_op jit(solution)/shard_map/pallas_call | solution.py:210
  71.4 4.9 %collective-permute-done.7 = bf16[64,16,128]{2,1,0:T(8,128)(2,1)S(1)} collective-permute-done((bf16[64,16,128]{2,1,0:T(8,128)(2,1)}, bf16[64,16,128]{2,1,0:T(8,128)(2,1)S(1)}, u32[]{:S(2)}, u32[]{:S(2)}) %collective-permute-start.7) | collective-permute-done | bytes 262176 | tf_op jit(solution)/shard_map/ppermute | solution.py:42
  76.4 0.7 copy-done.14
  77.1 1.1 pad_maximum_fusion.1.refs_1_
  78.2 0.6 collective-permute-start.12
  78.8 7.4 %all-to-all-start = ((bf16[8,24,16,128]{3,2,1,0:T(8,128)(2,1)}), bf16[8,24,16,128]{3,2,1,0:T(8,128)(2,1)}, u32[]{:S(2)}, u32[]{:S(2)}) async-start(bf16[8,24,16,128]{3,2,1,0:T(8,128)(2,1)} %shard_map.59), calls=%async_computation | async-start | bytes 1572864 | tf_op jit(solution)/shard_map/all_to_all | solution.py:375
  86.7 7.3 %shard_map.60 = (bf16[8,20,16,128]{3,2,1,0:T(8,128)(2,1)}, bf16[8,20,16,128]{3,2,1,0:T(8,128)(2,1)}) custom-call(bf16[4,128,2048]{2,1,0:T(8,128)(2,1)} %shard_map.58.weighted_ref, bf16[8,160,1024]{2,1,0:T(8,128)(2,1)} %constant.41.clone.table_ref), custom_call_target="tpu_custom_call" | custom-call | flops 2684354560 | bytes 6815744 | tf_op jit(solution)/shard_map/pallas_call | solution.py:210
  94.0 9.3 %collective-permute-done.12.refs_0_.refs_5_ = bf16[4,64,16,128]{3,2,1,0:T(8,128)(2,1)} collective-permute-done((bf16[4,64,16,128]{3,2,1,0:T(8,128)(2,1)S(1)}, bf16[4,64,16,128]{3,2,1,0:T(8,128)(2,1)}, u32[]{:S(2)}, u32[]{:S(2)}) %collective-permute-start.12) | collective-permute-done | bytes 1048608 | tf_op jit(solution)/shard_map/ppermute | solution.py:20
  103.4 0.6 broadcast_in_dim.3.token_ref
  104.0 1.3 shard_map.61.token_ref
  105.3 1.8 all-to-all-done.refs_8_
  107.0 1.5 collective-permute-start.15
  108.5 4.7 %all-to-all-start.1 = ((bf16[8,20,16,128]{3,2,1,0:T(8,128)(2,1)}), bf16[8,20,16,128]{3,2,1,0:T(8,128)(2,1)S(1)}, u32[]{:S(2)}, u32[]{:S(2)}) async-start(bf16[8,20,16,128]{3,2,1,0:T(8,128)(2,1)} %get-tuple-element.107), calls=%async_computation.1 | async-start | bytes 1310720 | tf_op jit(solution)/shard_map/all_to_all | solution.py:375
  113.5 12.6 %collective-permute-done.15.refs_0_.refs_10_ = bf16[8,24,16,128]{3,2,1,0:T(8,128)(2,1)S(1)} collective-permute-done((bf16[8,24,16,128]{3,2,1,0:T(8,128)(2,1)}, bf16[8,24,16,128]{3,2,1,0:T(8,128)(2,1)S(1)}, u32[]{:S(2)}, u32[]{:S(2)}) %collective-permute-start.15) | collective-permute-done | bytes 786464 | tf_op jit(solution)/shard_map/ppermute | solution.py:20
  126.1 0.9 copy-done.7
  127.0 1.3 shard_map.62.refs_12_.token_ref
  128.3 3.0 %all-to-all-done.1.refs_8_ = bf16[8,20,16,128]{3,2,1,0:T(8,128)(2,1)S(1)} async-done(((bf16[8,20,16,128]{3,2,1,0:T(8,128)(2,1)}), bf16[8,20,16,128]{3,2,1,0:T(8,128)(2,1)S(1)}, u32[]{:S(2)}, u32[]{:S(2)}) %all-to-all-start.1) | async-done | bytes 655392 | tf_op jit(solution)/shard_map/all_to_all | solution.py:375
  131.3 1.5 collective-permute-start.18
  133.1 3.7 %all-to-all-start.2 = ((bf16[8,20,16,128]{3,2,1,0:T(8,128)(2,1)}), bf16[8,20,16,128]{3,2,1,0:T(8,128)(2,1)S(1)}, u32[]{:S(2)}, u32[]{:S(2)}) async-start(bf16[8,20,16,128]{3,2,1,0:T(8,128)(2,1)} %get-tuple-element.118), calls=%async_computation.2 | async-start | bytes 1310720 | tf_op jit(solution)/shard_map/all_to_all | solution.py:375
  136.8 0.9 copy-done.8
  137.7 12.2 %shard_map.63.refs_1_.refs_12_ = f32[2,128,128,512]{3,2,1,0:T(8,128)} custom-call(s32[1]{0:T(128)} %bitcast.me_ref, bf16[4,64,16,128]{3,2,1,0:T(8,128)(2,1)} %copy-done, bf16[4,64,16,128]{3,2,1,0:T(8,128)(2,1)} %copy-done.1, bf16[4,64,16,128]{3,2,1,0:T(8,128)(2,1)} %collective-permute-done.9.refs_2_, ...), custom_call_target="tpu_custom_call" | custom-call | flops 1610612736 | bytes 25165824 | tf_op jit(solution)/shard_map/pallas_call | solution.py:312
  149.8 1.3 shard_map.64.refs_13_
  151.1 3.4 %all-to-all-done.2.refs_8_ = bf16[8,20,16,128]{3,2,1,0:T(8,128)(2,1)S(1)} async-done(((bf16[8,20,16,128]{3,2,1,0:T(8,128)(2,1)}), bf16[8,20,16,128]{3,2,1,0:T(8,128)(2,1)S(1)}, u32[]{:S(2)}, u32[]{:S(2)}) %all-to-all-start.2) | async-done | bytes 655392 | tf_op jit(solution)/shard_map/all_to_all | solution.py:375
  154.6 0.5 collective-permute-start.21
  155.3 1.6 collective-permute-done.19.refs_11_
  156.9 0.8 copy-done.12
  157.7 10.5 %shard_map.65.refs_12_ = f32[2,128,128,512]{3,2,1,0:T(8,128)} custom-call(s32[1]{0:T(128)} %bitcast.me_ref, bf16[4,64,16,128]{3,2,1,0:T(8,128)(2,1)} %copy-done, bf16[4,64,16,128]{3,2,1,0:T(8,128)(2,1)} %copy-done.1, bf16[4,64,16,128]{3,2,1,0:T(8,128)(2,1)} %collective-permute-done.9.refs_2_, ...), custom_call_target="tpu_custom_call", output_to_operand_aliasing={{}: (13, {})} | custom-call | flops 1342177280 | bytes 20971520 | tf_op jit(solution)/shard_map/pallas_call | solution.py:312
  168.2 3.5 %collective-permute-done.21.refs_10_ = bf16[8,20,16,128]{3,2,1,0:T(8,128)(2,1)S(1)} collective-permute-done((bf16[8,20,16,128]{3,2,1,0:T(8,128)(2,1)S(1)}, bf16[8,20,16,128]{3,2,1,0:T(8,128)(2,1)S(1)}, u32[]{:S(2)}, u32[]{:S(2)}) %collective-permute-start.21) | collective-permute-done | bytes 655392 | tf_op jit(solution)/shard_map/ppermute | solution.py:20
  171.8 2.1 %collective-permute-done.22.refs_11_ = bf16[8,20,16,128]{3,2,1,0:T(8,128)(2,1)S(1)} collective-permute-done((bf16[8,20,16,128]{3,2,1,0:T(8,128)(2,1)S(1)}, bf16[8,20,16,128]{3,2,1,0:T(8,128)(2,1)S(1)}, u32[]{:S(2)}, u32[]{:S(2)}) %collective-permute-start.22) | collective-permute-done | bytes 655392 | tf_op jit(solution)/shard_map/ppermute | solution.py:20
  173.9 0.8 copy-done.11
  174.7 10.5 %shard_map.66 = f32[2,128,128,512]{3,2,1,0:T(8,128)} custom-call(s32[1]{0:T(128)} %bitcast.me_ref, bf16[4,64,16,128]{3,2,1,0:T(8,128)(2,1)} %copy-done, bf16[4,64,16,128]{3,2,1,0:T(8,128)(2,1)} %copy-done.1, bf16[4,64,16,128]{3,2,1,0:T(8,128)(2,1)} %collective-permute-done.9.refs_2_, ...), custom_call_target="tpu_custom_call", output_to_operand_aliasing={{}: (13, {})} | custom-call | flops 1342177280 | bytes 20971520 | tf_op jit(solution)/shard_map/pallas_call | solution.py:312
  (51 shorter events, 1.4 us)
Async XLA Ops:
  2.1 39.9 %collective-permute-start.3 = (bf16[2,128,3072]{2,1,0:T(8,128)(2,1)S(1)}, bf16[2,128,3072]{2,1,0:T(8,128)(2,1)S(1)}, u32[]{:S(2)}, u32[]{:S(2)}) collective-permute-start(bf16[2,128,3072]{2,1,0:T(8,128)(2,1)S(1)} %dynamic-slice_convert_fusion), channel_id=1, source_target_pairs={{0,4},{1,29},{2,6},{3,31},{4,8},{5,1},{6,10},{7,3},{8,12},{9,5},{1... | collective-permute-start | bytes 4718600 | tf_op jit(solution)/shard_map/ppermute | solution.py:32
  19.2 12.4 %collective-permute-start = (bf16[64,16,128]{2,1,0:T(8,128)(2,1)}, bf16[64,16,128]{2,1,0:T(8,128)(2,1)S(1)}, u32[]{:S(2)}, u32[]{:S(2)}) collective-permute-start(bf16[64,16,128]{2,1,0:T(8,128)(2,1)} %get-tuple-element.82), channel_id=1, source_target_pairs={{0,8},{4,12},{8,16},{12,20},{16,24},{20,28},{24,0},{28,4},{1,9},{5... | collective-permute-start | bytes 786440 | tf_op jit(solution)/shard_map/ppermute | solution.py:42
  20.7 21.3 %collective-permute-start.1 = (bf16[64,16,128]{2,1,0:T(8,128)(2,1)}, bf16[64,16,128]{2,1,0:T(8,128)(2,1)S(1)}, u32[]{:S(2)}, u32[]{:S(2)}) collective-permute-start(bf16[64,16,128]{2,1,0:T(8,128)(2,1)} %get-tuple-element.83), channel_id=1, source_target_pairs={{0,16},{4,20},{8,24},{12,28},{16,0},{20,4},{24,8},{28,12},{1,17},{... | collective-permute-start | bytes 786440 | tf_op jit(solution)/shard_map/ppermute | solution.py:42
  23.3 19.9 %copy-start.13 = (bf16[64,16,128]{2,1,0:T(8,128)(2,1)S(1)}, bf16[64,16,128]{2,1,0:T(8,128)(2,1)}, u32[]{:S(2)}) copy-start(bf16[64,16,128]{2,1,0:T(8,128)(2,1)} %get-tuple-element.89) | copy-start | bytes 786436
  23.3 18.7 %collective-permute-start.2 = (bf16[64,16,128]{2,1,0:T(8,128)(2,1)}, bf16[64,16,128]{2,1,0:T(8,128)(2,1)}, u32[]{:S(2)}, u32[]{:S(2)}) collective-permute-start(bf16[64,16,128]{2,1,0:T(8,128)(2,1)} %get-tuple-element.84), channel_id=1, source_target_pairs={{0,24},{4,28},{8,0},{12,4},{16,8},{20,12},{24,16},{28,20},{1,25},{... | collective-permute-start | bytes 786440 | tf_op jit(solution)/shard_map/ppermute | solution.py:42
  42.0 1.2 copy-start.4
  44.3 41.9 %copy-start = (bf16[4,64,16,128]{3,2,1,0:T(8,128)(2,1)}, bf16[4,64,16,128]{3,2,1,0:T(8,128)(2,1)S(1)}, u32[]{:S(2)}) copy-start(bf16[4,64,16,128]{3,2,1,0:T(8,128)(2,1)S(1)} %pad_maximum_fusion.refs_0_) | copy-start | bytes 3145732
  44.3 33.9 %collective-permute-start.4 = (bf16[4,64,16,128]{3,2,1,0:T(8,128)(2,1)S(1)}, bf16[4,64,16,128]{3,2,1,0:T(8,128)(2,1)S(1)}, u32[]{:S(2)}, u32[]{:S(2)}) collective-permute-start(bf16[4,64,16,128]{3,2,1,0:T(8,128)(2,1)S(1)} %pad_maximum_fusion.refs_0_), channel_id=1, source_target_pairs={{0,2},{1,3},{2,0},{3,1},{4,6},{5,7},{6,4},{7,5},{8,10},{9,11},{10,... | collective-permute-start | bytes 3145736 | tf_op jit(solution)/shard_map/ppermute | solution.py:20
  45.9 25.6 %collective-permute-start.5 = (bf16[64,16,128]{2,1,0:T(8,128)(2,1)}, bf16[64,16,128]{2,1,0:T(8,128)(2,1)S(1)}, u32[]{:S(2)}, u32[]{:S(2)}) collective-permute-start(bf16[64,16,128]{2,1,0:T(8,128)(2,1)} %get-tuple-element.93), channel_id=1, source_target_pairs={{0,4},{4,0},{8,12},{12,8},{16,20},{20,16},{24,28},{28,24},{1,5},{5... | collective-permute-start | bytes 786440 | tf_op jit(solution)/shard_map/ppermute | solution.py:42
  47.8 23.6 %collective-permute-start.6 = (bf16[64,16,128]{2,1,0:T(8,128)(2,1)}, bf16[64,16,128]{2,1,0:T(8,128)(2,1)S(1)}, u32[]{:S(2)}, u32[]{:S(2)}) collective-permute-start(bf16[64,16,128]{2,1,0:T(8,128)(2,1)} %get-tuple-element.94), channel_id=1, source_target_pairs={{0,12},{4,8},{8,20},{12,16},{16,28},{20,24},{24,4},{28,0},{1,13},{... | collective-permute-start | bytes 786440 | tf_op jit(solution)/shard_map/ppermute | solution.py:42
  56.2 20.2 %collective-permute-start.7 = (bf16[64,16,128]{2,1,0:T(8,128)(2,1)}, bf16[64,16,128]{2,1,0:T(8,128)(2,1)S(1)}, u32[]{:S(2)}, u32[]{:S(2)}) collective-permute-start(bf16[64,16,128]{2,1,0:T(8,128)(2,1)} %get-tuple-element.95), channel_id=1, source_target_pairs={{0,20},{4,16},{8,28},{12,24},{16,4},{20,0},{24,12},{28,8},{1,21},{... | collective-permute-start | bytes 786440 | tf_op jit(solution)/shard_map/ppermute | solution.py:42
  58.9 17.5 %collective-permute-start.8 = (bf16[64,16,128]{2,1,0:T(8,128)(2,1)}, bf16[64,16,128]{2,1,0:T(8,128)(2,1)S(1)}, u32[]{:S(2)}, u32[]{:S(2)}) collective-permute-start(bf16[64,16,128]{2,1,0:T(8,128)(2,1)} %get-tuple-element.96), channel_id=1, source_target_pairs={{0,28},{4,24},{8,4},{12,0},{16,12},{20,8},{24,20},{28,16},{1,29},{... | collective-permute-start | bytes 786440 | tf_op jit(solution)/shard_map/ppermute | solution.py:42
  76.4 0.7 copy-start.14
  78.2 15.9 %copy-start.1 = (bf16[4,64,16,128]{3,2,1,0:T(8,128)(2,1)}, bf16[4,64,16,128]{3,2,1,0:T(8,128)(2,1)S(1)}, u32[]{:S(2)}) copy-start(bf16[4,64,16,128]{3,2,1,0:T(8,128)(2,1)S(1)} %pad_maximum_fusion.1.refs_1_) | copy-start | bytes 3145732
  78.2 15.8 %copy-start.2 = (bf16[4,64,16,128]{3,2,1,0:T(8,128)(2,1)}, bf16[4,64,16,128]{3,2,1,0:T(8,128)(2,1)S(1)}, u32[]{:S(2)}) copy-start(bf16[4,64,16,128]{3,2,1,0:T(8,128)(2,1)S(1)} %collective-permute-done.4.refs_4_) | copy-start | bytes 3145732
  78.2 25.2 %collective-permute-start.12 = (bf16[4,64,16,128]{3,2,1,0:T(8,128)(2,1)S(1)}, bf16[4,64,16,128]{3,2,1,0:T(8,128)(2,1)}, u32[]{:S(2)}, u32[]{:S(2)}) collective-permute-start(bf16[4,64,16,128]{3,2,1,0:T(8,128)(2,1)S(1)} %pad_maximum_fusion.1.refs_1_), channel_id=1, source_target_pairs={{0,2},{1,3},{2,0},{3,1},{4,6},{5,7},{6,4},{7,5},{8,10},{9,11},{10,... | collective-permute-start | bytes 3145736 | tf_op jit(solution)/shard_map/ppermute | solution.py:20
  78.8 26.5 %collective-permute-start.11 = (bf16[4,64,16,128]{3,2,1,0:T(8,128)(2,1)S(1)}, bf16[4,64,16,128]{3,2,1,0:T(8,128)(2,1)}, u32[]{:S(2)}, u32[]{:S(2)}) collective-permute-start(bf16[4,64,16,128]{3,2,1,0:T(8,128)(2,1)S(1)} %pad_maximum_fusion.1.refs_1_), channel_id=1, source_target_pairs={{0,1},{1,0},{2,3},{3,2},{4,5},{5,4},{6,7},{7,6},{8,9},{9,8},{10,11... | collective-permute-start | bytes 3145736 | tf_op jit(solution)/shard_map/ppermute | solution.py:20
  78.8 28.2 %all-to-all-start = ((bf16[8,24,16,128]{3,2,1,0:T(8,128)(2,1)}), bf16[8,24,16,128]{3,2,1,0:T(8,128)(2,1)}, u32[]{:S(2)}, u32[]{:S(2)}) async-start(bf16[8,24,16,128]{3,2,1,0:T(8,128)(2,1)} %shard_map.59), calls=%async_computation | async-start | bytes 1572864 | tf_op jit(solution)/shard_map/all_to_all | solution.py:375
  86.1 19.1 %collective-permute-start.9 = (bf16[4,64,16,128]{3,2,1,0:T(8,128)(2,1)S(1)}, bf16[4,64,16,128]{3,2,1,0:T(8,128)(2,1)}, u32[]{:S(2)}, u32[]{:S(2)}) collective-permute-start(bf16[4,64,16,128]{3,2,1,0:T(8,128)(2,1)S(1)} %pad_maximum_fusion.refs_0_), channel_id=1, source_target_pairs={{0,1},{1,0},{2,3},{3,2},{4,5},{5,4},{6,7},{7,6},{8,9},{9,8},{10,11... | collective-permute-start | bytes 3145736 | tf_op jit(solution)/shard_map/ppermute | solution.py:20
  86.4 18.8 %collective-permute-start.10 = (bf16[4,64,16,128]{3,2,1,0:T(8,128)(2,1)S(1)}, bf16[4,64,16,128]{3,2,1,0:T(8,128)(2,1)}, u32[]{:S(2)}, u32[]{:S(2)}) collective-permute-start(bf16[4,64,16,128]{3,2,1,0:T(8,128)(2,1)S(1)} %collective-permute-done.4.refs_4_), channel_id=1, source_target_pairs={{0,1},{1,0},{2,3},{3,2},{4,5},{5,4},{6,7},{7,6},{8,9},{9,8},{10,11... | collective-permute-start | bytes 3145736 | tf_op jit(solution)/shard_map/ppermute | solution.py:20
  107.0 19.1 %collective-permute-start.15 = (bf16[8,24,16,128]{3,2,1,0:T(8,128)(2,1)}, bf16[8,24,16,128]{3,2,1,0:T(8,128)(2,1)S(1)}, u32[]{:S(2)}, u32[]{:S(2)}) collective-permute-start(bf16[8,24,16,128]{3,2,1,0:T(8,128)(2,1)} %all-to-all-done.refs_8_), channel_id=1, source_target_pairs={{0,2},{1,3},{2,0},{3,1},{4,6},{5,7},{6,4},{7,5},{8,10},{9,11},{10,... | collective-permute-start | bytes 2359304 | tf_op jit(solution)/shard_map/ppermute | solution.py:20
  108.5 19.7 %collective-permute-start.14 = (bf16[8,24,16,128]{3,2,1,0:T(8,128)(2,1)}, bf16[8,24,16,128]{3,2,1,0:T(8,128)(2,1)}, u32[]{:S(2)}, u32[]{:S(2)}) collective-permute-start(bf16[8,24,16,128]{3,2,1,0:T(8,128)(2,1)} %all-to-all-done.refs_8_), channel_id=1, source_target_pairs={{0,1},{1,0},{2,3},{3,2},{4,5},{5,4},{6,7},{7,6},{8,9},{9,8},{10,11... | collective-permute-start | bytes 2359304 | tf_op jit(solution)/shard_map/ppermute | solution.py:20
  108.5 22.8 %all-to-all-start.1 = ((bf16[8,20,16,128]{3,2,1,0:T(8,128)(2,1)}), bf16[8,20,16,128]{3,2,1,0:T(8,128)(2,1)S(1)}, u32[]{:S(2)}, u32[]{:S(2)}) async-start(bf16[8,20,16,128]{3,2,1,0:T(8,128)(2,1)} %get-tuple-element.107), calls=%async_computation.1 | async-start | bytes 1310720 | tf_op jit(solution)/shard_map/all_to_all | solution.py:375
  113.3 15.0 %collective-permute-start.13 = (bf16[4,64,16,128]{3,2,1,0:T(8,128)(2,1)}, bf16[4,64,16,128]{3,2,1,0:T(8,128)(2,1)S(1)}, u32[]{:S(2)}, u32[]{:S(2)}) collective-permute-start(bf16[4,64,16,128]{3,2,1,0:T(8,128)(2,1)} %collective-permute-done.12.refs_0_.refs_5_), channel_id=1, source_target_pairs={{0,1},{1,0},{2,3},{3,2},{4,5},{5,4},{6,7},{7,6},{8,9},{9,8},{10,11... | collective-permute-start | bytes 3145736 | tf_op jit(solution)/shard_map/ppermute | solution.py:20
  126.1 0.9 copy-start.7
  128.3 8.5 %copy-start.3 = (bf16[4,64,16,128]{3,2,1,0:T(8,128)(2,1)}, bf16[4,64,16,128]{3,2,1,0:T(8,128)(2,1)S(1)}, u32[]{:S(2)}) copy-start(bf16[4,64,16,128]{3,2,1,0:T(8,128)(2,1)S(1)} %collective-permute-done.13.refs_7_) | copy-start | bytes 3145732
  131.3 18.5 %copy-start.5 = (bf16[8,20,16,128]{3,2,1,0:T(8,128)(2,1)}, bf16[8,20,16,128]{3,2,1,0:T(8,128)(2,1)S(1)}, u32[]{:S(2)}) copy-start(bf16[8,20,16,128]{3,2,1,0:T(8,128)(2,1)S(1)} %all-to-all-done.1.refs_8_) | copy-start | bytes 1966084
  131.3 5.5 %collective-permute-start.16 = (bf16[8,24,16,128]{3,2,1,0:T(8,128)(2,1)}, bf16[8,24,16,128]{3,2,1,0:T(8,128)(2,1)S(1)}, u32[]{:S(2)}, u32[]{:S(2)}) collective-permute-start(bf16[8,24,16,128]{3,2,1,0:T(8,128)(2,1)} %copy-done.7), channel_id=1, source_target_pairs={{0,1},{1,0},{2,3},{3,2},{4,5},{5,4},{6,7},{7,6},{8,9},{9,8},{10,11... | collective-permute-start | bytes 2359304 | tf_op jit(solution)/shard_map/ppermute | solution.py:20
  131.3 18.5 %collective-permute-start.18 = (bf16[8,20,16,128]{3,2,1,0:T(8,128)(2,1)S(1)}, bf16[8,20,16,128]{3,2,1,0:T(8,128)(2,1)}, u32[]{:S(2)}, u32[]{:S(2)}) collective-permute-start(bf16[8,20,16,128]{3,2,1,0:T(8,128)(2,1)S(1)} %all-to-all-done.1.refs_8_), channel_id=1, source_target_pairs={{0,2},{1,3},{2,0},{3,1},{4,6},{5,7},{6,4},{7,5},{8,10},{9,11},{10,... | collective-permute-start | bytes 1966088 | tf_op jit(solution)/shard_map/ppermute | solution.py:20
  132.8 18.3 %collective-permute-start.17 = (bf16[8,20,16,128]{3,2,1,0:T(8,128)(2,1)S(1)}, bf16[8,20,16,128]{3,2,1,0:T(8,128)(2,1)}, u32[]{:S(2)}, u32[]{:S(2)}) collective-permute-start(bf16[8,20,16,128]{3,2,1,0:T(8,128)(2,1)S(1)} %all-to-all-done.1.refs_8_), channel_id=1, source_target_pairs={{0,1},{1,0},{2,3},{3,2},{4,5},{5,4},{6,7},{7,6},{8,9},{9,8},{10,11... | collective-permute-start | bytes 1966088 | tf_op jit(solution)/shard_map/ppermute | solution.py:20
  133.1 21.5 %all-to-all-start.2 = ((bf16[8,20,16,128]{3,2,1,0:T(8,128)(2,1)}), bf16[8,20,16,128]{3,2,1,0:T(8,128)(2,1)S(1)}, u32[]{:S(2)}, u32[]{:S(2)}) async-start(bf16[8,20,16,128]{3,2,1,0:T(8,128)(2,1)} %get-tuple-element.118), calls=%async_computation.2 | async-start | bytes 1310720 | tf_op jit(solution)/shard_map/all_to_all | solution.py:375
  136.8 0.9 copy-start.8
  154.5 13.6 %copy-start.6 = (bf16[8,20,16,128]{3,2,1,0:T(8,128)(2,1)}, bf16[8,20,16,128]{3,2,1,0:T(8,128)(2,1)S(1)}, u32[]{:S(2)}) copy-start(bf16[8,20,16,128]{3,2,1,0:T(8,128)(2,1)S(1)} %all-to-all-done.2.refs_8_) | copy-start | bytes 1966084
  154.5 2.3 %collective-permute-start.19 = (bf16[8,20,16,128]{3,2,1,0:T(8,128)(2,1)}, bf16[8,20,16,128]{3,2,1,0:T(8,128)(2,1)S(1)}, u32[]{:S(2)}, u32[]{:S(2)}) collective-permute-start(bf16[8,20,16,128]{3,2,1,0:T(8,128)(2,1)} %collective-permute-done.18.refs_0_.refs_10_), channel_id=1, source_target_pairs={{0,1},{1,0},{2,3},{3,2},{4,5},{5,4},{6,7},{7,6},{8,9},{9,8},{10,11... | collective-permute-start | bytes 1966088 | tf_op jit(solution)/shard_map/ppermute | solution.py:20
  154.6 17.1 %collective-permute-start.21 = (bf16[8,20,16,128]{3,2,1,0:T(8,128)(2,1)S(1)}, bf16[8,20,16,128]{3,2,1,0:T(8,128)(2,1)S(1)}, u32[]{:S(2)}, u32[]{:S(2)}) collective-permute-start(bf16[8,20,16,128]{3,2,1,0:T(8,128)(2,1)S(1)} %all-to-all-done.2.refs_8_), channel_id=1, source_target_pairs={{0,2},{1,3},{2,0},{3,1},{4,6},{5,7},{6,4},{7,5},{8,10},{9,11},{10,... | collective-permute-start | bytes 1966088 | tf_op jit(solution)/shard_map/ppermute | solution.py:20
  155.1 16.6 %collective-permute-start.20 = (bf16[8,20,16,128]{3,2,1,0:T(8,128)(2,1)S(1)}, bf16[8,20,16,128]{3,2,1,0:T(8,128)(2,1)S(1)}, u32[]{:S(2)}, u32[]{:S(2)}) collective-permute-start(bf16[8,20,16,128]{3,2,1,0:T(8,128)(2,1)S(1)} %all-to-all-done.2.refs_8_), channel_id=1, source_target_pairs={{0,1},{1,0},{2,3},{3,2},{4,5},{5,4},{6,7},{7,6},{8,9},{9,8},{10,11... | collective-permute-start | bytes 1966088 | tf_op jit(solution)/shard_map/ppermute | solution.py:20
  156.9 0.8 copy-start.12
  171.7 2.2 %copy-start.9 = (bf16[8,20,16,128]{3,2,1,0:T(8,128)(2,1)}, bf16[8,20,16,128]{3,2,1,0:T(8,128)(2,1)S(1)}, u32[]{:S(2)}) copy-start(bf16[8,20,16,128]{3,2,1,0:T(8,128)(2,1)S(1)} %collective-permute-done.21.refs_10_) | copy-start | bytes 1966084
  171.7 2.2 %copy-start.10 = (bf16[8,20,16,128]{3,2,1,0:T(8,128)(2,1)}, bf16[8,20,16,128]{3,2,1,0:T(8,128)(2,1)S(1)}, u32[]{:S(2)}) copy-start(bf16[8,20,16,128]{3,2,1,0:T(8,128)(2,1)S(1)} %collective-permute-done.20.refs_9_) | copy-start | bytes 1966084
  171.7 2.2 %collective-permute-start.22 = (bf16[8,20,16,128]{3,2,1,0:T(8,128)(2,1)S(1)}, bf16[8,20,16,128]{3,2,1,0:T(8,128)(2,1)S(1)}, u32[]{:S(2)}, u32[]{:S(2)}) collective-permute-start(bf16[8,20,16,128]{3,2,1,0:T(8,128)(2,1)S(1)} %collective-permute-done.21.refs_10_), channel_id=1, source_target_pairs={{0,1},{1,0},{2,3},{3,2},{4,5},{5,4},{6,7},{7,6},{8,9},{9,8},{10,11... | collective-permute-start | bytes 1966088 | tf_op jit(solution)/shard_map/ppermute | solution.py:20
  173.9 0.8 copy-start.11

commit v4 on v3

--- a/solution.py
+++ b/solution.py
@@ -9,7 +9,7 @@
 from jax.experimental.pallas import tpu as pltpu
 from jax.sharding import PartitionSpec as P
 
-EARLY = (6, 5, 5)
+EARLY = (7, 5, 4)
 MIB = 1 << 20
 VMEM = 60 * MIB
 RATED = 10**11
@@ -134,7 +134,7 @@
         cost_estimate=pl.CostEstimate(
             flops=count * inputs * channels * 16, bytes_accessed=2 * inputs * samples * 4, transcendentals=0
         ),
-        compiler_params=pltpu.CompilerParams(vmem_limit_bytes=VMEM),
+        compiler_params=pltpu.CompilerParams(vmem_limit_bytes=VMEM if passed is None else 32 * MIB),
     )(*operands)
 
 
@@ -222,7 +222,7 @@
             bytes_accessed=groups * rows * depth * 2 + weighted.size * 4,
             transcendentals=0,
         ),
-        compiler_params=pltpu.CompilerParams(vmem_limit_bytes=VMEM),
+        compiler_params=pltpu.CompilerParams(vmem_limit_bytes=32 * MIB),
     )(weighted, table)
 
 
@@ -324,7 +324,7 @@
         cost_estimate=pl.CostEstimate(
             flops=2 * 2 * pairs * 2 * inputs * wide * depth, bytes_accessed=2 * pairs * 2 * inputs * wide * 4, transcendentals=0
         ),
-        compiler_params=pltpu.CompilerParams(vmem_limit_bytes=VMEM),
+        compiler_params=pltpu.CompilerParams(vmem_limit_bytes=36 * MIB),
     )(*operands)
 
 
@@ -383,7 +383,7 @@
         if step >= 2:
             parts = [held[0], held[1], {**held[step], 3: new[step, 3]}]
             visible = correlated(blk.reshape(1), parts, (0, 1, 2, 3), ends[step - 2], shape, factor, ntaps, visible, token)
-        if step < nearly:
+        if step < nearly - 1:
             token = tick(token, new[step + 1, 2], *([] if visible is None else [visible]))
         if step == nearly + 1:
             break

time: 186 us -> 181 us (0.973)
  Pallas kernels: 75.2 us -> 62.7 us
  local copies, waits for them, and re-layouts: 5.93 us -> 14.1 us
    unnamed x30 -> x32, local copies, waits for them, and re-layouts: 5.33 us -> 13.5 us
    pallas_call x2, Pallas kernels: 12.8 us -> 7.46 us  [spectra_by(): pl.pallas_call(functools.partial(transform_by, ends), out_shape=[jax.Shap...]
    pallas_call x2, Pallas kernels: 11.6 us -> 7.25 us  [weighted_spectra(): pl.pallas_call(weigh_late if passed is None else weigh_early, out_shape=j...]
    all_to_all x3, waiting for transfers between devices: 8.23 us -> 5.89 us  [local(): lax.all_to_all(early[step], 'freq', split_axis=0, concat_axis=0, tiled=True)]
    pallas_call x3 -> x2, Pallas kernels: 3.83 us -> 2.5 us  [tick(): pl.pallas_call(body, out_shape=jax.ShapeDtypeStruct(token.shape, token.dt...]
  transfers between devices with their start and end apart: 26 -> 26, of which waited for: 10 -> 11; matrix products, arithmetic and copies ran while one was open for 1% -> 0% of each run, Pallas kernels for 35% -> 30%
where the time goes in v4:
time: 181 us; the launch traced here: 180 us
  Pallas kernels  62.7 us (35%)
  waiting for transfers between devices  52.1 us (29%)
  starting transfers between devices  47.1 us (26%)
  local copies, waits for them, and re-layouts  14.1 us (8%)
  other arithmetic  3.64 us (2%)
    pallas_call x3, Pallas kernels, correlated(): pl.pallas_call(functools.partial(correlate, factor, distances, len(late),...  31.6 us
    ppermute x15, waiting for transfers between devices, swapped(): return lax.ppermute(value, axis, pairs)  28.8 us
    ppermute x7, starting transfers between devices, shifted(): return lax.ppermute(value, 'freq', pairs)  18.8 us
    ppermute x7, waiting for transfers between devices, shifted(): return lax.ppermute(value, 'freq', pairs)  17.2 us
    all_to_all x3, starting transfers between devices, local(): lax.all_to_all(early[step], 'freq', split_axis=0, concat_axis=0, tiled=True)  15.9 us
    pallas_call x2, Pallas kernels, spectra_to(): pl.pallas_call(transform_to, out_shape=[jax.ShapeDtypeStruct(shape, jnp.b...  13.9 us
    unnamed x32, local copies, waits for them, and re-layouts  13.5 us
    pallas_call x2, Pallas kernels, spectra_by(): pl.pallas_call(functools.partial(transform_by, ends), out_shape=[jax.Shap...  7.46 us
  transfers between devices with their start and end apart: 26, of which 11 were waited for; matrix products, arithmetic and copies ran while one was open for 0% of the time, Pallas kernels for 30%

profile of v4, /device:TPU:0, one launch (start us, length us, event | category | flops | bytes accessed | tf_op | source)
XLA Modules:
  0.0 179.7 jit_solution(6794559660293004230)
XLA Ops:
  0.0 3.3 %dynamic-slice_convert_fusion = bf16[2,128,3072]{2,1,0:T(8,128)(2,1)} fusion(s32[2,128,8192]{2,1,0:T(8,128)} %imag_ref.3, s32[]{:T(128)S(6)} %select_n.16), kind=kLoop, calls=%fused_computation | loop fusion | flops 786432 | bytes 4718596 | tf_op jit(solution)/shard_map/convert_element_type | solution.py:351
  3.3 4.9 %collective-permute-start.3 = (bf16[2,128,3072]{2,1,0:T(8,128)(2,1)}, bf16[2,128,3072]{2,1,0:T(8,128)(2,1)S(1)}, u32[]{:S(2)}, u32[]{:S(2)}) collective-permute-start(bf16[2,128,3072]{2,1,0:T(8,128)(2,1)} %dynamic-slice_convert_fusion), channel_id=1, source_target_pairs={{0,4},{1,29},{2,6},{3,31},{4,8},{5,1},{6,10},{7,3},{8,12},{9,5},{1... | collective-permute-start | bytes 4718600 | tf_op jit(solution)/shard_map/ppermute | solution.py:32
  8.2 5.2 %shard_map.55.weighted_ref = bf16[4,128,2048]{2,1,0:T(8,128)(2,1)} custom-call(s32[4,1024]{1,0:T(4,128)} %taps_ref.3, s32[2,128,8192]{2,1,0:T(8,128)} %imag_ref.3, s32[2,128,8192]{2,1,0:T(8,128)} %imag_ref.3), custom_call_target="tpu_custom_call" | custom-call | flops 8388608 | bytes 8388608 | tf_op jit(solution)/shard_map/pallas_call | solution.py:125
  13.4 6.9 %shard_map.56 = (bf16[64,16,128]{2,1,0:T(8,128)(2,1)}, bf16[64,16,128]{2,1,0:T(8,128)(2,1)}, bf16[64,16,128]{2,1,0:T(8,128)(2,1)}, bf16[64,16,128]{2,1,0:T(8,128)(2,1)}) custom-call(s32[1]{0:T(128)} %bitcast.1.me_ref, bf16[4,128,2048]{2,1,0:T(8,128)(2,1)} %shard_map.55.weighted_ref, bf16[8,256,1024]{2,1,0:T(8,128)(2,1)} %constant.39.clone.table_ref), custom_call_target="tpu_custom_call" | custom-call | flops 2147483648 | bytes 5242880 | tf_op jit(solution)/shard_map/pallas_call | solution.py:175
  20.3 1.5 collective-permute-start
  21.8 2.6 %collective-permute-start.1 = (bf16[64,16,128]{2,1,0:T(8,128)(2,1)}, bf16[64,16,128]{2,1,0:T(8,128)(2,1)S(1)}, u32[]{:S(2)}, u32[]{:S(2)}) collective-permute-start(bf16[64,16,128]{2,1,0:T(8,128)(2,1)} %get-tuple-element.83), channel_id=1, source_target_pairs={{0,16},{4,20},{8,24},{12,28},{16,0},{20,4},{24,8},{28,12},{1,17},{... | collective-permute-start | bytes 786440 | tf_op jit(solution)/shard_map/ppermute | solution.py:42
  24.4 1.3 collective-permute-start.2
  25.8 6.9 %shard_map.57 = (bf16[64,16,128]{2,1,0:T(8,128)(2,1)}, bf16[64,16,128]{2,1,0:T(8,128)(2,1)}, bf16[64,16,128]{2,1,0:T(8,128)(2,1)}, bf16[64,16,128]{2,1,0:T(8,128)(2,1)}) custom-call(s32[1]{0:T(128)} %bitcast.1.me_ref, bf16[4,128,2048]{2,1,0:T(8,128)(2,1)} %shard_map.55.weighted_ref, bf16[8,256,1024]{2,1,0:T(8,128)(2,1)} %constant.39.clone.table_ref), custom_call_target="tpu_custom_call" | custom-call | flops 2147483648 | bytes 5242880 | tf_op jit(solution)/shard_map/pallas_call | solution.py:175
  32.7 10.1 %collective-permute-done.1 = bf16[64,16,128]{2,1,0:T(8,128)(2,1)S(1)} collective-permute-done((bf16[64,16,128]{2,1,0:T(8,128)(2,1)}, bf16[64,16,128]{2,1,0:T(8,128)(2,1)S(1)}, u32[]{:S(2)}, u32[]{:S(2)}) %collective-permute-start.1) | collective-permute-done | bytes 262176 | tf_op jit(solution)/shard_map/ppermute | solution.py:42
  43.0 1.1 copy-done.1
  44.3 1.6 collective-permute-start.4
  45.9 2.4 %collective-permute-start.5 = (bf16[64,16,128]{2,1,0:T(8,128)(2,1)}, bf16[64,16,128]{2,1,0:T(8,128)(2,1)S(1)}, u32[]{:S(2)}, u32[]{:S(2)}) collective-permute-start(bf16[64,16,128]{2,1,0:T(8,128)(2,1)} %get-tuple-element.93), channel_id=1, source_target_pairs={{0,4},{4,0},{8,12},{12,8},{16,20},{20,16},{24,28},{28,24},{1,5},{5... | collective-permute-start | bytes 786440 | tf_op jit(solution)/shard_map/ppermute | solution.py:42
  48.2 8.3 %collective-permute-start.6 = (bf16[64,16,128]{2,1,0:T(8,128)(2,1)}, bf16[64,16,128]{2,1,0:T(8,128)(2,1)S(1)}, u32[]{:S(2)}, u32[]{:S(2)}) collective-permute-start(bf16[64,16,128]{2,1,0:T(8,128)(2,1)} %get-tuple-element.94), channel_id=1, source_target_pairs={{0,12},{4,8},{8,20},{12,16},{16,28},{20,24},{24,4},{28,0},{1,13},{... | collective-permute-start | bytes 786440 | tf_op jit(solution)/shard_map/ppermute | solution.py:42
  56.5 2.7 %collective-permute-start.7 = (bf16[64,16,128]{2,1,0:T(8,128)(2,1)}, bf16[64,16,128]{2,1,0:T(8,128)(2,1)S(1)}, u32[]{:S(2)}, u32[]{:S(2)}) collective-permute-start(bf16[64,16,128]{2,1,0:T(8,128)(2,1)} %get-tuple-element.95), channel_id=1, source_target_pairs={{0,20},{4,16},{8,28},{12,24},{16,4},{20,0},{24,12},{28,8},{1,21},{... | collective-permute-start | bytes 786440 | tf_op jit(solution)/shard_map/ppermute | solution.py:42
  59.3 3.4 %copy-done = s32[2,128,8192]{2,1,0:T(8,128)S(1)} copy-done((s32[2,128,8192]{2,1,0:T(8,128)S(1)}, s32[2,128,8192]{2,1,0:T(8,128)}, u32[]{:S(2)}) %copy-start) | copy-done | bytes 8388632
  62.7 1.4 copy-done.2
  64.1 2.1 %shard_map.58.weighted_ref = bf16[4,128,2048]{2,1,0:T(8,128)(2,1)S(1)} custom-call(s32[2]{0:T(128)S(1)} %pad_add_fusion.where_ref, s32[4,1024]{1,0:T(4,128)S(1)} %copy-done.10, s32[2,128,8192]{2,1,0:T(8,128)S(1)} %copy-done, s32[2,128,8192]{2,1,0:T(8,128)S(1)} %copy-done, bf16[2,128,3072]{2,1,0:T(8,128)(2,1)S(1)} %copy-done.2, ...), custom_call_target="tpu_custom_call" | custom-call | flops 8388608 | bytes 8388608 | tf_op jit(solution)/shard_map/pallas_call | solution.py:125
  66.3 3.3 %shard_map.59 = bf16[8,28,16,128]{3,2,1,0:T(8,128)(2,1)S(1)} custom-call(bf16[4,128,2048]{2,1,0:T(8,128)(2,1)S(1)} %shard_map.58.weighted_ref, bf16[8,112,1024]{2,1,0:T(8,128)(2,1)S(1)} %copy-done.14), custom_call_target="tpu_custom_call" | custom-call | flops 1879048192 | bytes 6029312 | tf_op jit(solution)/shard_map/pallas_call | solution.py:210
  69.6 7.1 %collective-permute-done.7 = bf16[64,16,128]{2,1,0:T(8,128)(2,1)S(1)} collective-permute-done((bf16[64,16,128]{2,1,0:T(8,128)(2,1)}, bf16[64,16,128]{2,1,0:T(8,128)(2,1)S(1)}, u32[]{:S(2)}, u32[]{:S(2)}) %collective-permute-start.7) | collective-permute-done | bytes 262176 | tf_op jit(solution)/shard_map/ppermute | solution.py:42
  76.9 0.6 collective-permute-start.12
  78.0 7.4 %all-to-all-start = ((bf16[8,28,16,128]{3,2,1,0:T(8,128)(2,1)}), bf16[8,28,16,128]{3,2,1,0:T(8,128)(2,1)}, u32[]{:S(2)}, u32[]{:S(2)}) async-start(bf16[8,28,16,128]{3,2,1,0:T(8,128)(2,1)} %copy-done.5), calls=%async_computation | async-start | bytes 1835008 | tf_op jit(solution)/shard_map/all_to_all | solution.py:375
  85.4 1.6 copy-done.4
  87.0 1.7 copy-done.13
  88.6 4.1 %shard_map.60 = (bf16[8,20,16,128]{3,2,1,0:T(8,128)(2,1)S(1)}, bf16[8,16,16,128]{3,2,1,0:T(8,128)(2,1)S(1)}) custom-call(bf16[4,128,2048]{2,1,0:T(8,128)(2,1)S(1)} %copy-done.4, bf16[8,144,1024]{2,1,0:T(8,128)(2,1)S(1)} %copy-done.13), custom_call_target="tpu_custom_call" | custom-call | flops 2415919104 | bytes 6553600 | tf_op jit(solution)/shard_map/pallas_call | solution.py:210
  92.8 0.8 copy-done.8
  93.6 0.8 copy-done.9
  94.4 7.7 %collective-permute-done.12.refs_0_.refs_5_ = bf16[4,64,16,128]{3,2,1,0:T(8,128)(2,1)} collective-permute-done((bf16[4,64,16,128]{3,2,1,0:T(8,128)(2,1)S(1)}, bf16[4,64,16,128]{3,2,1,0:T(8,128)(2,1)}, u32[]{:S(2)}, u32[]{:S(2)}) %collective-permute-start.12) | collective-permute-done | bytes 1048608 | tf_op jit(solution)/shard_map/ppermute | solution.py:20
  102.1 0.6 broadcast_in_dim.3.token_ref
  102.7 1.3 shard_map.61.token_ref
  103.9 5.1 %all-to-all-done.refs_8_ = bf16[8,28,16,128]{3,2,1,0:T(8,128)(2,1)} async-done(((bf16[8,28,16,128]{3,2,1,0:T(8,128)(2,1)}), bf16[8,28,16,128]{3,2,1,0:T(8,128)(2,1)}, u32[]{:S(2)}, u32[]{:S(2)}) %all-to-all-start) | async-done | bytes 917536 | tf_op jit(solution)/shard_map/all_to_all | solution.py:375
  109.1 1.5 collective-permute-start.15
  111.1 4.2 %all-to-all-start.1 = ((bf16[8,20,16,128]{3,2,1,0:T(8,128)(2,1)}), bf16[8,20,16,128]{3,2,1,0:T(8,128)(2,1)}, u32[]{:S(2)}, u32[]{:S(2)}) async-start(bf16[8,20,16,128]{3,2,1,0:T(8,128)(2,1)} %copy-done.8), calls=%async_computation.1 | async-start | bytes 1310720 | tf_op jit(solution)/shard_map/all_to_all | solution.py:375
  115.3 15.7 %collective-permute-done.15.refs_0_.refs_10_ = bf16[8,28,16,128]{3,2,1,0:T(8,128)(2,1)} collective-permute-done((bf16[8,28,16,128]{3,2,1,0:T(8,128)(2,1)}, bf16[8,28,16,128]{3,2,1,0:T(8,128)(2,1)}, u32[]{:S(2)}, u32[]{:S(2)}) %collective-permute-start.15) | collective-permute-done | bytes 917536 | tf_op jit(solution)/shard_map/ppermute | solution.py:20
  131.0 1.2 shard_map.62.refs_12_.refs_13_
  132.3 0.8 all-to-all-done.1.refs_8_
  133.1 4.3 %all-to-all-start.2 = ((bf16[8,16,16,128]{3,2,1,0:T(8,128)(2,1)}), bf16[8,16,16,128]{3,2,1,0:T(8,128)(2,1)}, u32[]{:S(2)}, u32[]{:S(2)}) async-start(bf16[8,16,16,128]{3,2,1,0:T(8,128)(2,1)} %copy-done.9), calls=%async_computation.2 | async-start | bytes 1048576 | tf_op jit(solution)/shard_map/all_to_all | solution.py:375
  138.0 0.8 collective-permute-start.18
  138.8 0.7 copy-done.11
  139.5 13.5 %shard_map.63.refs_12_ = f32[2,128,128,512]{3,2,1,0:T(8,128)} custom-call(s32[1]{0:T(128)} %bitcast.me_ref, bf16[4,64,16,128]{3,2,1,0:T(8,128)(2,1)S(1)} %pad_maximum_fusion.refs_0_, bf16[4,64,16,128]{3,2,1,0:T(8,128)(2,1)S(1)} %pad_maximum_fusion.1.refs_1_, bf16[4,64,16,128]{3,2,1,0:T(8,128)(2,1)} %collective-permute-done.9.refs_2_, ...), custom_call_target="tpu_custom_call" | custom-call | flops 1879048192 | bytes 29360128 | tf_op jit(solution)/shard_map/pallas_call | solution.py:312
  153.0 0.8 copy-done.6
  153.9 1.1 collective-permute-done.18.refs_10_
  155.5 0.8 collective-permute-start.21
  156.3 1.0 collective-permute-done.19.refs_11_
  157.3 1.1 copy-done.7
  158.4 9.8 %shard_map.64.refs_12_ = f32[2,128,128,512]{3,2,1,0:T(8,128)} custom-call(s32[1]{0:T(128)} %bitcast.me_ref, bf16[4,64,16,128]{3,2,1,0:T(8,128)(2,1)S(1)} %pad_maximum_fusion.refs_0_, bf16[4,64,16,128]{3,2,1,0:T(8,128)(2,1)S(1)} %pad_maximum_fusion.1.refs_1_, ...), custom_call_target="tpu_custom_call", output_to_operand_aliasing={{}: (13, {})} | custom-call | flops 1342177280 | bytes 20971520 | tf_op jit(solution)/shard_map/pallas_call | solution.py:312
  168.2 1.4 collective-permute-done.21.refs_10_
  169.6 1.9 %collective-permute-done.22.refs_11_ = bf16[8,16,16,128]{3,2,1,0:T(8,128)(2,1)S(1)} collective-permute-done((bf16[8,16,16,128]{3,2,1,0:T(8,128)(2,1)S(1)}, bf16[8,16,16,128]{3,2,1,0:T(8,128)(2,1)S(1)}, u32[]{:S(2)}, u32[]{:S(2)}) %collective-permute-start.22) | collective-permute-done | bytes 524320 | tf_op jit(solution)/shard_map/ppermute | solution.py:20
  171.5 8.3 %shard_map.65 = f32[2,128,128,512]{3,2,1,0:T(8,128)} custom-call(s32[1]{0:T(128)} %bitcast.me_ref, bf16[4,64,16,128]{3,2,1,0:T(8,128)(2,1)S(1)} %pad_maximum_fusion.refs_0_, bf16[4,64,16,128]{3,2,1,0:T(8,128)(2,1)S(1)} %pad_maximum_fusion.1.refs_1_, bf16[4,64,16,128]{3,2,1,0:T(8,128)(2,1)} %collective-permute-done.9.refs_2_, ...), custom_call_target="tpu_custom_call", output_to_operand_aliasing={{}: (13, {})} | custom-call | flops 1073741824 | bytes 16777216 | tf_op jit(solution)/shard_map/pallas_call | solution.py:312
  (52 shorter events, 2.8 us)
Async XLA Ops:
  3.3 39.7 %collective-permute-start.3 = (bf16[2,128,3072]{2,1,0:T(8,128)(2,1)}, bf16[2,128,3072]{2,1,0:T(8,128)(2,1)S(1)}, u32[]{:S(2)}, u32[]{:S(2)}) collective-permute-start(bf16[2,128,3072]{2,1,0:T(8,128)(2,1)} %dynamic-slice_convert_fusion), channel_id=1, source_target_pairs={{0,4},{1,29},{2,6},{3,31},{4,8},{5,1},{6,10},{7,3},{8,12},{9,5},{1... | collective-permute-start | bytes 4718600 | tf_op jit(solution)/shard_map/ppermute | solution.py:32
  20.3 12.4 %collective-permute-start = (bf16[64,16,128]{2,1,0:T(8,128)(2,1)}, bf16[64,16,128]{2,1,0:T(8,128)(2,1)S(1)}, u32[]{:S(2)}, u32[]{:S(2)}) collective-permute-start(bf16[64,16,128]{2,1,0:T(8,128)(2,1)} %get-tuple-element.82), channel_id=1, source_target_pairs={{0,8},{4,12},{8,16},{12,20},{16,24},{20,28},{24,0},{28,4},{1,9},{5... | collective-permute-start | bytes 786440 | tf_op jit(solution)/shard_map/ppermute | solution.py:42
  21.8 20.9 %collective-permute-start.1 = (bf16[64,16,128]{2,1,0:T(8,128)(2,1)}, bf16[64,16,128]{2,1,0:T(8,128)(2,1)S(1)}, u32[]{:S(2)}, u32[]{:S(2)}) collective-permute-start(bf16[64,16,128]{2,1,0:T(8,128)(2,1)} %get-tuple-element.83), channel_id=1, source_target_pairs={{0,16},{4,20},{8,24},{12,28},{16,0},{20,4},{24,8},{28,12},{1,17},{... | collective-permute-start | bytes 786440 | tf_op jit(solution)/shard_map/ppermute | solution.py:42
  24.4 19.7 %copy-start.15 = (bf16[64,16,128]{2,1,0:T(8,128)(2,1)S(1)}, bf16[64,16,128]{2,1,0:T(8,128)(2,1)}, u32[]{:S(2)}) copy-start(bf16[64,16,128]{2,1,0:T(8,128)(2,1)} %get-tuple-element.89) | copy-start | bytes 786436
  24.4 34.9 %copy-start.10 = (s32[4,1024]{1,0:T(4,128)S(1)}, s32[4,1024]{1,0:T(4,128)}, u32[]{:S(2)}) copy-start(s32[4,1024]{1,0:T(4,128)} %taps_ref.3) | copy-start | bytes 49156
  24.4 18.3 %collective-permute-start.2 = (bf16[64,16,128]{2,1,0:T(8,128)(2,1)}, bf16[64,16,128]{2,1,0:T(8,128)(2,1)S(1)}, u32[]{:S(2)}, u32[]{:S(2)}) collective-permute-start(bf16[64,16,128]{2,1,0:T(8,128)(2,1)} %get-tuple-element.84), channel_id=1, source_target_pairs={{0,24},{4,28},{8,0},{12,4},{16,8},{20,12},{24,16},{28,20},{1,25},{... | collective-permute-start | bytes 786440 | tf_op jit(solution)/shard_map/ppermute | solution.py:42
  43.0 1.1 copy-start.1
  44.3 32.6 %collective-permute-start.4 = (bf16[4,64,16,128]{3,2,1,0:T(8,128)(2,1)S(1)}, bf16[4,64,16,128]{3,2,1,0:T(8,128)(2,1)S(1)}, u32[]{:S(2)}, u32[]{:S(2)}) collective-permute-start(bf16[4,64,16,128]{3,2,1,0:T(8,128)(2,1)S(1)} %pad_maximum_fusion.refs_0_), channel_id=1, source_target_pairs={{0,2},{1,3},{2,0},{3,1},{4,6},{5,7},{6,4},{7,5},{8,10},{9,11},{10,... | collective-permute-start | bytes 3145736 | tf_op jit(solution)/shard_map/ppermute | solution.py:20
  45.9 23.8 %collective-permute-start.5 = (bf16[64,16,128]{2,1,0:T(8,128)(2,1)}, bf16[64,16,128]{2,1,0:T(8,128)(2,1)S(1)}, u32[]{:S(2)}, u32[]{:S(2)}) collective-permute-start(bf16[64,16,128]{2,1,0:T(8,128)(2,1)} %get-tuple-element.93), channel_id=1, source_target_pairs={{0,4},{4,0},{8,12},{12,8},{16,20},{20,16},{24,28},{28,24},{1,5},{5... | collective-permute-start | bytes 786440 | tf_op jit(solution)/shard_map/ppermute | solution.py:42
  48.2 21.4 %collective-permute-start.6 = (bf16[64,16,128]{2,1,0:T(8,128)(2,1)}, bf16[64,16,128]{2,1,0:T(8,128)(2,1)S(1)}, u32[]{:S(2)}, u32[]{:S(2)}) collective-permute-start(bf16[64,16,128]{2,1,0:T(8,128)(2,1)} %get-tuple-element.94), channel_id=1, source_target_pairs={{0,12},{4,8},{8,20},{12,16},{16,28},{20,24},{24,4},{28,0},{1,13},{... | collective-permute-start | bytes 786440 | tf_op jit(solution)/shard_map/ppermute | solution.py:42
  56.5 20.2 %collective-permute-start.7 = (bf16[64,16,128]{2,1,0:T(8,128)(2,1)}, bf16[64,16,128]{2,1,0:T(8,128)(2,1)S(1)}, u32[]{:S(2)}, u32[]{:S(2)}) collective-permute-start(bf16[64,16,128]{2,1,0:T(8,128)(2,1)} %get-tuple-element.95), channel_id=1, source_target_pairs={{0,20},{4,16},{8,28},{12,24},{16,4},{20,0},{24,12},{28,8},{1,21},{... | collective-permute-start | bytes 786440 | tf_op jit(solution)/shard_map/ppermute | solution.py:42
  59.3 17.5 %collective-permute-start.8 = (bf16[64,16,128]{2,1,0:T(8,128)(2,1)}, bf16[64,16,128]{2,1,0:T(8,128)(2,1)S(1)}, u32[]{:S(2)}, u32[]{:S(2)}) collective-permute-start(bf16[64,16,128]{2,1,0:T(8,128)(2,1)} %get-tuple-element.96), channel_id=1, source_target_pairs={{0,28},{4,24},{8,4},{12,0},{16,12},{20,8},{24,20},{28,16},{1,29},{... | collective-permute-start | bytes 786440 | tf_op jit(solution)/shard_map/ppermute | solution.py:42
  59.3 3.4 %copy-start = (s32[2,128,8192]{2,1,0:T(8,128)S(1)}, s32[2,128,8192]{2,1,0:T(8,128)}, u32[]{:S(2)}) copy-start(s32[2,128,8192]{2,1,0:T(8,128)} %imag_ref.3) | copy-start | bytes 25165828
  62.7 1.4 copy-start.2
  64.1 2.1 %copy-start.14 = (bf16[8,112,1024]{2,1,0:T(8,128)(2,1)S(1)}, bf16[8,112,1024]{2,1,0:T(8,128)(2,1)}, u32[]{:S(2)}) copy-start(bf16[8,112,1024]{2,1,0:T(8,128)(2,1)} %constant.40.clone.table_ref) | copy-start | bytes 5505028
  66.3 3.3 %copy-start.3 = (bf16[4,128,2048]{2,1,0:T(8,128)(2,1)}, bf16[4,128,2048]{2,1,0:T(8,128)(2,1)S(1)}, u32[]{:S(2)}) copy-start(bf16[4,128,2048]{2,1,0:T(8,128)(2,1)S(1)} %shard_map.58.weighted_ref) | copy-start | bytes 6291460
  69.6 8.4 %copy-start.5 = (bf16[8,28,16,128]{3,2,1,0:T(8,128)(2,1)}, bf16[8,28,16,128]{3,2,1,0:T(8,128)(2,1)S(1)}, u32[]{:S(2)}) copy-start(bf16[8,28,16,128]{3,2,1,0:T(8,128)(2,1)S(1)} %shard_map.59) | copy-start | bytes 2752516
  76.9 25.2 %collective-permute-start.12 = (bf16[4,64,16,128]{3,2,1,0:T(8,128)(2,1)S(1)}, bf16[4,64,16,128]{3,2,1,0:T(8,128)(2,1)}, u32[]{:S(2)}, u32[]{:S(2)}) collective-permute-start(bf16[4,64,16,128]{3,2,1,0:T(8,128)(2,1)S(1)} %pad_maximum_fusion.1.refs_1_), channel_id=1, source_target_pairs={{0,2},{1,3},{2,0},{3,1},{4,6},{5,7},{6,4},{7,5},{8,10},{9,11},{10,... | collective-permute-start | bytes 3145736 | tf_op jit(solution)/shard_map/ppermute | solution.py:20
  77.5 26.4 %collective-permute-start.11 = (bf16[4,64,16,128]{3,2,1,0:T(8,128)(2,1)S(1)}, bf16[4,64,16,128]{3,2,1,0:T(8,128)(2,1)}, u32[]{:S(2)}, u32[]{:S(2)}) collective-permute-start(bf16[4,64,16,128]{3,2,1,0:T(8,128)(2,1)S(1)} %pad_maximum_fusion.1.refs_1_), channel_id=1, source_target_pairs={{0,1},{1,0},{2,3},{3,2},{4,5},{5,4},{6,7},{7,6},{8,9},{9,8},{10,11... | collective-permute-start | bytes 3145736 | tf_op jit(solution)/shard_map/ppermute | solution.py:20
  77.5 26.4 %collective-permute-start.10 = (bf16[4,64,16,128]{3,2,1,0:T(8,128)(2,1)S(1)}, bf16[4,64,16,128]{3,2,1,0:T(8,128)(2,1)}, u32[]{:S(2)}, u32[]{:S(2)}) collective-permute-start(bf16[4,64,16,128]{3,2,1,0:T(8,128)(2,1)S(1)} %collective-permute-done.4.refs_4_), channel_id=1, source_target_pairs={{0,1},{1,0},{2,3},{3,2},{4,5},{5,4},{6,7},{7,6},{8,9},{9,8},{10,11... | collective-permute-start | bytes 3145736 | tf_op jit(solution)/shard_map/ppermute | solution.py:20
  78.0 25.9 %collective-permute-start.9 = (bf16[4,64,16,128]{3,2,1,0:T(8,128)(2,1)S(1)}, bf16[4,64,16,128]{3,2,1,0:T(8,128)(2,1)}, u32[]{:S(2)}, u32[]{:S(2)}) collective-permute-start(bf16[4,64,16,128]{3,2,1,0:T(8,128)(2,1)S(1)} %pad_maximum_fusion.refs_0_), channel_id=1, source_target_pairs={{0,1},{1,0},{2,3},{3,2},{4,5},{5,4},{6,7},{7,6},{8,9},{9,8},{10,11... | collective-permute-start | bytes 3145736 | tf_op jit(solution)/shard_map/ppermute | solution.py:20
  78.0 31.1 %all-to-all-start = ((bf16[8,28,16,128]{3,2,1,0:T(8,128)(2,1)}), bf16[8,28,16,128]{3,2,1,0:T(8,128)(2,1)}, u32[]{:S(2)}, u32[]{:S(2)}) async-start(bf16[8,28,16,128]{3,2,1,0:T(8,128)(2,1)} %copy-done.5), calls=%async_computation | async-start | bytes 1835008 | tf_op jit(solution)/shard_map/all_to_all | solution.py:375
  85.4 1.6 copy-start.4
  87.0 1.7 copy-start.13
  92.8 0.8 copy-start.8
  93.6 0.8 copy-start.9
  109.1 22.0 %collective-permute-start.15 = (bf16[8,28,16,128]{3,2,1,0:T(8,128)(2,1)}, bf16[8,28,16,128]{3,2,1,0:T(8,128)(2,1)}, u32[]{:S(2)}, u32[]{:S(2)}) collective-permute-start(bf16[8,28,16,128]{3,2,1,0:T(8,128)(2,1)} %all-to-all-done.refs_8_), channel_id=1, source_target_pairs={{0,2},{1,3},{2,0},{3,1},{4,6},{5,7},{6,4},{7,5},{8,10},{9,11},{10,... | collective-permute-start | bytes 2752520 | tf_op jit(solution)/shard_map/ppermute | solution.py:20
  110.6 21.7 %collective-permute-start.14 = (bf16[8,28,16,128]{3,2,1,0:T(8,128)(2,1)}, bf16[8,28,16,128]{3,2,1,0:T(8,128)(2,1)}, u32[]{:S(2)}, u32[]{:S(2)}) collective-permute-start(bf16[8,28,16,128]{3,2,1,0:T(8,128)(2,1)} %all-to-all-done.refs_8_), channel_id=1, source_target_pairs={{0,1},{1,0},{2,3},{3,2},{4,5},{5,4},{6,7},{7,6},{8,9},{9,8},{10,11... | collective-permute-start | bytes 2752520 | tf_op jit(solution)/shard_map/ppermute | solution.py:20
  110.6 21.7 %collective-permute-start.13 = (bf16[4,64,16,128]{3,2,1,0:T(8,128)(2,1)}, bf16[4,64,16,128]{3,2,1,0:T(8,128)(2,1)}, u32[]{:S(2)}, u32[]{:S(2)}) collective-permute-start(bf16[4,64,16,128]{3,2,1,0:T(8,128)(2,1)} %collective-permute-done.12.refs_0_.refs_5_), channel_id=1, source_target_pairs={{0,1},{1,0},{2,3},{3,2},{4,5},{5,4},{6,7},{7,6},{8,9},{9,8},{10,11... | collective-permute-start | bytes 3145736 | tf_op jit(solution)/shard_map/ppermute | solution.py:20
  111.1 22.0 %all-to-all-start.1 = ((bf16[8,20,16,128]{3,2,1,0:T(8,128)(2,1)}), bf16[8,20,16,128]{3,2,1,0:T(8,128)(2,1)}, u32[]{:S(2)}, u32[]{:S(2)}) async-start(bf16[8,20,16,128]{3,2,1,0:T(8,128)(2,1)} %copy-done.8), calls=%async_computation.1 | async-start | bytes 1310720 | tf_op jit(solution)/shard_map/all_to_all | solution.py:375
  133.1 5.7 %collective-permute-start.16 = (bf16[8,28,16,128]{3,2,1,0:T(8,128)(2,1)}, bf16[8,28,16,128]{3,2,1,0:T(8,128)(2,1)}, u32[]{:S(2)}, u32[]{:S(2)}) collective-permute-start(bf16[8,28,16,128]{3,2,1,0:T(8,128)(2,1)} %collective-permute-done.15.refs_0_.refs_10_), channel_id=1, source_target_pairs={{0,1},{1,0},{2,3},{3,2},{4,5},{5,4},{6,7},{7,6},{8,9},{9,8},{10,11... | collective-permute-start | bytes 2752520 | tf_op jit(solution)/shard_map/ppermute | solution.py:20
  133.1 21.9 %all-to-all-start.2 = ((bf16[8,16,16,128]{3,2,1,0:T(8,128)(2,1)}), bf16[8,16,16,128]{3,2,1,0:T(8,128)(2,1)}, u32[]{:S(2)}, u32[]{:S(2)}) async-start(bf16[8,16,16,128]{3,2,1,0:T(8,128)(2,1)} %copy-done.9), calls=%async_computation.2 | async-start | bytes 1048576 | tf_op jit(solution)/shard_map/all_to_all | solution.py:375
  137.4 15.6 %collective-permute-start.17 = (bf16[8,20,16,128]{3,2,1,0:T(8,128)(2,1)}, bf16[8,20,16,128]{3,2,1,0:T(8,128)(2,1)S(1)}, u32[]{:S(2)}, u32[]{:S(2)}) collective-permute-start(bf16[8,20,16,128]{3,2,1,0:T(8,128)(2,1)} %all-to-all-done.1.refs_8_), channel_id=1, source_target_pairs={{0,1},{1,0},{2,3},{3,2},{4,5},{5,4},{6,7},{7,6},{8,9},{9,8},{10,11... | collective-permute-start | bytes 1966088 | tf_op jit(solution)/shard_map/ppermute | solution.py:20
  138.0 17.0 %collective-permute-start.18 = (bf16[8,20,16,128]{3,2,1,0:T(8,128)(2,1)}, bf16[8,20,16,128]{3,2,1,0:T(8,128)(2,1)}, u32[]{:S(2)}, u32[]{:S(2)}) collective-permute-start(bf16[8,20,16,128]{3,2,1,0:T(8,128)(2,1)} %all-to-all-done.1.refs_8_), channel_id=1, source_target_pairs={{0,2},{1,3},{2,0},{3,1},{4,6},{5,7},{6,4},{7,5},{8,10},{9,11},{10,... | collective-permute-start | bytes 1966088 | tf_op jit(solution)/shard_map/ppermute | solution.py:20
  138.8 0.7 copy-start.11
  139.5 17.8 %copy-start.12 = (f32[8,128]{1,0:T(8,128)S(1)}, f32[8,128]{1,0:T(8,128)}, u32[]{:S(2)}) copy-start(f32[8,128]{1,0:T(8,128)} %shard_map.62.refs_12_.refs_13_) | copy-start | bytes 12292
  153.0 0.9 copy-start.6
  155.0 2.3 %collective-permute-start.19 = (bf16[8,20,16,128]{3,2,1,0:T(8,128)(2,1)}, bf16[8,20,16,128]{3,2,1,0:T(8,128)(2,1)S(1)}, u32[]{:S(2)}, u32[]{:S(2)}) collective-permute-start(bf16[8,20,16,128]{3,2,1,0:T(8,128)(2,1)} %collective-permute-done.18.refs_10_), channel_id=1, source_target_pairs={{0,1},{1,0},{2,3},{3,2},{4,5},{5,4},{6,7},{7,6},{8,9},{9,8},{10,11... | collective-permute-start | bytes 1966088 | tf_op jit(solution)/shard_map/ppermute | solution.py:20
  155.0 13.2 %collective-permute-start.20 = (bf16[8,16,16,128]{3,2,1,0:T(8,128)(2,1)}, bf16[8,16,16,128]{3,2,1,0:T(8,128)(2,1)S(1)}, u32[]{:S(2)}, u32[]{:S(2)}) collective-permute-start(bf16[8,16,16,128]{3,2,1,0:T(8,128)(2,1)} %all-to-all-done.2.refs_8_), channel_id=1, source_target_pairs={{0,1},{1,0},{2,3},{3,2},{4,5},{5,4},{6,7},{7,6},{8,9},{9,8},{10,11... | collective-permute-start | bytes 1572872 | tf_op jit(solution)/shard_map/ppermute | solution.py:20
  155.5 14.0 %collective-permute-start.21 = (bf16[8,16,16,128]{3,2,1,0:T(8,128)(2,1)}, bf16[8,16,16,128]{3,2,1,0:T(8,128)(2,1)S(1)}, u32[]{:S(2)}, u32[]{:S(2)}) collective-permute-start(bf16[8,16,16,128]{3,2,1,0:T(8,128)(2,1)} %all-to-all-done.2.refs_8_), channel_id=1, source_target_pairs={{0,2},{1,3},{2,0},{3,1},{4,6},{5,7},{6,4},{7,5},{8,10},{9,11},{10,... | collective-permute-start | bytes 1572872 | tf_op jit(solution)/shard_map/ppermute | solution.py:20
  157.3 1.1 copy-start.7
  169.6 1.9 %collective-permute-start.22 = (bf16[8,16,16,128]{3,2,1,0:T(8,128)(2,1)S(1)}, bf16[8,16,16,128]{3,2,1,0:T(8,128)(2,1)S(1)}, u32[]{:S(2)}, u32[]{:S(2)}) collective-permute-start(bf16[8,16,16,128]{3,2,1,0:T(8,128)(2,1)S(1)} %collective-permute-done.21.refs_10_), channel_id=1, source_target_pairs={{0,1},{1,0},{2,3},{3,2},{4,5},{5,4},{6,7},{7,6},{8,9},{9,8},{10,11... | collective-permute-start | bytes 1572872 | tf_op jit(solution)/shard_map/ppermute | solution.py:20
